TPU v7x, 32 devices: a whole 2x2x4 slice. The times are simulated.
32 devices in a mesh: group: 2 (over y), section: 4 (over z), span: 2 (over x), mp: 2 (over core).
Axes of the slice: x: 2, y: 2, z: 4, core: 2. Of those that a mesh axis runs over, the one named last changes fastest.
Arguments:
- queries: bfloat16 [8, 256, 4096], P(('group', 'section'), None, ('span', 'mp')), parts along dimension 0, may hold values from -5 to 5
- keys_values: bfloat16 [2, 8, 256, 4096], P(None, ('group', 'section'), None, ('span', 'mp')), parts along dimension 1, may hold values from -5 to 5
- latents: bfloat16 [8, 256, 5120], P(('group', 'section'), ('span', 'mp')), parts along dimension 0, may hold values from -6 to 6
- out_weight: bfloat16 [4096, 5120], P(('span', 'mp')), may hold values from -3 to 3
- gate_table: float32 [8, 5120], replicated, may hold values from 0.5 to 1.5
- level_index: int32 [8], P(('group', 'section')), parts along dimension 0, may hold values from 0 to 7
- pair_window: int32 [6], P('group'), parts along dimension 0, may hold values from 0 to 256
Outputs:
- shifted: bfloat16 [8, 256, 5120], P(('group', 'section'), ('span', 'mp')), parts along dimension 0
There are 2 independent parts, one for each index of `group`. A program takes and returns all parts, laid end to end along the dimension named above; an argument that names none is the same for every part. Nothing has to cross between parts.
All inputs are finite; a program needn't handle non-finite values.
Results may differ from a plain program's by a relative error of at most 0.015.
Values may be sent and summed in bfloat16 or wider, within the bound.
No kernel may reach another device: no remote copies, remote signals or barrier semaphores. Data moves between devices by JAX's collectives and lax.ppermute only.
A program may use at most 64 MiB of HBM per device.

v0:
```python
import math

import jax
import jax.numpy as jnp
from jax import lax
from jax.sharding import PartitionSpec as P

HD = 128


NEG_BIG = -1e30


def extended(array, sides, width):
    for axis, dim in sides:
        size, length = (lax.axis_size(axis), array.shape[dim])
        up = [(i, (i + 1) % size) for i in range(size - 1)]
        down = [(j, i) for i, j in up]
        last = lax.slice_in_dim(array, length - width, length, axis=dim)
        first = lax.slice_in_dim(array, 0, width, axis=dim)
        before = lax.ppermute(last, axis, up)
        after = lax.ppermute(first, axis, down)
        array = jnp.concatenate([before, array, after], axis=dim)
    return array


def from_behind(value, axis, steps):
    count = lax.axis_size(axis)
    pairs = [(source, (source + steps) % count) for source in range(count)]
    return lax.ppermute(value, axis, pairs)


def split_heads(flat_rows):
    return flat_rows.reshape(flat_rows.shape[0], -1, HD)


def block_partial(query_block, key_rows, value_rows, key_mask):
    score_scale = 1.0 / math.sqrt(HD)
    scores = (
        jnp.einsum("bhd,khd->hbk", query_block, key_rows, preferred_element_type=jnp.float32)
        * score_scale
    )
    scores = jnp.where(key_mask[None, None, :], scores, NEG_BIG)
    row_max = jnp.max(scores, axis=-1)
    probabilities = jnp.where(key_mask[None, None, :], jnp.exp(scores - row_max[..., None]), 0.0)
    row_total = jnp.sum(probabilities, axis=-1)
    weighted = jnp.einsum(
        "hbk,khd->bhd",
        probabilities.astype(jnp.bfloat16),
        value_rows,
        preferred_element_type=jnp.float32,
    )
    return (weighted, row_max, row_total)


def shards(queries, keys_values, latents, out_weight, gate_table, level_index, pair_window):
    sections = lax.axis_size("section")
    section_id = lax.axis_index("section")
    span_tok = queries.shape[1]
    width_local = queries.shape[2]
    block_rows = min(512, span_tok)
    blocks = span_tok // block_rows
    final_pair = pair_window.shape[0] - 1
    prev_width = jnp.where(section_id > 0, pair_window[jnp.clip(section_id - 1, 0, final_pair)], 0)
    next_width = jnp.where(
        section_id < sections - 1, pair_window[jnp.clip(section_id, 0, final_pair)], 0
    )
    row_ids = jnp.arange(span_tok, dtype=jnp.int32)
    own_queries = queries[0]
    query_blocks = split_heads(own_queries).reshape(blocks, block_rows, -1, HD)
    ones_mask = jnp.ones((span_tok,), bool)
    padded = extended(keys_values, (("section", 1),), 1)
    key_rows = split_heads(padded[0].reshape(3 * span_tok, width_local))
    value_rows = split_heads(padded[1].reshape(3 * span_tok, width_local))
    key_mask = jnp.concatenate(
        [row_ids >= span_tok - prev_width, ones_mask, row_ids < next_width], 0
    )

    def one_block(query_block):
        weighted, row_max, row_total = block_partial(query_block, key_rows, value_rows, key_mask)
        return (weighted / jnp.swapaxes(row_total, 0, 1)[:, :, None]).astype(jnp.bfloat16)

    attended = lax.map(one_block, query_blocks)
    attended = attended.reshape(span_tok, width_local)
    summed = lax.psum_scatter(
        jnp.dot(attended, out_weight, preferred_element_type=jnp.float32).astype(jnp.bfloat16),
        ("span", "mp"),
        scatter_dimension=0,
        tiled=True,
    ).astype(jnp.float32)
    one_hot = (level_index[0] == jnp.arange(gate_table.shape[0], dtype=jnp.int32)).astype(
        jnp.float32
    )
    gate_row = jnp.sum(one_hot[:, None] * gate_table, axis=0)
    updated = (latents[0].astype(jnp.float32) + gate_row[None, :] * summed).astype(jnp.bfloat16)
    shifted = from_behind(updated, "section", 1)
    return shifted[None]


def solution(mesh):
    in_specs = (
        P(("group", "section"), None, ("span", "mp")),
        P(None, ("group", "section"), None, ("span", "mp")),
        P(("group", "section"), ("span", "mp"), None),
        P(("span", "mp"), None),
        P(),
        P(("group", "section")),
        P("group"),
    )
    out_specs = P(("group", "section"), ("span", "mp"), None)
    return jax.shard_map(shards, mesh=mesh, in_specs=in_specs, out_specs=out_specs, check_vma=False)
```

profile of v0, /device:TPU:0, one launch (start us, length us, event | category | flops | bytes accessed | tf_op | source)
XLA Modules:
  0.0 110.8 jit_solution(15434429009313025589)
XLA Ops:
  6.5 0.0 reduce-scatter.2.cloned.1.call-start
  6.5 6.0 %collective-permute-start = (bf16[2,1,256,1024]{3,2,1,0:T(8,128)(2,1)}, bf16[2,1,256,1024]{3,2,1,0:T(8,128)(2,1)}, u32[]{:S(2)}, u32[]{:S(2)}) collective-permute-start(bf16[2,1,256,1024]{3,2,1,0:T(8,128)(2,1)} %param.8), channel_id=1, source_target_pairs={{0,4},{4,8},{8,12},{1,5},{5,9},{9,13},{2,6},{6,10},{10,14},{3,7},{... | collective-permute-start | bytes 3145736 | tf_op jit(solution)/shard_map/ppermute | solution.py:21
  12.6 1.3 %collective-permute-start.1 = (bf16[2,1,256,1024]{3,2,1,0:T(8,128)(2,1)}, bf16[2,1,256,1024]{3,2,1,0:T(8,128)(2,1)S(1)}, u32[]{:S(2)}, u32[]{:S(2)}) collective-permute-start(bf16[2,1,256,1024]{3,2,1,0:T(8,128)(2,1)} %param.8), channel_id=1, source_target_pairs={{4,0},{8,4},{12,8},{5,1},{9,5},{13,9},{6,2},{10,6},{14,10},{7,3},{... | collective-permute-start | bytes 3145736 | tf_op jit(solution)/shard_map/ppermute | solution.py:22
  13.9 1.1 %copy.18 = bf16[32,8,8,128]{3,2,1,0:T(8,128)(2,1)S(1)} copy(bf16[32,8,8,128]{3,1,2,0:T(8,128)(2,1)} %bitcast.52) | data formatting | bytes 1048576
  15.0 1.4 %fusion.34 = (s32[1]{0:T(128)}, s32[1]{0:T(128)}) fusion(s32[3]{0:T(128)} %param.13, s32[]{:T(128)S(6)} %min.7, s32[]{:T(128)S(6)} %min.8), kind=kLoop, calls=%fused_computation.33 | loop fusion | bytes 24 | tf_op jit(solution)/shard_map/dynamic_slice | solution.py:64
  17.7 16.6 %collective-permute-done = bf16[2,1,256,1024]{3,2,1,0:T(8,128)(2,1)} collective-permute-done((bf16[2,1,256,1024]{3,2,1,0:T(8,128)(2,1)}, bf16[2,1,256,1024]{3,2,1,0:T(8,128)(2,1)}, u32[]{:S(2)}, u32[]{:S(2)}) %collective-permute-start) | collective-permute-done | bytes 1048608 | tf_op jit(solution)/shard_map/ppermute | solution.py:21
  34.3 1.3 %constant_dynamic-update-slice_fusion.2 = bf16[2,3,256,1024]{3,2,1,0:T(8,128)(2,1)S(1)} fusion(bf16[2,1,256,1024]{3,2,1,0:T(8,128)(2,1)} %collective-permute-done), kind=kLoop, calls=%fused_computation.25 | loop fusion | bytes 2097152
  35.6 0.0 copy-done
  35.6 0.1 constant_dynamic-update-slice_fusion.1
  35.7 3.6 %collective-permute-done.1 = bf16[2,1,256,1024]{3,2,1,0:T(8,128)(2,1)S(1)} collective-permute-done((bf16[2,1,256,1024]{3,2,1,0:T(8,128)(2,1)}, bf16[2,1,256,1024]{3,2,1,0:T(8,128)(2,1)S(1)}, u32[]{:S(2)}, u32[]{:S(2)}) %collective-permute-start.1) | collective-permute-done | bytes 1048608 | tf_op jit(solution)/shard_map/ppermute | solution.py:22
  39.3 0.1 constant_dynamic-update-slice_fusion
  39.3 0.6 fusion.33
  39.9 0.4 copy.17
  40.4 0.4 copy.16
  40.8 0.0 slice-start
  40.9 1.0 fusion.12
  41.8 0.0 slice-start.1
  41.8 0.0 slice-start.2
  41.9 2.4 %fusion.35 = (f32[8,256]{1,0:T(8,128)S(1)}, bf16[8,256,768]{1,2,0:T(8,128)(2,1)S(1)}) fusion(f32[8,768,256]{2,1,0:T(8,128)S(1)} %fusion.12, pred[768]{0:T(1024)(128)(4,1)S(1)} %pad_add_fusion), kind=kOutput, calls=%fused_computation.34 | output fusion | flops 12583679 | bytes 9446144 | tf_op jit(solution)/shard_map/while/body/eval_jaxpr/sub | solution.py:45
  44.3 0.7 fusion.25
  45.0 0.0 slice-done
  45.0 0.0 slice-done.1
  45.0 0.1 slice-done.2
  45.1 4.3 %convolution_convert_fusion = bf16[256,5120]{1,0:T(8,128)(2,1)} fusion(bf16[256,1024]{0,1:T(8,128)(2,1)S(1)} %bitcast.50, bf16[1024,5120]{1,0:T(8,128)(2,1)S(1)} %bitcast.44), kind=kOutput, calls=%fused_computation.1 | convolution fusion | flops 2685665280 | bytes 13631488 | tf_op jit(solution)/shard_map/dot_general | solution.py:86
  49.4 0.0 reduce-scatter.2.cloned.1.call-update
  50.2 0.0 copy-done.2
  50.2 0.1 multiply_reduce_fusion
  50.3 33.3 %reduce-scatter.2.cloned.1.call-done = bf16[64,5120]{1,0:T(8,128)(2,1)} async-done(((bf16[256,5120]{1,0:T(8,128)(2,1)}), bf16[64,5120]{1,0:T(8,128)(2,1)}) %reduce-scatter.2.cloned.1.call-update) | async-done | bytes 655376 | tf_op jit(solution)/shard_map/reduce_scatter | solution.py:85
  83.6 1.3 %fusion.19 = bf16[64,5120]{1,0:T(8,128)(2,1)S(1)} fusion(bf16[64,5120]{1,0:T(8,128)(2,1)} %reduce-scatter.2.cloned.1.call-done, bf16[1,64,5120]{2,1,0:T(8,128)(2,1)S(1)} %copy-done.1, f32[5120]{0:T(1024)S(1)} %multiply_reduce_fusion), kind=kLoop, calls=%fused_computation.18 | loop fusion | flops 1638400 | bytes 1986560 | tf_op jit(solution)/shard_map/convert_element_type | solution.py:95
  84.8 1.5 %collective-permute-start.2 = (bf16[64,5120]{1,0:T(8,128)(2,1)S(1)}, bf16[64,5120]{1,0:T(8,128)(2,1)S(1)}, u32[]{:S(2)}, u32[]{:S(2)}) collective-permute-start(bf16[64,5120]{1,0:T(8,128)(2,1)S(1)} %fusion.19), channel_id=1, source_target_pairs={{0,4},{4,8},{8,12},{12,0},{1,5},{5,9},{9,13},{13,1},{2,6},{6,10},{... | collective-permute-start | bytes 1966088 | tf_op jit(solution)/shard_map/ppermute | solution.py:30
  86.4 16.8 %collective-permute-done.2 = bf16[64,5120]{1,0:T(8,128)(2,1)S(1)} collective-permute-done((bf16[64,5120]{1,0:T(8,128)(2,1)S(1)}, bf16[64,5120]{1,0:T(8,128)(2,1)S(1)}, u32[]{:S(2)}, u32[]{:S(2)}) %collective-permute-start.2) | collective-permute-done | bytes 655392 | tf_op jit(solution)/shard_map/ppermute | solution.py:30
  103.2 0.8 copy.35
  (9 shorter events, 0.0 us)
Async XLA Ops:
  6.5 29.1 %copy-start = (bf16[2,1,256,1024]{3,2,1,0:T(8,128)(2,1)S(1)}, bf16[2,1,256,1024]{3,2,1,0:T(8,128)(2,1)}, u32[]{:S(2)}) copy-start(bf16[2,1,256,1024]{3,2,1,0:T(8,128)(2,1)} %param.8) | copy-start | bytes 3145732
  6.5 77.0 %reduce-scatter.2.cloned.1.call-start = ((), (), s32[]{:S(2)}) async-start(), calls=%async_computation.1 | async-start | bytes 3276800 | tf_op jit(solution)/shard_map/reduce_scatter | solution.py:85
  6.5 27.8 %collective-permute-start = (bf16[2,1,256,1024]{3,2,1,0:T(8,128)(2,1)}, bf16[2,1,256,1024]{3,2,1,0:T(8,128)(2,1)}, u32[]{:S(2)}, u32[]{:S(2)}) collective-permute-start(bf16[2,1,256,1024]{3,2,1,0:T(8,128)(2,1)} %param.8), channel_id=1, source_target_pairs={{0,4},{4,8},{8,12},{1,5},{5,9},{9,13},{2,6},{6,10},{10,14},{3,7},{... | collective-permute-start | bytes 3145736 | tf_op jit(solution)/shard_map/ppermute | solution.py:21
  12.6 26.7 %collective-permute-start.1 = (bf16[2,1,256,1024]{3,2,1,0:T(8,128)(2,1)}, bf16[2,1,256,1024]{3,2,1,0:T(8,128)(2,1)S(1)}, u32[]{:S(2)}, u32[]{:S(2)}) collective-permute-start(bf16[2,1,256,1024]{3,2,1,0:T(8,128)(2,1)} %param.8), channel_id=1, source_target_pairs={{4,0},{8,4},{12,8},{5,1},{9,5},{13,9},{6,2},{10,6},{14,10},{7,3},{... | collective-permute-start | bytes 3145736 | tf_op jit(solution)/shard_map/ppermute | solution.py:22
  40.8 4.1 %slice-start = ((s8[10485760]{0:T(1024)(128)(4,1)}), s8[4194304]{0:T(1024)(128)(4,1)S(1)}, s32[]{:S(2)}) async-start(s8[10485760]{0:T(1024)(128)(4,1)} %bitcast.43), calls=%async_computation.2 | async-start | bytes 8388608
  41.8 3.2 %slice-start.1 = ((s8[10485760]{0:T(1024)(128)(4,1)}), s8[4194304]{0:T(1024)(128)(4,1)S(1)}, s32[]{:S(2)}) async-start(s8[10485760]{0:T(1024)(128)(4,1)} %bitcast.43), calls=%async_computation.3 | async-start | bytes 8388608
  41.8 3.3 %slice-start.2 = ((s8[10485760]{0:T(1024)(128)(4,1)}), s8[2097152]{0:T(1024)(128)(4,1)S(1)}, s32[]{:S(2)}) async-start(s8[10485760]{0:T(1024)(128)(4,1)} %bitcast.43), calls=%async_computation.4 | async-start | bytes 4194304
  45.1 5.0 %copy-start.2 = (f32[8,5120]{1,0:T(8,128)S(1)}, f32[8,5120]{1,0:T(8,128)}, u32[]{:S(2)}) copy-start(f32[8,5120]{1,0:T(8,128)} %param.11) | copy-start | bytes 491524
  49.4 34.1 %copy-start.1 = (bf16[1,64,5120]{2,1,0:T(8,128)(2,1)S(1)}, bf16[1,64,5120]{2,1,0:T(8,128)(2,1)}, u32[]{:S(2)}) copy-start(bf16[1,64,5120]{2,1,0:T(8,128)(2,1)} %param.9) | copy-start | bytes 1966084
  84.8 18.3 %collective-permute-start.2 = (bf16[64,5120]{1,0:T(8,128)(2,1)S(1)}, bf16[64,5120]{1,0:T(8,128)(2,1)S(1)}, u32[]{:S(2)}, u32[]{:S(2)}) collective-permute-start(bf16[64,5120]{1,0:T(8,128)(2,1)S(1)} %fusion.19), channel_id=1, source_target_pairs={{0,4},{4,8},{8,12},{12,0},{1,5},{5,9},{9,13},{13,1},{2,6},{6,10},{... | collective-permute-start | bytes 1966088 | tf_op jit(solution)/shard_map/ppermute | solution.py:30
Sparse Core Ops, SparseCore 0:
  49.6 33.9 reduce-scatter.1
where the time goes:
time: 111 us
  waiting for transfers between devices  70.2 us (63%)
  between operations  15.5 us (14%)
  starting transfers between devices  8.82 us (8%)
  local copies, waits for them, and re-layouts  6.43 us (6%)
  matrix products  5.97 us (5%)
  other arithmetic  3.82 us (3%)
    reduce_scatter x1, waiting for transfers between devices, shards(): lax.psum_scatter(jnp.dot(attended, out_weight, preferred_element_type=jnp...  33.3 us
    ppermute x1, waiting for transfers between devices, from_behind(): return lax.ppermute(value, axis, pairs)  16.8 us
    ppermute x1, waiting for transfers between devices, extended(): before = lax.ppermute(last, axis, up)  16.6 us
    ppermute x1, starting transfers between devices, extended(): before = lax.ppermute(last, axis, up)  6.02 us
    unnamed x18, local copies, waits for them, and re-layouts  4.4 us
    dot_general x1, matrix products, shards(): jnp.dot(attended, out_weight, preferred_element_type=jnp.float32)  4.28 us
    ppermute x1, waiting for transfers between devices, extended(): after = lax.ppermute(first, axis, down)  3.58 us
    sub x1, other arithmetic, block_partial(): scores - row_max[..., None]  2.4 us
  transfers between devices with their start and end apart: 4, of which 4 were waited for; matrix products, arithmetic and copies ran while one was open for 4% of the time, Pallas kernels for 0%

commit v1 on v0

v1 whole, which is shorter than its diff:
```python
import functools
import math

import jax
import jax.numpy as jnp
from jax import lax
from jax.experimental import pallas as pl
from jax.experimental.pallas import tpu as pltpu
from jax.sharding import PartitionSpec as P

HD = 128
CHUNKS = 4
NEG_BIG = -1e30
VMEM_LIMIT = 48 * 1024 * 1024


def attention_kernel(spans, cores, places, q_ref, own_ref, prev_ref, next_ref, out_ref, v_ext):
    span_tok, width = q_ref.shape
    rows = span_tok // (spans * cores)
    span_id, core_id, prev_width, next_width = (places[0], places[1], places[2], places[3])
    factor = math.log2(math.e) / math.sqrt(HD)
    col = lax.broadcasted_iota(jnp.int32, (1, span_tok), 1)
    prev_mask = col >= span_tok - prev_width
    next_mask = col < next_width
    v_ext[:, HD:] = jnp.ones((3 * span_tok, HD), v_ext.dtype)
    starts = []
    for l in range(cores - 1, -1, -1):
        for k in range(spans - 1, -1, -1):
            block = lax.rem(span_id + k, spans) * cores + lax.rem(core_id + l, cores)
            starts.append(pl.multiple_of(block * rows, rows))
    contract = (((1,), (1,)), ((), ()))
    for h in range(width // HD):
        head = slice(h * HD, (h + 1) * HD)
        q = jnp.concatenate([q_ref[pl.ds(s, rows), head] for s in starts], axis=0)
        s_prev = lax.dot_general(q, prev_ref[0, :, head], contract, preferred_element_type=jnp.float32)
        s_own = lax.dot_general(q, own_ref[0, :, head], contract, preferred_element_type=jnp.float32)
        s_next = lax.dot_general(q, next_ref[0, :, head], contract, preferred_element_type=jnp.float32)
        s_prev = jnp.where(prev_mask, s_prev, NEG_BIG)
        s_next = jnp.where(next_mask, s_next, NEG_BIG)
        scores = jnp.concatenate([s_prev, s_own, s_next], axis=1)
        top = jnp.max(scores, axis=1, keepdims=True)
        probs = jnp.exp2((scores - top) * factor).astype(jnp.bfloat16)
        v_ext[:span_tok, :HD] = prev_ref[1, :, head]
        v_ext[span_tok : 2 * span_tok, :HD] = own_ref[1, :, head]
        v_ext[2 * span_tok :, :HD] = next_ref[1, :, head]
        both = jnp.dot(probs, v_ext[...], preferred_element_type=jnp.float32)
        out_ref[:, head] = (both[:, :HD] / both[:, HD:]).astype(out_ref.dtype)


def attention(spans, cores, places, queries, own, before, after):
    span_tok, width = queries.shape
    whole = pl.BlockSpec(memory_space=pltpu.VMEM)
    return pl.pallas_call(
        functools.partial(attention_kernel, spans, cores),
        out_shape=jax.ShapeDtypeStruct((span_tok, width), jnp.bfloat16),
        in_specs=[pl.BlockSpec(memory_space=pltpu.SMEM)] + [whole] * 4,
        out_specs=whole,
        scratch_shapes=[pltpu.VMEM((3 * span_tok, 2 * HD), jnp.bfloat16)],
        compiler_params=pltpu.CompilerParams(vmem_limit_bytes=VMEM_LIMIT),
        cost_estimate=pl.CostEstimate(
            flops=12 * span_tok * span_tok * width,
            bytes_accessed=16 * span_tok * width,
            transcendentals=3 * span_tok * span_tok * width // HD,
        ),
        name="attention",
    )(places, queries, own, before, after)


def project_kernel(parts, rows, *refs):
    att, weights, (send_ref, keep_ref) = refs[:parts], refs[parts : 2 * parts], refs[2 * parts :]
    total = jnp.dot(att[0][...], weights[0][...], preferred_element_type=jnp.float32)
    for a, w in zip(att[1:], weights[1:]):
        total += jnp.dot(a[...], w[...], preferred_element_type=jnp.float32)
    send_ref[...] = total[:-rows].astype(send_ref.dtype)
    keep_ref[...] = total[-rows:]


def project(att, weights, rows, chunk, chunks):
    parts = len(att)
    all_rows, depth = att[0].shape
    columns = weights[0].shape[1] // chunks
    tile = columns
    for size in (640, 512, 256, 128):
        if columns % size == 0:
            tile = size
            break
    steps = columns // tile
    first = chunk * steps
    return pl.pallas_call(
        functools.partial(project_kernel, parts, rows),
        grid=(steps,),
        out_shape=(
            jax.ShapeDtypeStruct((all_rows - rows, columns), jnp.bfloat16),
            jax.ShapeDtypeStruct((rows, columns), jnp.float32),
        ),
        in_specs=[pl.BlockSpec((all_rows, depth), lambda t: (0, 0))] * parts
        + [pl.BlockSpec((depth, tile), lambda t: (0, first + t))] * parts,
        out_specs=(
            pl.BlockSpec((all_rows - rows, tile), lambda t: (0, t)),
            pl.BlockSpec((rows, tile), lambda t: (0, t)),
        ),
        compiler_params=pltpu.CompilerParams(vmem_limit_bytes=VMEM_LIMIT),
        cost_estimate=pl.CostEstimate(
            flops=2 * parts * all_rows * depth * columns,
            bytes_accessed=2 * parts * depth * columns,
            transcendentals=0,
        ),
        name="project",
    )(*att, *weights)


def rotate(value, axis, steps):
    count = lax.axis_size(axis)
    return lax.ppermute(value, axis, [(i, (i + steps) % count) for i in range(count)])


def shards(queries, keys_values, latents, out_weight, gate_table, level_index, pair_window):
    sections, spans, cores = (lax.axis_size(a) for a in ("section", "span", "mp"))
    section_id = lax.axis_index("section")
    rows = latents.shape[1]
    final_pair = pair_window.shape[0] - 1
    prev_width = jnp.where(section_id > 0, pair_window[jnp.clip(section_id - 1, 0, final_pair)], 0)
    next_width = jnp.where(
        section_id < sections - 1, pair_window[jnp.clip(section_id, 0, final_pair)], 0
    )
    places = jnp.stack(
        [lax.axis_index("span"), lax.axis_index("mp"), prev_width, next_width]
    ).astype(jnp.int32)
    up = [(i, i + 1) for i in range(sections - 1)]
    down = [(j, i) for i, j in up]
    before = lax.ppermute(keys_values, "section", up)
    after = lax.ppermute(keys_values, "section", down)
    weights = [out_weight] + [rotate(out_weight, "mp", l) for l in range(1, cores)]
    gate_row = gate_table[level_index[0]]

    attended = attention(
        spans, cores, places, queries[0], keys_values[:, 0], before[:, 0], after[:, 0]
    )
    per_core = spans * rows
    att = [attended[(cores - 1) * per_core :]]
    for l in range(1, cores):
        att.append(rotate(attended[(cores - 1 - l) * per_core : (cores - l) * per_core], "mp", l))

    columns = latents.shape[2] // CHUNKS
    pieces = []
    for c in range(CHUNKS):
        send, keep = project(att, weights, rows, c, CHUNKS)
        total = keep
        for k in range(1, spans):
            block = send[(spans - 1 - k) * rows : (spans - k) * rows]
            total = total + rotate(block, "span", k).astype(jnp.float32)
        part = slice(c * columns, (c + 1) * columns)
        updated = latents[0, :, part].astype(jnp.float32) + gate_row[None, part] * total
        pieces.append(rotate(updated.astype(jnp.bfloat16), "section", 1))
    return jnp.concatenate(pieces, axis=1)[None]


def solution(mesh):
    in_specs = (
        P(("group", "section"), None, ("span", "mp")),
        P(None, ("group", "section"), None, ("span", "mp")),
        P(("group", "section"), ("span", "mp"), None),
        P(("span", "mp"), None),
        P(),
        P(("group", "section")),
        P("group"),
    )
    out_specs = P(("group", "section"), ("span", "mp"), None)
    return jax.shard_map(shards, mesh=mesh, in_specs=in_specs, out_specs=out_specs, check_vma=False)
```

time: 111 us -> 79.8 us (0.72)
  waiting for transfers between devices: 70.2 us -> 40 us
  Pallas kernels: 0 us -> 15.9 us
  between operations: 15.5 us -> 2.07 us
  starting transfers between devices: 8.82 us -> 15.7 us
  matrix products: 5.97 us -> 0 us
  other arithmetic: 3.82 us -> 1.21 us
  local copies, waits for them, and re-layouts: 6.43 us -> 4.61 us
    reduce_scatter x1 -> x0, waiting for transfers between devices: 33.3 us -> none  [shards(): lax.psum_scatter(jnp.dot(attended, out_weight, preferred_element_type=jnp...]
    pallas_call x0 -> x5, Pallas kernels: none -> 15.9 us  [the longest x4 12.6 us: project(): pl.pallas_call(functools.partial(project_kernel, parts, rows), grid=(step...]
    ppermute x3 -> x12, starting transfers between devices: 8.82 us -> 15.7 us  [the longest x10 9.84 us: rotate(): lax.ppermute(value, axis, [(i, (i + steps) % count) for i in range(count)])]
    dot_general x3 -> x0, matrix products: 5.97 us -> none  [the longest x1 4.28 us: shards(): jnp.dot(attended, out_weight, preferred_element_type=jnp.float32)]
    ppermute x3 -> x12, waiting for transfers between devices: 37 us -> 40 us  [the longest x1 19.3 us: shards(): before = lax.ppermute(keys_values, 'section', up)]
    sub x1 -> x0, other arithmetic: 2.4 us -> none  [block_partial(): scores - row_max[..., None]]
    unnamed x18 -> x6, local copies, waits for them, and re-layouts: 4.4 us -> 2.27 us
  transfers between devices with their start and end apart: 4 -> 12, of which waited for: 4 -> 8; matrix products, arithmetic and copies ran while one was open for 4% -> 3% of each run, Pallas kernels for 0% -> 16%
where the time goes in v1:
time: 79.8 us; the launch traced here: 79.5 us
  waiting for transfers between devices  40 us (50%)
  Pallas kernels  15.9 us (20%)
  starting transfers between devices  15.7 us (20%)
  local copies, waits for them, and re-layouts  4.61 us (6%)
  between operations  2.07 us (3%)
  other arithmetic  1.21 us (2%)
    ppermute x1, waiting for transfers between devices, shards(): before = lax.ppermute(keys_values, 'section', up)  19.3 us
    ppermute x10, waiting for transfers between devices, rotate(): lax.ppermute(value, axis, [(i, (i + steps) % count) for i in range(count)])  16.6 us
    pallas_call x4, Pallas kernels, project(): pl.pallas_call(functools.partial(project_kernel, parts, rows), grid=(step...  12.6 us
    ppermute x10, starting transfers between devices, rotate(): lax.ppermute(value, axis, [(i, (i + steps) % count) for i in range(count)])  9.84 us
    ppermute x1, starting transfers between devices, shards(): before = lax.ppermute(keys_values, 'section', up)  4.53 us
    ppermute x1, waiting for transfers between devices, shards(): after = lax.ppermute(keys_values, 'section', down)  4.08 us
    pallas_call x1, Pallas kernels, attention(): pl.pallas_call(functools.partial(attention_kernel, spans, cores), out_sha...  3.25 us
    unnamed x6, local copies, waits for them, and re-layouts  2.27 us
  transfers between devices with their start and end apart: 12, of which 8 were waited for; matrix products, arithmetic and copies ran while one was open for 3% of the time, Pallas kernels for 16%

profile of v1, /device:TPU:0, one launch (start us, length us, event | category | flops | bytes accessed | tf_op | source)
XLA Modules:
  0.0 79.5 jit_solution(5096112734567650986)
XLA Ops:
  0.0 0.5 collective-permute-start.3
  0.5 4.5 %collective-permute-start = (bf16[2,1,256,1024]{3,2,0,1:T(8,128)(2,1)}, bf16[2,1,256,1024]{3,2,0,1:T(8,128)(2,1)S(1)}, u32[]{:S(2)}, u32[]{:S(2)}) collective-permute-start(bf16[2,1,256,1024]{3,2,0,1:T(8,128)(2,1)} %bitcast.29), channel_id=1, source_target_pairs={{0,4},{4,8},{8,12},{1,5},{5,9},{9,13},{2,6},{6,10},{10,14},{3,7},{... | collective-permute-start | bytes 3145736 | tf_op jit(solution)/shard_map/ppermute | solution.py:131
  5.0 1.3 %collective-permute-start.1 = (bf16[2,1,256,1024]{3,2,0,1:T(8,128)(2,1)}, bf16[2,1,256,1024]{3,2,0,1:T(8,128)(2,1)S(1)}, u32[]{:S(2)}, u32[]{:S(2)}) collective-permute-start(bf16[2,1,256,1024]{3,2,0,1:T(8,128)(2,1)} %bitcast.30), channel_id=1, source_target_pairs={{4,0},{8,4},{12,8},{5,1},{9,5},{13,9},{6,2},{10,6},{14,10},{7,3},{... | collective-permute-start | bytes 3145736 | tf_op jit(solution)/shard_map/ppermute | solution.py:132
  6.3 1.3 %fusion.5 = (s32[1]{0:T(128)}, s32[1]{0:T(128)}) fusion(s32[3]{0:T(128)} %param.13, s32[]{:T(128)S(6)} %min.7, s32[]{:T(128)S(6)} %min.8), kind=kLoop, calls=%fused_computation.15 | loop fusion | bytes 24 | tf_op jit(solution)/shard_map/dynamic_slice | solution.py:122
  8.9 0.1 pad_add_fusion.places
  9.0 19.3 %collective-permute-done = bf16[2,1,256,1024]{3,2,0,1:T(8,128)(2,1)S(1)} collective-permute-done((bf16[2,1,256,1024]{3,2,0,1:T(8,128)(2,1)}, bf16[2,1,256,1024]{3,2,0,1:T(8,128)(2,1)S(1)}, u32[]{:S(2)}, u32[]{:S(2)}) %collective-permute-start) | collective-permute-done | bytes 1048608 | tf_op jit(solution)/shard_map/ppermute | solution.py:131
  28.3 4.1 %collective-permute-done.1 = bf16[2,1,256,1024]{3,2,0,1:T(8,128)(2,1)S(1)} collective-permute-done((bf16[2,1,256,1024]{3,2,0,1:T(8,128)(2,1)}, bf16[2,1,256,1024]{3,2,0,1:T(8,128)(2,1)S(1)}, u32[]{:S(2)}, u32[]{:S(2)}) %collective-permute-start.1) | collective-permute-done | bytes 1048608 | tf_op jit(solution)/shard_map/ppermute | solution.py:132
  32.4 1.2 %copy-done = bf16[2,1,256,1024]{3,2,1,0:T(8,128)(2,1)S(1)} copy-done((bf16[2,1,256,1024]{3,2,1,0:T(8,128)(2,1)S(1)}, bf16[2,1,256,1024]{3,2,1,0:T(8,128)(2,1)}, u32[]{:S(2)}) %copy-start) | copy-done | bytes 1048600
  33.6 1.0 %copy-done.1 = bf16[1,256,1024]{2,1,0:T(8,128)(2,1)S(1)} copy-done((bf16[1,256,1024]{2,1,0:T(8,128)(2,1)S(1)}, bf16[1,256,1024]{2,1,0:T(8,128)(2,1)}, u32[]{:S(2)}) %copy-start.1) | copy-done | bytes 524312
  34.7 3.3 %attention.1 = bf16[256,1024]{1,0:T(8,128)(2,1)S(1)} custom-call(s32[4]{0:T(128)S(1)} %pad_add_fusion.places, bf16[256,1024]{1,0:T(8,128)(2,1)S(1)} %bitcast.34, bf16[2,256,1024]{2,1,0:T(8,128)(2,1)S(1)} %bitcast.31, bf16[2,256,1024]{2,1,0:T(8,128)(2,1)S(1)} %bitcast.32, bf16[2,256,1024]{2,1,0:T(8,128)(2,1)S(1)} %bitcast.33), custom_call_target="tpu_custom_call" | custom-call | flops 805306368 | bytes 4194304 | tf_op jit(solution)/shard_map/attention/pallas_call | solution.py:53
  38.0 0.1 collective-permute-start.2
  38.0 1.5 %collective-permute-done.2.refs_1_ = bf16[128,1024]{1,0:T(8,128)(2,1)S(1)} collective-permute-done((bf16[128,1024]{1,0:T(8,128)(2,1)S(1)}, bf16[128,1024]{1,0:T(8,128)(2,1)S(1)}, u32[]{:S(2)}, u32[]{:S(2)}) %collective-permute-start.2) | collective-permute-done | bytes 262176 | tf_op jit(solution)/shard_map/ppermute | solution.py:114
  39.6 3.2 %project.6 = (bf16[64,1280]{1,0:T(8,128)(2,1)S(1)}, f32[64,1280]{1,0:T(8,128)S(1)}) custom-call(bf16[128,1024]{1,0:T(8,128)(2,1)S(1)} %get-tuple-element.30.refs_0_, bf16[128,1024]{1,0:T(8,128)(2,1)S(1)} %collective-permute-done.2.refs_1_, bf16[1024,5120]{1,0:T(8,128)(2,1)} %refs_2_.7, bf16[1024,5120]{1,0:T(8,128)(2,1)} %collective-permute-done.3.refs_3_), custom_call_target="tpu_custom_call" | custom-call | flops 671088640 | bytes 5242880 | tf_op jit(solution)/shard_map/project/pallas_call | solution.py:89
  42.8 1.6 %collective-permute-start.8 = (bf16[64,1280]{1,0:T(8,128)(2,1)S(1)}, bf16[64,1280]{1,0:T(8,128)(2,1)S(1)}, u32[]{:S(2)}, u32[]{:S(2)}) collective-permute-start(bf16[64,1280]{1,0:T(8,128)(2,1)S(1)} %get-tuple-element.18), channel_id=1, source_target_pairs={{0,2},{2,0},{1,3},{3,1},{4,6},{6,4},{5,7},{7,5},{8,10},{10,8},{9,1... | collective-permute-start | bytes 491528 | tf_op jit(solution)/shard_map/ppermute | solution.py:114
  44.3 3.2 %project.7 = (bf16[64,1280]{1,0:T(8,128)(2,1)S(1)}, f32[64,1280]{1,0:T(8,128)S(1)}) custom-call(bf16[128,1024]{1,0:T(8,128)(2,1)S(1)} %get-tuple-element.30.refs_0_, bf16[128,1024]{1,0:T(8,128)(2,1)S(1)} %collective-permute-done.2.refs_1_, bf16[1024,5120]{1,0:T(8,128)(2,1)} %refs_2_.7, bf16[1024,5120]{1,0:T(8,128)(2,1)} %collective-permute-done.3.refs_3_), custom_call_target="tpu_custom_call" | custom-call | flops 671088640 | bytes 5242880 | tf_op jit(solution)/shard_map/project/pallas_call | solution.py:89
  47.5 0.6 collective-permute-start.10
  48.1 3.2 %project.5 = (bf16[64,1280]{1,0:T(8,128)(2,1)S(1)}, f32[64,1280]{1,0:T(8,128)S(1)}) custom-call(bf16[128,1024]{1,0:T(8,128)(2,1)S(1)} %get-tuple-element.30.refs_0_, bf16[128,1024]{1,0:T(8,128)(2,1)S(1)} %collective-permute-done.2.refs_1_, bf16[1024,5120]{1,0:T(8,128)(2,1)} %refs_2_.7, bf16[1024,5120]{1,0:T(8,128)(2,1)} %collective-permute-done.3.refs_3_), custom_call_target="tpu_custom_call" | custom-call | flops 671088640 | bytes 5242880 | tf_op jit(solution)/shard_map/project/pallas_call | solution.py:89
  51.3 1.6 %collective-permute-start.6 = (bf16[64,1280]{1,0:T(8,128)(2,1)S(1)}, bf16[64,1280]{1,0:T(8,128)(2,1)S(1)}, u32[]{:S(2)}, u32[]{:S(2)}) collective-permute-start(bf16[64,1280]{1,0:T(8,128)(2,1)S(1)} %get-tuple-element.16), channel_id=1, source_target_pairs={{0,2},{2,0},{1,3},{3,1},{4,6},{6,4},{5,7},{7,5},{8,10},{10,8},{9,1... | collective-permute-start | bytes 491528 | tf_op jit(solution)/shard_map/ppermute | solution.py:114
  52.8 3.1 %project.4 = (bf16[64,1280]{1,0:T(8,128)(2,1)S(1)}, f32[64,1280]{1,0:T(8,128)S(1)}) custom-call(bf16[128,1024]{1,0:T(8,128)(2,1)S(1)} %get-tuple-element.30.refs_0_, bf16[128,1024]{1,0:T(8,128)(2,1)S(1)} %collective-permute-done.2.refs_1_, bf16[1024,5120]{1,0:T(8,128)(2,1)} %refs_2_.7, bf16[1024,5120]{1,0:T(8,128)(2,1)} %collective-permute-done.3.refs_3_), custom_call_target="tpu_custom_call" | custom-call | flops 671088640 | bytes 5242880 | tf_op jit(solution)/shard_map/project/pallas_call | solution.py:89
  56.0 0.6 collective-permute-start.4
  57.2 1.0 %dynamic-slice_reduce_fusion.3 = (f32[1280]{0:T(1024)S(1)}, f32[1280]{0:T(1024)S(1)}, f32[1280]{0:T(1024)S(1)}, f32[1280]{0:T(1024)S(1)}) fusion(f32[8,5120]{1,0:T(8,128)} %param.11, s32[]{:T(128)S(6)} %select_n.12, s32[]{:T(128)S(6)} %add.47, s32[]{:T(128)S(6)} %add.46, s32[]{:T(128)S(6)} %add.48), kind=kLoop, calls=%fused_computation.12 | loop fusion | bytes 40976 | tf_op jit(solution)/shard_map/slice | solution.py:153
  58.2 3.2 %collective-permute-done.4 = bf16[64,1280]{1,0:T(8,128)(2,1)S(1)} collective-permute-done((bf16[64,1280]{1,0:T(8,128)(2,1)S(1)}, bf16[64,1280]{1,0:T(8,128)(2,1)S(1)}, u32[]{:S(2)}, u32[]{:S(2)}) %collective-permute-start.4) | collective-permute-done | bytes 163872 | tf_op jit(solution)/shard_map/ppermute | solution.py:114
  61.4 0.2 fusion.3
  61.7 1.5 %collective-permute-start.11 = (bf16[64,1280]{1,0:T(8,128)(2,1)S(1)}, bf16[64,1280]{1,0:T(8,128)(2,1)S(1)}, u32[]{:S(2)}, u32[]{:S(2)}) collective-permute-start(bf16[64,1280]{1,0:T(8,128)(2,1)S(1)} %get-tuple-element.27), channel_id=1, source_target_pairs={{0,4},{4,8},{8,12},{12,0},{1,5},{5,9},{9,13},{13,1},{2,6},{6,10},{... | collective-permute-start | bytes 491528 | tf_op jit(solution)/shard_map/ppermute | solution.py:114
  63.2 1.6 %collective-permute-start.5 = (bf16[64,1280]{1,0:T(8,128)(2,1)S(1)}, bf16[64,1280]{1,0:T(8,128)(2,1)S(1)}, u32[]{:S(2)}, u32[]{:S(2)}) collective-permute-start(bf16[64,1280]{1,0:T(8,128)(2,1)S(1)} %get-tuple-element.25), channel_id=1, source_target_pairs={{0,4},{4,8},{8,12},{12,0},{1,5},{5,9},{9,13},{13,1},{2,6},{6,10},{... | collective-permute-start | bytes 491528 | tf_op jit(solution)/shard_map/ppermute | solution.py:114
  64.8 0.1 collective-permute-start.7
  64.9 1.8 %collective-permute-start.9 = (bf16[64,1280]{1,0:T(8,128)(2,1)S(1)}, bf16[64,1280]{1,0:T(8,128)(2,1)S(1)}, u32[]{:S(2)}, u32[]{:S(2)}) collective-permute-start(bf16[64,1280]{1,0:T(8,128)(2,1)S(1)} %get-tuple-element.28), channel_id=1, source_target_pairs={{0,4},{4,8},{8,12},{12,0},{1,5},{5,9},{9,13},{13,1},{2,6},{6,10},{... | collective-permute-start | bytes 491528 | tf_op jit(solution)/shard_map/ppermute | solution.py:114
  66.7 4.0 %collective-permute-done.11 = bf16[64,1280]{1,0:T(8,128)(2,1)S(1)} collective-permute-done((bf16[64,1280]{1,0:T(8,128)(2,1)S(1)}, bf16[64,1280]{1,0:T(8,128)(2,1)S(1)}, u32[]{:S(2)}, u32[]{:S(2)}) %collective-permute-start.11) | collective-permute-done | bytes 163872 | tf_op jit(solution)/shard_map/ppermute | solution.py:114
  70.7 3.5 %collective-permute-done.5 = bf16[64,1280]{1,0:T(8,128)(2,1)S(1)} collective-permute-done((bf16[64,1280]{1,0:T(8,128)(2,1)S(1)}, bf16[64,1280]{1,0:T(8,128)(2,1)S(1)}, u32[]{:S(2)}, u32[]{:S(2)}) %collective-permute-start.5) | collective-permute-done | bytes 163872 | tf_op jit(solution)/shard_map/ppermute | solution.py:114
  74.2 2.6 %collective-permute-done.7 = bf16[64,1280]{1,0:T(8,128)(2,1)S(1)} collective-permute-done((bf16[64,1280]{1,0:T(8,128)(2,1)S(1)}, bf16[64,1280]{1,0:T(8,128)(2,1)S(1)}, u32[]{:S(2)}, u32[]{:S(2)}) %collective-permute-start.7) | collective-permute-done | bytes 163872 | tf_op jit(solution)/shard_map/ppermute | solution.py:114
  76.8 1.8 %collective-permute-done.9 = bf16[64,1280]{1,0:T(8,128)(2,1)S(1)} collective-permute-done((bf16[64,1280]{1,0:T(8,128)(2,1)S(1)}, bf16[64,1280]{1,0:T(8,128)(2,1)S(1)}, u32[]{:S(2)}, u32[]{:S(2)}) %collective-permute-start.9) | collective-permute-done | bytes 163872 | tf_op jit(solution)/shard_map/ppermute | solution.py:114
  78.6 0.9 %maximum_bitcast_fusion = bf16[1,64,5120]{2,1,0:T(8,128)(2,1)} fusion(bf16[64,1280]{1,0:T(8,128)(2,1)S(1)} %collective-permute-done.11, bf16[64,1280]{1,0:T(8,128)(2,1)S(1)} %collective-permute-done.9, bf16[64,1280]{1,0:T(8,128)(2,1)S(1)} %collective-permute-done.7, bf16[64,1280]{1,0:T(8,128)(2,1)S(1)} %collective-permute-done.5), kind=kLoop, calls=%fused_computation | loop fusion | flops 2621440 | bytes 1310720 | tf_op jit(solution)/shard_map/broadcast_in_dim | solution.py:155
  (9 shorter events, 0.1 us)
Async XLA Ops:
  0.0 39.6 %collective-permute-start.3 = (bf16[1024,5120]{1,0:T(8,128)(2,1)}, bf16[1024,5120]{1,0:T(8,128)(2,1)}, u32[]{:S(2)}, u32[]{:S(2)}) collective-permute-start(bf16[1024,5120]{1,0:T(8,128)(2,1)} %refs_2_.7), channel_id=1, source_target_pairs={{0,1},{1,0},{2,3},{3,2},{4,5},{5,4},{6,7},{7,6},{8,9},{9,8},{10,11... | collective-permute-start | bytes 31457288 | tf_op jit(solution)/shard_map/ppermute | solution.py:114
  0.5 27.9 %collective-permute-start = (bf16[2,1,256,1024]{3,2,0,1:T(8,128)(2,1)}, bf16[2,1,256,1024]{3,2,0,1:T(8,128)(2,1)S(1)}, u32[]{:S(2)}, u32[]{:S(2)}) collective-permute-start(bf16[2,1,256,1024]{3,2,0,1:T(8,128)(2,1)} %bitcast.29), channel_id=1, source_target_pairs={{0,4},{4,8},{8,12},{1,5},{5,9},{9,13},{2,6},{6,10},{10,14},{3,7},{... | collective-permute-start | bytes 3145736 | tf_op jit(solution)/shard_map/ppermute | solution.py:131
  5.0 27.4 %collective-permute-start.1 = (bf16[2,1,256,1024]{3,2,0,1:T(8,128)(2,1)}, bf16[2,1,256,1024]{3,2,0,1:T(8,128)(2,1)S(1)}, u32[]{:S(2)}, u32[]{:S(2)}) collective-permute-start(bf16[2,1,256,1024]{3,2,0,1:T(8,128)(2,1)} %bitcast.30), channel_id=1, source_target_pairs={{4,0},{8,4},{12,8},{5,1},{9,5},{13,9},{6,2},{10,6},{14,10},{7,3},{... | collective-permute-start | bytes 3145736 | tf_op jit(solution)/shard_map/ppermute | solution.py:132
  32.4 1.2 %copy-start = (bf16[2,1,256,1024]{3,2,1,0:T(8,128)(2,1)S(1)}, bf16[2,1,256,1024]{3,2,1,0:T(8,128)(2,1)}, u32[]{:S(2)}) copy-start(bf16[2,1,256,1024]{3,2,1,0:T(8,128)(2,1)} %param.8) | copy-start | bytes 3145732
  33.6 1.0 %copy-start.1 = (bf16[1,256,1024]{2,1,0:T(8,128)(2,1)S(1)}, bf16[1,256,1024]{2,1,0:T(8,128)(2,1)}, u32[]{:S(2)}) copy-start(bf16[1,256,1024]{2,1,0:T(8,128)(2,1)} %param.7) | copy-start | bytes 1572868
  38.0 1.6 %collective-permute-start.2 = (bf16[128,1024]{1,0:T(8,128)(2,1)S(1)}, bf16[128,1024]{1,0:T(8,128)(2,1)S(1)}, u32[]{:S(2)}, u32[]{:S(2)}) collective-permute-start(bf16[128,1024]{1,0:T(8,128)(2,1)S(1)} %get-tuple-element.29), channel_id=1, source_target_pairs={{0,1},{1,0},{2,3},{3,2},{4,5},{5,4},{6,7},{7,6},{8,9},{9,8},{10,11... | collective-permute-start | bytes 786440 | tf_op jit(solution)/shard_map/ppermute | solution.py:114
  42.8 15.4 %collective-permute-start.8 = (bf16[64,1280]{1,0:T(8,128)(2,1)S(1)}, bf16[64,1280]{1,0:T(8,128)(2,1)S(1)}, u32[]{:S(2)}, u32[]{:S(2)}) collective-permute-start(bf16[64,1280]{1,0:T(8,128)(2,1)S(1)} %get-tuple-element.18), channel_id=1, source_target_pairs={{0,2},{2,0},{1,3},{3,1},{4,6},{6,4},{5,7},{7,5},{8,10},{10,8},{9,1... | collective-permute-start | bytes 491528 | tf_op jit(solution)/shard_map/ppermute | solution.py:114
  47.5 10.7 %collective-permute-start.10 = (bf16[64,1280]{1,0:T(8,128)(2,1)S(1)}, bf16[64,1280]{1,0:T(8,128)(2,1)S(1)}, u32[]{:S(2)}, u32[]{:S(2)}) collective-permute-start(bf16[64,1280]{1,0:T(8,128)(2,1)S(1)} %get-tuple-element.20), channel_id=1, source_target_pairs={{0,2},{2,0},{1,3},{3,1},{4,6},{6,4},{5,7},{7,5},{8,10},{10,8},{9,1... | collective-permute-start | bytes 491528 | tf_op jit(solution)/shard_map/ppermute | solution.py:114
  51.2 10.2 %copy-start.2 = (bf16[1,64,5120]{2,1,0:T(8,128)(2,1)S(1)}, bf16[1,64,5120]{2,1,0:T(8,128)(2,1)}, u32[]{:S(2)}) copy-start(bf16[1,64,5120]{2,1,0:T(8,128)(2,1)} %param.9) | copy-start | bytes 1966084
  51.3 7.0 %collective-permute-start.6 = (bf16[64,1280]{1,0:T(8,128)(2,1)S(1)}, bf16[64,1280]{1,0:T(8,128)(2,1)S(1)}, u32[]{:S(2)}, u32[]{:S(2)}) collective-permute-start(bf16[64,1280]{1,0:T(8,128)(2,1)S(1)} %get-tuple-element.16), channel_id=1, source_target_pairs={{0,2},{2,0},{1,3},{3,1},{4,6},{6,4},{5,7},{7,5},{8,10},{10,8},{9,1... | collective-permute-start | bytes 491528 | tf_op jit(solution)/shard_map/ppermute | solution.py:114
  56.0 5.5 %collective-permute-start.4 = (bf16[64,1280]{1,0:T(8,128)(2,1)S(1)}, bf16[64,1280]{1,0:T(8,128)(2,1)S(1)}, u32[]{:S(2)}, u32[]{:S(2)}) collective-permute-start(bf16[64,1280]{1,0:T(8,128)(2,1)S(1)} %get-tuple-element.14), channel_id=1, source_target_pairs={{0,2},{2,0},{1,3},{3,1},{4,6},{6,4},{5,7},{7,5},{8,10},{10,8},{9,1... | collective-permute-start | bytes 491528 | tf_op jit(solution)/shard_map/ppermute | solution.py:114
  61.7 9.0 %collective-permute-start.11 = (bf16[64,1280]{1,0:T(8,128)(2,1)S(1)}, bf16[64,1280]{1,0:T(8,128)(2,1)S(1)}, u32[]{:S(2)}, u32[]{:S(2)}) collective-permute-start(bf16[64,1280]{1,0:T(8,128)(2,1)S(1)} %get-tuple-element.27), channel_id=1, source_target_pairs={{0,4},{4,8},{8,12},{12,0},{1,5},{5,9},{9,13},{13,1},{2,6},{6,10},{... | collective-permute-start | bytes 491528 | tf_op jit(solution)/shard_map/ppermute | solution.py:114
  63.2 11.0 %collective-permute-start.5 = (bf16[64,1280]{1,0:T(8,128)(2,1)S(1)}, bf16[64,1280]{1,0:T(8,128)(2,1)S(1)}, u32[]{:S(2)}, u32[]{:S(2)}) collective-permute-start(bf16[64,1280]{1,0:T(8,128)(2,1)S(1)} %get-tuple-element.25), channel_id=1, source_target_pairs={{0,4},{4,8},{8,12},{12,0},{1,5},{5,9},{9,13},{13,1},{2,6},{6,10},{... | collective-permute-start | bytes 491528 | tf_op jit(solution)/shard_map/ppermute | solution.py:114
  64.8 12.0 %collective-permute-start.7 = (bf16[64,1280]{1,0:T(8,128)(2,1)S(1)}, bf16[64,1280]{1,0:T(8,128)(2,1)S(1)}, u32[]{:S(2)}, u32[]{:S(2)}) collective-permute-start(bf16[64,1280]{1,0:T(8,128)(2,1)S(1)} %get-tuple-element.26), channel_id=1, source_target_pairs={{0,4},{4,8},{8,12},{12,0},{1,5},{5,9},{9,13},{13,1},{2,6},{6,10},{... | collective-permute-start | bytes 491528 | tf_op jit(solution)/shard_map/ppermute | solution.py:114
  64.9 13.7 %collective-permute-start.9 = (bf16[64,1280]{1,0:T(8,128)(2,1)S(1)}, bf16[64,1280]{1,0:T(8,128)(2,1)S(1)}, u32[]{:S(2)}, u32[]{:S(2)}) collective-permute-start(bf16[64,1280]{1,0:T(8,128)(2,1)S(1)} %get-tuple-element.28), channel_id=1, source_target_pairs={{0,4},{4,8},{8,12},{12,0},{1,5},{5,9},{9,13},{13,1},{2,6},{6,10},{... | collective-permute-start | bytes 491528 | tf_op jit(solution)/shard_map/ppermute | solution.py:114

commit v2 on v1

v2 whole, which is shorter than its diff:
```python
import functools
import math

import jax
import jax.numpy as jnp
from jax import lax
from jax.experimental import pallas as pl
from jax.experimental.pallas import tpu as pltpu
from jax.sharding import PartitionSpec as P

HD = 128
CHUNKS = 4
NEG_BIG = -1e30
VMEM_LIMIT = 12 * 1024 * 1024


def send_order(spans, cores, rows, span_id, core_id):
    groups = []
    for l in range(cores - 1, -1, -1):
        starts = []
        for k in range(spans - 1, -1, -1):
            block = lax.rem(span_id + k, spans) * cores + lax.rem(core_id + l, cores)
            starts.append(pl.multiple_of(block * rows, rows))
        groups.append(starts)
    return groups


def scores_of(q, keys):
    return lax.dot_general(
        q, keys, (((1,), (1,)), ((), ())), preferred_element_type=jnp.float32
    )


def first_kernel(
    spans, cores, places, q_ref, own_ref, prev_ref, acc_ref, den_ref, top_ref, v_ext
):
    span_tok, width = q_ref.shape
    rows = span_tok // (spans * cores)
    factor = math.log2(math.e) / math.sqrt(HD)
    col = lax.broadcasted_iota(jnp.int32, (1, span_tok), 1)
    prev_mask = col >= span_tok - places[2]
    v_ext[:, HD:] = jnp.ones((2 * span_tok, HD), v_ext.dtype)
    starts = sum(send_order(spans, cores, rows, places[0], places[1]), [])
    for h in range(width // HD):
        head = slice(h * HD, (h + 1) * HD)
        q = jnp.concatenate([q_ref[pl.ds(s, rows), head] for s in starts], axis=0)
        s_prev = jnp.where(prev_mask, scores_of(q, prev_ref[0, 0, :, head]), NEG_BIG)
        s_own = scores_of(q, own_ref[0, 0, :, head])
        scores = jnp.concatenate([s_prev, s_own], axis=1)
        top = jnp.max(scores, axis=1, keepdims=True)
        probs = jnp.exp2((scores - top) * factor).astype(jnp.bfloat16)
        v_ext[:span_tok, :HD] = prev_ref[1, 0, :, head]
        v_ext[span_tok:, :HD] = own_ref[1, 0, :, head]
        both = jnp.dot(probs, v_ext[...], preferred_element_type=jnp.float32)
        acc_ref[:, head] = both[:, :HD]
        den_ref[:, head] = both[:, HD:]
        top_ref[:, head] = jnp.broadcast_to(top, (span_tok, HD))


def second_kernel(
    spans, cores, l, places, q_ref, next_ref, acc_ref, den_ref, top_ref, out_ref, v_ext
):
    span_tok, width = q_ref.shape
    rows = span_tok // (spans * cores)
    factor = math.log2(math.e) / math.sqrt(HD)
    col = lax.broadcasted_iota(jnp.int32, (1, span_tok), 1)
    next_mask = col < places[3]
    v_ext[:, HD:] = jnp.ones((span_tok, HD), v_ext.dtype)
    starts = send_order(spans, cores, rows, places[0], places[1])[cores - 1 - l]
    part = slice((cores - 1 - l) * spans * rows, (cores - l) * spans * rows)
    for h in range(width // HD):
        head = slice(h * HD, (h + 1) * HD)
        q = jnp.concatenate([q_ref[pl.ds(s, rows), head] for s in starts], axis=0)
        scores = jnp.where(next_mask, scores_of(q, next_ref[0, 0, :, head]), NEG_BIG)
        before = top_ref[part, head]
        top = jnp.maximum(before, jnp.max(scores, axis=1, keepdims=True))
        probs = jnp.exp2((scores - top[:, :1]) * factor).astype(jnp.bfloat16)
        fade = jnp.exp2((before - top) * factor)
        v_ext[:, :HD] = next_ref[1, 0, :, head]
        both = jnp.dot(probs, v_ext[...], preferred_element_type=jnp.float32)
        weighted = acc_ref[part, head] * fade + both[:, :HD]
        total = den_ref[part, head] * fade + both[:, HD:]
        out_ref[:, head] = (weighted / total).astype(out_ref.dtype)


SMEM_SPEC = pl.BlockSpec(memory_space=pltpu.SMEM)
VMEM_SPEC = pl.BlockSpec(memory_space=pltpu.VMEM)


def attend_first(spans, cores, places, queries, own, before):
    span_tok, width = queries.shape
    state = jax.ShapeDtypeStruct((span_tok, width), jnp.float32)
    return pl.pallas_call(
        functools.partial(first_kernel, spans, cores),
        out_shape=(state,) * 3,
        in_specs=[SMEM_SPEC] + [VMEM_SPEC] * 3,
        out_specs=(VMEM_SPEC,) * 3,
        scratch_shapes=[pltpu.VMEM((2 * span_tok, 2 * HD), jnp.bfloat16)],
        compiler_params=pltpu.CompilerParams(vmem_limit_bytes=VMEM_LIMIT),
        cost_estimate=pl.CostEstimate(
            flops=8 * span_tok * span_tok * width,
            bytes_accessed=22 * span_tok * width,
            transcendentals=2 * span_tok * span_tok * width // HD,
        ),
        name="attend_first",
    )(places, queries, own, before)


def attend_second(spans, cores, l, places, queries, after, state):
    span_tok, width = queries.shape
    return pl.pallas_call(
        functools.partial(second_kernel, spans, cores, l),
        out_shape=jax.ShapeDtypeStruct((span_tok // cores, width), jnp.bfloat16),
        in_specs=[SMEM_SPEC] + [VMEM_SPEC] * 5,
        out_specs=VMEM_SPEC,
        scratch_shapes=[pltpu.VMEM((span_tok, 2 * HD), jnp.bfloat16)],
        compiler_params=pltpu.CompilerParams(vmem_limit_bytes=VMEM_LIMIT),
        cost_estimate=pl.CostEstimate(
            flops=4 * span_tok * span_tok * width // cores,
            bytes_accessed=10 * span_tok * width,
            transcendentals=span_tok * span_tok * width // HD // cores,
        ),
        name="attend_second",
    )(places, queries, after, *state)


def project_kernel(parts, rows, first, *refs):
    att, weights, outs = refs[:parts], refs[parts : 2 * parts], refs[2 * parts :]
    columns = outs[-1].shape[1]
    tile = math.gcd(columns, 256)
    for t in range(0, columns, tile):
        total = None
        for a, w in zip(att, weights):
            term = jnp.dot(
                a[...], w[:, first + t : first + t + tile], preferred_element_type=jnp.float32
            )
            total = term if total is None else total + term
        for i, out in enumerate(outs):
            out[:, t : t + tile] = total[i * rows : (i + 1) * rows].astype(out.dtype)


def project(att, weights, rows, first, columns):
    parts = len(att)
    all_rows, depth = att[0].shape
    send = jax.ShapeDtypeStruct((rows, columns), jnp.bfloat16)
    keep = jax.ShapeDtypeStruct((rows, columns), jnp.float32)
    blocks = all_rows // rows
    return pl.pallas_call(
        functools.partial(project_kernel, parts, rows, first),
        out_shape=(send,) * (blocks - 1) + (keep,),
        in_specs=[VMEM_SPEC] * (2 * parts),
        out_specs=(VMEM_SPEC,) * blocks,
        compiler_params=pltpu.CompilerParams(vmem_limit_bytes=VMEM_LIMIT),
        cost_estimate=pl.CostEstimate(
            flops=2 * parts * all_rows * depth * columns,
            bytes_accessed=2 * parts * depth * columns,
            transcendentals=0,
        ),
        name="project",
    )(*att, *weights)


def combine_kernel(first, level, latents_ref, gate_ref, keep_ref, *refs):
    others, out_ref = refs[:-1], refs[-1]
    part = slice(first, first + keep_ref.shape[1])
    total = keep_ref[...]
    for other in others:
        total += other[...].astype(jnp.float32)
    gate = gate_ref[pl.ds(level[0], 1), part]
    out_ref[...] = (latents_ref[:, part].astype(jnp.float32) + gate * total).astype(out_ref.dtype)


def combine(level, latents, gates, keep, others, first):
    rows, columns = keep.shape
    return pl.pallas_call(
        functools.partial(combine_kernel, first),
        out_shape=jax.ShapeDtypeStruct((rows, columns), latents.dtype),
        in_specs=[SMEM_SPEC] + [VMEM_SPEC] * (3 + len(others)),
        out_specs=VMEM_SPEC,
        compiler_params=pltpu.CompilerParams(vmem_limit_bytes=VMEM_LIMIT),
        cost_estimate=pl.CostEstimate(
            flops=4 * rows * columns, bytes_accessed=12 * rows * columns, transcendentals=0
        ),
        name="combine",
    )(level, latents, gates, keep, *others)


def rotate(value, axis, steps):
    count = lax.axis_size(axis)
    return lax.ppermute(value, axis, [(i, (i + steps) % count) for i in range(count)])


def shards(queries, keys_values, latents, out_weight, gate_table, level_index, pair_window):
    sections, spans, cores = (lax.axis_size(a) for a in ("section", "span", "mp"))
    section_id = lax.axis_index("section")
    rows = latents.shape[1]
    final_pair = pair_window.shape[0] - 1
    prev_width = jnp.where(section_id > 0, pair_window[jnp.clip(section_id - 1, 0, final_pair)], 0)
    next_width = jnp.where(
        section_id < sections - 1, pair_window[jnp.clip(section_id, 0, final_pair)], 0
    )
    places = jnp.stack(
        [lax.axis_index("span"), lax.axis_index("mp"), prev_width, next_width]
    ).astype(jnp.int32)
    up = [(i, i + 1) for i in range(sections - 1)]
    down = [(j, i) for i, j in up]
    before = lax.ppermute(keys_values, "section", up)
    after = lax.ppermute(keys_values, "section", down)
    weights = [out_weight] + [rotate(out_weight, "mp", l) for l in range(1, cores)]
    own_queries, own_latents = queries[0], latents[0]
    state = attend_first(spans, cores, places, own_queries, keys_values, before)
    att = []
    for l in range(cores - 1, -1, -1):
        out = attend_second(spans, cores, l, places, own_queries, after, state)
        att.insert(0, out if l == 0 else rotate(out, "mp", l))

    columns = latents.shape[2] // CHUNKS
    pieces = []
    for first in range(0, latents.shape[2], columns):
        *send, keep = project(att, weights, rows, first, columns)
        others = [rotate(send[spans - 1 - k], "span", k) for k in range(1, spans)]
        updated = combine(level_index, own_latents, gate_table, keep, others, first)
        pieces.append(rotate(updated, "section", 1))
    return jnp.concatenate(pieces, axis=1)[None]


def solution(mesh):
    in_specs = (
        P(("group", "section"), None, ("span", "mp")),
        P(None, ("group", "section"), None, ("span", "mp")),
        P(("group", "section"), ("span", "mp"), None),
        P(("span", "mp"), None),
        P(),
        P(("group", "section")),
        P("group"),
    )
    out_specs = P(("group", "section"), ("span", "mp"), None)
    return jax.shard_map(shards, mesh=mesh, in_specs=in_specs, out_specs=out_specs, check_vma=False)
```

time: 79.8 us -> 81.4 us (1.020)
  Pallas kernels: 15.9 us -> 25.8 us
  waiting for transfers between devices: 40 us -> 31 us
  starting transfers between devices: 15.7 us -> 17.4 us
  local copies, waits for them, and re-layouts: 4.61 us -> 3.68 us
    pallas_call x5 -> x11, Pallas kernels: 15.9 us -> 25.8 us  [the longest x4 19.5 us: project(): pl.pallas_call(functools.partial(project_kernel, parts, rows, first), out...]
    ppermute x10, waiting for transfers between devices: 16.6 us -> 11.8 us  [rotate(): lax.ppermute(value, axis, [(i, (i + steps) % count) for i in range(count)])]
    ppermute x1, waiting for transfers between devices: 4.08 us -> 0.01 us  [shards(): after = lax.ppermute(keys_values, 'section', down)]
    ppermute x10, starting transfers between devices: 9.84 us -> 11.6 us  [rotate(): lax.ppermute(value, axis, [(i, (i + steps) % count) for i in range(count)])]
    slice x2 -> x0, local copies, waits for them, and re-layouts: 1 us -> none  [the longest x1 0.96 us: shards(): gate_row[None, part] * total]
    unnamed x6 -> x10, local copies, waits for them, and re-layouts: 2.27 us -> 2.28 us
  transfers between devices with their start and end apart: 12 -> 12, of which waited for: 8 -> 5; matrix products, arithmetic and copies ran while one was open for 3% -> 2% of each run, Pallas kernels for 16% -> 26%
where the time goes in v2:
time: 81.4 us; the launch traced here: 81 us
  waiting for transfers between devices  31 us (38%)
  Pallas kernels  25.8 us (32%)
  starting transfers between devices  17.4 us (21%)
  local copies, waits for them, and re-layouts  3.68 us (5%)
  between operations  2.17 us (3%)
  other arithmetic  0.96 us (1%)
    pallas_call x4, Pallas kernels, project(): pl.pallas_call(functools.partial(project_kernel, parts, rows, first), out...  19.5 us
    ppermute x1, waiting for transfers between devices, shards(): before = lax.ppermute(keys_values, 'section', up)  19.2 us
    ppermute x10, waiting for transfers between devices, rotate(): lax.ppermute(value, axis, [(i, (i + steps) % count) for i in range(count)])  11.8 us
    ppermute x10, starting transfers between devices, rotate(): lax.ppermute(value, axis, [(i, (i + steps) % count) for i in range(count)])  11.6 us
    ppermute x1, starting transfers between devices, shards(): before = lax.ppermute(keys_values, 'section', up)  4.53 us
    pallas_call x2, Pallas kernels, attend_second(): pl.pallas_call(functools.partial(second_kernel, spans, cores, l), out_sha...  3.61 us
    pallas_call x1, Pallas kernels, attend_first(): pl.pallas_call(functools.partial(first_kernel, spans, cores), out_shape=(...  2.4 us
    unnamed x10, local copies, waits for them, and re-layouts  2.28 us
  transfers between devices with their start and end apart: 12, of which 5 were waited for; matrix products, arithmetic and copies ran while one was open for 2% of the time, Pallas kernels for 26%

profile of v2, /device:TPU:0, one launch (start us, length us, event | category | flops | bytes accessed | tf_op | source)
XLA Modules:
  0.0 81.0 jit_solution(9463436187656760340)
XLA Ops:
  0.0 0.5 collective-permute-start.3
  0.5 4.5 %collective-permute-start.1 = (bf16[2,1,256,1024]{3,2,1,0:T(8,128)(2,1)}, bf16[2,1,256,1024]{3,2,1,0:T(8,128)(2,1)S(1)}, u32[]{:S(2)}, u32[]{:S(2)}) collective-permute-start(bf16[2,1,256,1024]{3,2,1,0:T(8,128)(2,1)} %own_ref.1), channel_id=1, source_target_pairs={{0,4},{4,8},{8,12},{1,5},{5,9},{9,13},{2,6},{6,10},{10,14},{3,7},{... | collective-permute-start | bytes 3145736 | tf_op jit(solution)/shard_map/ppermute | solution.py:207
  5.0 1.3 %collective-permute-start = (bf16[2,1,256,1024]{3,2,1,0:T(8,128)(2,1)}, bf16[2,1,256,1024]{3,2,1,0:T(8,128)(2,1)S(1)}, u32[]{:S(2)}, u32[]{:S(2)}) collective-permute-start(bf16[2,1,256,1024]{3,2,1,0:T(8,128)(2,1)} %own_ref.1), channel_id=1, source_target_pairs={{4,0},{8,4},{12,8},{5,1},{9,5},{13,9},{6,2},{10,6},{14,10},{7,3},{... | collective-permute-start | bytes 3145736 | tf_op jit(solution)/shard_map/ppermute | solution.py:208
  6.3 1.4 %fusion = (s32[1]{0:T(128)}, s32[1]{0:T(128)}) fusion(s32[3]{0:T(128)} %param.13, s32[]{:T(128)S(6)} %min.7, s32[]{:T(128)S(6)} %min.8), kind=kLoop, calls=%fused_computation.2 | loop fusion | bytes 24 | tf_op jit(solution)/shard_map/dynamic_slice | solution.py:198
  9.1 0.1 pad_add_fusion.places
  9.1 19.2 %collective-permute-done.1.prev_ref = bf16[2,1,256,1024]{3,2,1,0:T(8,128)(2,1)S(1)} collective-permute-done((bf16[2,1,256,1024]{3,2,1,0:T(8,128)(2,1)}, bf16[2,1,256,1024]{3,2,1,0:T(8,128)(2,1)S(1)}, u32[]{:S(2)}, u32[]{:S(2)}) %collective-permute-start.1) | collective-permute-done | bytes 1048608 | tf_op jit(solution)/shard_map/ppermute | solution.py:207
  28.3 1.0 %copy-done.2 = bf16[1,256,1024]{2,1,0:T(8,128)(2,1)S(1)} copy-done((bf16[1,256,1024]{2,1,0:T(8,128)(2,1)S(1)}, bf16[1,256,1024]{2,1,0:T(8,128)(2,1)}, u32[]{:S(2)}) %copy-start.2) | copy-done | bytes 524312
  29.4 1.2 %copy-done.4 = bf16[2,1,256,1024]{3,2,1,0:T(8,128)(2,1)S(1)} copy-done((bf16[2,1,256,1024]{3,2,1,0:T(8,128)(2,1)S(1)}, bf16[2,1,256,1024]{3,2,1,0:T(8,128)(2,1)}, u32[]{:S(2)}) %copy-start.4) | copy-done | bytes 1048600
  30.6 2.4 %attend_first.1 = (f32[256,1024]{1,0:T(8,128)S(1)}, f32[256,1024]{1,0:T(8,128)S(1)}, f32[256,1024]{1,0:T(8,128)S(1)}) custom-call(s32[4]{0:T(128)S(1)} %pad_add_fusion.places, bf16[256,1024]{1,0:T(8,128)(2,1)S(1)} %bitcast.14, bf16[2,1,256,1024]{3,2,1,0:T(8,128)(2,1)S(1)} %copy-done.4, bf16[2,1,256,1024]{3,2,1,0:T(8,128)(2,1)S(1)} %collective-permute-done.1.prev_ref), custom_call_target="tpu_custom_call" | custom-call | flops 536870912 | bytes 5767168 | tf_op jit(solution)/shard_map/attend_first/pallas_call | solution.py:93
  33.0 1.8 %attend_second.3 = bf16[128,1024]{1,0:T(8,128)(2,1)S(1)} custom-call(s32[4]{0:T(128)S(1)} %pad_add_fusion.places, bf16[256,1024]{1,0:T(8,128)(2,1)S(1)} %bitcast.15, bf16[2,1,256,1024]{3,2,1,0:T(8,128)(2,1)S(1)} %collective-permute-done.next_ref, f32[256,1024]{1,0:T(8,128)S(1)} %get-tuple-element.16.acc_ref, f32[256,1024]{1,0:T(8,128)S(1)} %get-tuple-element.17.den_ref, ...), custom_call_target="tpu_custom_call" | custom-call | flops 134217728 | bytes 2621440 | tf_op jit(solution)/shard_map/attend_second/pallas_call | solution.py:111
  34.9 1.8 %attend_second.2.refs_0_ = bf16[128,1024]{1,0:T(8,128)(2,1)S(1)} custom-call(s32[4]{0:T(128)S(1)} %pad_add_fusion.places, bf16[256,1024]{1,0:T(8,128)(2,1)S(1)} %bitcast.16, bf16[2,1,256,1024]{3,2,1,0:T(8,128)(2,1)S(1)} %collective-permute-done.next_ref, f32[256,1024]{1,0:T(8,128)S(1)} %get-tuple-element.16.acc_ref, ...), custom_call_target="tpu_custom_call" | custom-call | flops 134217728 | bytes 2621440 | tf_op jit(solution)/shard_map/attend_second/pallas_call | solution.py:111
  36.7 4.9 %project.7 = (bf16[64,1280]{1,0:T(8,128)(2,1)S(1)}, f32[64,1280]{1,0:T(8,128)S(1)}) custom-call(bf16[128,1024]{1,0:T(8,128)(2,1)S(1)} %attend_second.2.refs_0_, bf16[128,1024]{1,0:T(8,128)(2,1)S(1)} %collective-permute-done.2.refs_1_, bf16[1024,5120]{1,0:T(8,128)(2,1)S(1)} %copy-done, bf16[1024,5120]{1,0:T(8,128)(2,1)} %collective-permute-done.3.refs_3_), custom_call_target="tpu_custom_call" | custom-call | flops 671088640 | bytes 5242880 | tf_op jit(solution)/shard_map/project/pallas_call | solution.py:148
  41.6 1.6 %collective-permute-start.10 = (bf16[64,1280]{1,0:T(8,128)(2,1)S(1)}, bf16[64,1280]{1,0:T(8,128)(2,1)S(1)}, u32[]{:S(2)}, u32[]{:S(2)}) collective-permute-start(bf16[64,1280]{1,0:T(8,128)(2,1)S(1)} %get-tuple-element.26), channel_id=1, source_target_pairs={{0,2},{2,0},{1,3},{3,1},{4,6},{6,4},{5,7},{7,5},{8,10},{10,8},{9,1... | collective-permute-start | bytes 491528 | tf_op jit(solution)/shard_map/ppermute | solution.py:190
  43.2 4.9 %project.6 = (bf16[64,1280]{1,0:T(8,128)(2,1)S(1)}, f32[64,1280]{1,0:T(8,128)S(1)}) custom-call(bf16[128,1024]{1,0:T(8,128)(2,1)S(1)} %attend_second.2.refs_0_, bf16[128,1024]{1,0:T(8,128)(2,1)S(1)} %collective-permute-done.2.refs_1_, bf16[1024,5120]{1,0:T(8,128)(2,1)S(1)} %copy-done, bf16[1024,5120]{1,0:T(8,128)(2,1)} %collective-permute-done.3.refs_3_), custom_call_target="tpu_custom_call" | custom-call | flops 671088640 | bytes 5242880 | tf_op jit(solution)/shard_map/project/pallas_call | solution.py:148
  48.1 0.6 collective-permute-start.8
  48.7 4.9 %project.5 = (bf16[64,1280]{1,0:T(8,128)(2,1)S(1)}, f32[64,1280]{1,0:T(8,128)S(1)}) custom-call(bf16[128,1024]{1,0:T(8,128)(2,1)S(1)} %attend_second.2.refs_0_, bf16[128,1024]{1,0:T(8,128)(2,1)S(1)} %collective-permute-done.2.refs_1_, bf16[1024,5120]{1,0:T(8,128)(2,1)S(1)} %copy-done, bf16[1024,5120]{1,0:T(8,128)(2,1)} %collective-permute-done.3.refs_3_), custom_call_target="tpu_custom_call" | custom-call | flops 671088640 | bytes 5242880 | tf_op jit(solution)/shard_map/project/pallas_call | solution.py:148
  53.6 1.6 %collective-permute-start.6 = (bf16[64,1280]{1,0:T(8,128)(2,1)S(1)}, bf16[64,1280]{1,0:T(8,128)(2,1)S(1)}, u32[]{:S(2)}, u32[]{:S(2)}) collective-permute-start(bf16[64,1280]{1,0:T(8,128)(2,1)S(1)} %get-tuple-element.22), channel_id=1, source_target_pairs={{0,2},{2,0},{1,3},{3,1},{4,6},{6,4},{5,7},{7,5},{8,10},{10,8},{9,1... | collective-permute-start | bytes 491528 | tf_op jit(solution)/shard_map/ppermute | solution.py:190
  55.1 4.9 %project.4 = (bf16[64,1280]{1,0:T(8,128)(2,1)S(1)}, f32[64,1280]{1,0:T(8,128)S(1)}) custom-call(bf16[128,1024]{1,0:T(8,128)(2,1)S(1)} %attend_second.2.refs_0_, bf16[128,1024]{1,0:T(8,128)(2,1)S(1)} %collective-permute-done.2.refs_1_, bf16[1024,5120]{1,0:T(8,128)(2,1)S(1)} %copy-done, bf16[1024,5120]{1,0:T(8,128)(2,1)} %collective-permute-done.3.refs_3_), custom_call_target="tpu_custom_call" | custom-call | flops 671088640 | bytes 5242880 | tf_op jit(solution)/shard_map/project/pallas_call | solution.py:148
  60.0 0.6 collective-permute-start.4
  61.3 0.1 combine.7
  61.4 2.4 %collective-permute-start.11 = (bf16[64,1280]{1,0:T(8,128)(2,1)S(1)}, bf16[64,1280]{1,0:T(8,128)(2,1)S(1)}, u32[]{:S(2)}, u32[]{:S(2)}) collective-permute-start(bf16[64,1280]{1,0:T(8,128)(2,1)S(1)} %combine.7), channel_id=1, source_target_pairs={{0,4},{4,8},{8,12},{12,0},{1,5},{5,9},{9,13},{13,1},{2,6},{6,10},{... | collective-permute-start | bytes 491528 | tf_op jit(solution)/shard_map/ppermute | solution.py:190
  63.8 0.1 combine.6
  63.9 1.6 %collective-permute-start.9 = (bf16[64,1280]{1,0:T(8,128)(2,1)S(1)}, bf16[64,1280]{1,0:T(8,128)(2,1)S(1)}, u32[]{:S(2)}, u32[]{:S(2)}) collective-permute-start(bf16[64,1280]{1,0:T(8,128)(2,1)S(1)} %combine.6), channel_id=1, source_target_pairs={{0,4},{4,8},{8,12},{12,0},{1,5},{5,9},{9,13},{13,1},{2,6},{6,10},{... | collective-permute-start | bytes 491528 | tf_op jit(solution)/shard_map/ppermute | solution.py:190
  65.5 0.1 combine.5
  65.6 1.6 %collective-permute-start.7 = (bf16[64,1280]{1,0:T(8,128)(2,1)S(1)}, bf16[64,1280]{1,0:T(8,128)(2,1)S(1)}, u32[]{:S(2)}, u32[]{:S(2)}) collective-permute-start(bf16[64,1280]{1,0:T(8,128)(2,1)S(1)} %combine.5), channel_id=1, source_target_pairs={{0,4},{4,8},{8,12},{12,0},{1,5},{5,9},{9,13},{13,1},{2,6},{6,10},{... | collective-permute-start | bytes 491528 | tf_op jit(solution)/shard_map/ppermute | solution.py:190
  67.2 0.1 combine.4
  67.3 1.1 %collective-permute-start.5 = (bf16[64,1280]{1,0:T(8,128)(2,1)S(1)}, bf16[64,1280]{1,0:T(8,128)(2,1)S(1)}, u32[]{:S(2)}, u32[]{:S(2)}) collective-permute-start(bf16[64,1280]{1,0:T(8,128)(2,1)S(1)} %combine.4), channel_id=1, source_target_pairs={{0,4},{4,8},{8,12},{12,0},{1,5},{5,9},{9,13},{13,1},{2,6},{6,10},{... | collective-permute-start | bytes 491528 | tf_op jit(solution)/shard_map/ppermute | solution.py:190
  68.3 2.6 %collective-permute-done.11 = bf16[64,1280]{1,0:T(8,128)(2,1)S(1)} collective-permute-done((bf16[64,1280]{1,0:T(8,128)(2,1)S(1)}, bf16[64,1280]{1,0:T(8,128)(2,1)S(1)}, u32[]{:S(2)}, u32[]{:S(2)}) %collective-permute-start.11) | collective-permute-done | bytes 163872 | tf_op jit(solution)/shard_map/ppermute | solution.py:190
  70.9 3.5 %collective-permute-done.9 = bf16[64,1280]{1,0:T(8,128)(2,1)S(1)} collective-permute-done((bf16[64,1280]{1,0:T(8,128)(2,1)S(1)}, bf16[64,1280]{1,0:T(8,128)(2,1)S(1)}, u32[]{:S(2)}, u32[]{:S(2)}) %collective-permute-start.9) | collective-permute-done | bytes 163872 | tf_op jit(solution)/shard_map/ppermute | solution.py:190
  74.4 3.5 %collective-permute-done.7 = bf16[64,1280]{1,0:T(8,128)(2,1)S(1)} collective-permute-done((bf16[64,1280]{1,0:T(8,128)(2,1)S(1)}, bf16[64,1280]{1,0:T(8,128)(2,1)S(1)}, u32[]{:S(2)}, u32[]{:S(2)}) %collective-permute-start.7) | collective-permute-done | bytes 163872 | tf_op jit(solution)/shard_map/ppermute | solution.py:190
  77.9 2.2 %collective-permute-done.5 = bf16[64,1280]{1,0:T(8,128)(2,1)S(1)} collective-permute-done((bf16[64,1280]{1,0:T(8,128)(2,1)S(1)}, bf16[64,1280]{1,0:T(8,128)(2,1)S(1)}, u32[]{:S(2)}, u32[]{:S(2)}) %collective-permute-start.5) | collective-permute-done | bytes 163872 | tf_op jit(solution)/shard_map/ppermute | solution.py:190
  80.1 0.9 %maximum_bitcast_fusion = bf16[1,64,5120]{2,1,0:T(8,128)(2,1)} fusion(bf16[64,1280]{1,0:T(8,128)(2,1)S(1)} %collective-permute-done.11, bf16[64,1280]{1,0:T(8,128)(2,1)S(1)} %collective-permute-done.9, bf16[64,1280]{1,0:T(8,128)(2,1)S(1)} %collective-permute-done.7, bf16[64,1280]{1,0:T(8,128)(2,1)S(1)} %collective-permute-done.5), kind=kLoop, calls=%fused_computation | loop fusion | flops 2621440 | bytes 1310720 | tf_op jit(solution)/shard_map/broadcast_in_dim | solution.py:224
  (16 shorter events, 0.1 us)
Async XLA Ops:
  0.0 36.7 %collective-permute-start.3 = (bf16[1024,5120]{1,0:T(8,128)(2,1)}, bf16[1024,5120]{1,0:T(8,128)(2,1)}, u32[]{:S(2)}, u32[]{:S(2)}) collective-permute-start(bf16[1024,5120]{1,0:T(8,128)(2,1)} %refs_2_.7), channel_id=1, source_target_pairs={{0,1},{1,0},{2,3},{3,2},{4,5},{5,4},{6,7},{7,6},{8,9},{9,8},{10,11... | collective-permute-start | bytes 31457288 | tf_op jit(solution)/shard_map/ppermute | solution.py:190
  0.5 27.9 %collective-permute-start.1 = (bf16[2,1,256,1024]{3,2,1,0:T(8,128)(2,1)}, bf16[2,1,256,1024]{3,2,1,0:T(8,128)(2,1)S(1)}, u32[]{:S(2)}, u32[]{:S(2)}) collective-permute-start(bf16[2,1,256,1024]{3,2,1,0:T(8,128)(2,1)} %own_ref.1), channel_id=1, source_target_pairs={{0,4},{4,8},{8,12},{1,5},{5,9},{9,13},{2,6},{6,10},{10,14},{3,7},{... | collective-permute-start | bytes 3145736 | tf_op jit(solution)/shard_map/ppermute | solution.py:207
  5.0 28.0 %collective-permute-start = (bf16[2,1,256,1024]{3,2,1,0:T(8,128)(2,1)}, bf16[2,1,256,1024]{3,2,1,0:T(8,128)(2,1)S(1)}, u32[]{:S(2)}, u32[]{:S(2)}) collective-permute-start(bf16[2,1,256,1024]{3,2,1,0:T(8,128)(2,1)} %own_ref.1), channel_id=1, source_target_pairs={{4,0},{8,4},{12,8},{5,1},{9,5},{13,9},{6,2},{10,6},{14,10},{7,3},{... | collective-permute-start | bytes 3145736 | tf_op jit(solution)/shard_map/ppermute | solution.py:208
  28.3 1.0 %copy-start.2 = (bf16[1,256,1024]{2,1,0:T(8,128)(2,1)S(1)}, bf16[1,256,1024]{2,1,0:T(8,128)(2,1)}, u32[]{:S(2)}) copy-start(bf16[1,256,1024]{2,1,0:T(8,128)(2,1)} %param.7) | copy-start | bytes 1572868
  29.4 1.2 %copy-start.4 = (bf16[2,1,256,1024]{3,2,1,0:T(8,128)(2,1)S(1)}, bf16[2,1,256,1024]{3,2,1,0:T(8,128)(2,1)}, u32[]{:S(2)}) copy-start(bf16[2,1,256,1024]{3,2,1,0:T(8,128)(2,1)} %own_ref.1) | copy-start | bytes 3145732
  30.6 6.1 %copy-start = (bf16[1024,5120]{1,0:T(8,128)(2,1)S(1)}, bf16[1024,5120]{1,0:T(8,128)(2,1)}, u32[]{:S(2)}) copy-start(bf16[1024,5120]{1,0:T(8,128)(2,1)} %refs_2_.7) | copy-start | bytes 31457284
  34.8 1.9 %collective-permute-start.2 = (bf16[128,1024]{1,0:T(8,128)(2,1)S(1)}, bf16[128,1024]{1,0:T(8,128)(2,1)S(1)}, u32[]{:S(2)}, u32[]{:S(2)}) collective-permute-start(bf16[128,1024]{1,0:T(8,128)(2,1)S(1)} %attend_second.3), channel_id=1, source_target_pairs={{0,1},{1,0},{2,3},{3,2},{4,5},{5,4},{6,7},{7,6},{8,9},{9,8},{10,11... | collective-permute-start | bytes 786440 | tf_op jit(solution)/shard_map/ppermute | solution.py:190
  41.6 19.7 %collective-permute-start.10 = (bf16[64,1280]{1,0:T(8,128)(2,1)S(1)}, bf16[64,1280]{1,0:T(8,128)(2,1)S(1)}, u32[]{:S(2)}, u32[]{:S(2)}) collective-permute-start(bf16[64,1280]{1,0:T(8,128)(2,1)S(1)} %get-tuple-element.26), channel_id=1, source_target_pairs={{0,2},{2,0},{1,3},{3,1},{4,6},{6,4},{5,7},{7,5},{8,10},{10,8},{9,1... | collective-permute-start | bytes 491528 | tf_op jit(solution)/shard_map/ppermute | solution.py:190
  48.1 15.7 %collective-permute-start.8 = (bf16[64,1280]{1,0:T(8,128)(2,1)S(1)}, bf16[64,1280]{1,0:T(8,128)(2,1)S(1)}, u32[]{:S(2)}, u32[]{:S(2)}) collective-permute-start(bf16[64,1280]{1,0:T(8,128)(2,1)S(1)} %get-tuple-element.24), channel_id=1, source_target_pairs={{0,2},{2,0},{1,3},{3,1},{4,6},{6,4},{5,7},{7,5},{8,10},{10,8},{9,1... | collective-permute-start | bytes 491528 | tf_op jit(solution)/shard_map/ppermute | solution.py:190
  53.5 7.7 %copy-start.1 = (bf16[1,64,5120]{2,1,0:T(8,128)(2,1)S(1)}, bf16[1,64,5120]{2,1,0:T(8,128)(2,1)}, u32[]{:S(2)}) copy-start(bf16[1,64,5120]{2,1,0:T(8,128)(2,1)} %param.9) | copy-start | bytes 1966084
  53.6 7.7 %copy-start.3 = (f32[8,5120]{1,0:T(8,128)S(1)}, f32[8,5120]{1,0:T(8,128)}, u32[]{:S(2)}) copy-start(f32[8,5120]{1,0:T(8,128)} %gate_ref.7) | copy-start | bytes 491524
  53.6 11.9 %collective-permute-start.6 = (bf16[64,1280]{1,0:T(8,128)(2,1)S(1)}, bf16[64,1280]{1,0:T(8,128)(2,1)S(1)}, u32[]{:S(2)}, u32[]{:S(2)}) collective-permute-start(bf16[64,1280]{1,0:T(8,128)(2,1)S(1)} %get-tuple-element.22), channel_id=1, source_target_pairs={{0,2},{2,0},{1,3},{3,1},{4,6},{6,4},{5,7},{7,5},{8,10},{10,8},{9,1... | collective-permute-start | bytes 491528 | tf_op jit(solution)/shard_map/ppermute | solution.py:190
  60.0 7.2 %collective-permute-start.4 = (bf16[64,1280]{1,0:T(8,128)(2,1)S(1)}, bf16[64,1280]{1,0:T(8,128)(2,1)S(1)}, u32[]{:S(2)}, u32[]{:S(2)}) collective-permute-start(bf16[64,1280]{1,0:T(8,128)(2,1)S(1)} %get-tuple-element.20), channel_id=1, source_target_pairs={{0,2},{2,0},{1,3},{3,1},{4,6},{6,4},{5,7},{7,5},{8,10},{10,8},{9,1... | collective-permute-start | bytes 491528 | tf_op jit(solution)/shard_map/ppermute | solution.py:190
  61.4 9.6 %collective-permute-start.11 = (bf16[64,1280]{1,0:T(8,128)(2,1)S(1)}, bf16[64,1280]{1,0:T(8,128)(2,1)S(1)}, u32[]{:S(2)}, u32[]{:S(2)}) collective-permute-start(bf16[64,1280]{1,0:T(8,128)(2,1)S(1)} %combine.7), channel_id=1, source_target_pairs={{0,4},{4,8},{8,12},{12,0},{1,5},{5,9},{9,13},{13,1},{2,6},{6,10},{... | collective-permute-start | bytes 491528 | tf_op jit(solution)/shard_map/ppermute | solution.py:190
  63.9 10.6 %collective-permute-start.9 = (bf16[64,1280]{1,0:T(8,128)(2,1)S(1)}, bf16[64,1280]{1,0:T(8,128)(2,1)S(1)}, u32[]{:S(2)}, u32[]{:S(2)}) collective-permute-start(bf16[64,1280]{1,0:T(8,128)(2,1)S(1)} %combine.6), channel_id=1, source_target_pairs={{0,4},{4,8},{8,12},{12,0},{1,5},{5,9},{9,13},{13,1},{2,6},{6,10},{... | collective-permute-start | bytes 491528 | tf_op jit(solution)/shard_map/ppermute | solution.py:190
  65.6 12.4 %collective-permute-start.7 = (bf16[64,1280]{1,0:T(8,128)(2,1)S(1)}, bf16[64,1280]{1,0:T(8,128)(2,1)S(1)}, u32[]{:S(2)}, u32[]{:S(2)}) collective-permute-start(bf16[64,1280]{1,0:T(8,128)(2,1)S(1)} %combine.5), channel_id=1, source_target_pairs={{0,4},{4,8},{8,12},{12,0},{1,5},{5,9},{9,13},{13,1},{2,6},{6,10},{... | collective-permute-start | bytes 491528 | tf_op jit(solution)/shard_map/ppermute | solution.py:190
  67.3 12.8 %collective-permute-start.5 = (bf16[64,1280]{1,0:T(8,128)(2,1)S(1)}, bf16[64,1280]{1,0:T(8,128)(2,1)S(1)}, u32[]{:S(2)}, u32[]{:S(2)}) collective-permute-start(bf16[64,1280]{1,0:T(8,128)(2,1)S(1)} %combine.4), channel_id=1, source_target_pairs={{0,4},{4,8},{8,12},{12,0},{1,5},{5,9},{9,13},{13,1},{2,6},{6,10},{... | collective-permute-start | bytes 491528 | tf_op jit(solution)/shard_map/ppermute | solution.py:190

commit v3 on v2

v3 whole, which is shorter than its diff:
```python
import functools
import math

import jax
import jax.numpy as jnp
from jax import lax
from jax.experimental import pallas as pl
from jax.experimental.pallas import tpu as pltpu
from jax.sharding import PartitionSpec as P

HD = 128
CHUNKS = 4
NEG_BIG = -1e30
VMEM_LIMIT = 4 * 1024 * 1024


def scores_of(q, keys):
    return lax.dot_general(
        q, keys, (((1,), (1,)), ((), ())), preferred_element_type=jnp.float32
    )


FACTOR = math.log2(math.e) / math.sqrt(HD)


def own_kernel(q_ref, own_ref, acc_ref, den_ref, top_ref):
    rows, width = q_ref.shape
    ones = jnp.ones((own_ref.shape[2], HD), jnp.bfloat16)
    for h in range(width // HD):
        head = slice(h * HD, (h + 1) * HD)
        scores = scores_of(q_ref[:, head], own_ref[0, 0, :, head])
        top = jnp.max(scores, axis=1, keepdims=True)
        probs = jnp.exp2((scores - top) * FACTOR).astype(jnp.bfloat16)
        values = jnp.concatenate([own_ref[1, 0, :, head], ones], axis=1)
        both = jnp.dot(probs, values, preferred_element_type=jnp.float32)
        acc_ref[:, head] = both[:, :HD]
        den_ref[:, head] = both[:, HD:]
        top_ref[:, head] = jnp.broadcast_to(top, (rows, HD))


def halo_kernel(
    first, last, q_ref, halo_ref, mask_ref, acc_ref, den_ref, top_ref, *outs
):
    rows, width = outs[0].shape
    part = slice(first, first + rows)
    mask = mask_ref[...]
    ones = jnp.ones((halo_ref.shape[2], HD), jnp.bfloat16)
    for h in range(width // HD):
        head = slice(h * HD, (h + 1) * HD)
        scores = scores_of(q_ref[part, head], halo_ref[0, 0, :, head]) + mask
        before = top_ref[part, head]
        top = jnp.maximum(before, jnp.max(scores, axis=1, keepdims=True))
        probs = jnp.exp2((scores - top[:, :1]) * FACTOR).astype(jnp.bfloat16)
        fade = jnp.exp2((before - top) * FACTOR)
        values = jnp.concatenate([halo_ref[1, 0, :, head], ones], axis=1)
        both = jnp.dot(probs, values, preferred_element_type=jnp.float32)
        weighted = acc_ref[part, head] * fade + both[:, :HD]
        total = den_ref[part, head] * fade + both[:, HD:]
        if last:
            outs[0][:, head] = (weighted / total).astype(outs[0].dtype)
        else:
            outs[0][:, head] = weighted
            outs[1][:, head] = total
            outs[2][:, head] = top


SMEM_SPEC = pl.BlockSpec(memory_space=pltpu.SMEM)
VMEM_SPEC = pl.BlockSpec(memory_space=pltpu.VMEM)


def attend_own(queries, own):
    rows, width = queries.shape
    span_tok = own.shape[2]
    state = jax.ShapeDtypeStruct((rows, width), jnp.float32)
    return pl.pallas_call(
        own_kernel,
        out_shape=(state,) * 3,
        in_specs=[VMEM_SPEC] * 2,
        out_specs=(VMEM_SPEC,) * 3,
        compiler_params=pltpu.CompilerParams(vmem_limit_bytes=VMEM_LIMIT),
        cost_estimate=pl.CostEstimate(
            flops=4 * rows * span_tok * width,
            bytes_accessed=18 * span_tok * width,
            transcendentals=rows * span_tok * width // HD,
        ),
        name="attend_own",
    )(queries, own)


def attend_halo(queries, halo, mask, state, first, rows, last):
    width = queries.shape[1]
    span_tok = halo.shape[2]
    if last:
        out_shape = (jax.ShapeDtypeStruct((rows, width), jnp.bfloat16),)
    else:
        out_shape = (jax.ShapeDtypeStruct((rows, width), jnp.float32),) * 3
    return pl.pallas_call(
        functools.partial(halo_kernel, first, last),
        out_shape=out_shape,
        in_specs=[VMEM_SPEC] * 6,
        out_specs=(VMEM_SPEC,) * len(out_shape),
        compiler_params=pltpu.CompilerParams(vmem_limit_bytes=VMEM_LIMIT),
        cost_estimate=pl.CostEstimate(
            flops=4 * rows * span_tok * width,
            bytes_accessed=20 * rows * width,
            transcendentals=rows * span_tok * width // HD,
        ),
        name="attend_halo",
    )(queries, halo, mask, *state)


def hold_kernel(src_ref, dst_ref, sem):
    copy = pltpu.make_async_copy(src_ref, dst_ref, sem)
    copy.start()
    copy.wait()


def hold(array):
    return pl.pallas_call(
        hold_kernel,
        out_shape=jax.ShapeDtypeStruct(array.shape, array.dtype),
        in_specs=[pl.BlockSpec(memory_space=pl.ANY)],
        out_specs=VMEM_SPEC,
        scratch_shapes=[pltpu.SemaphoreType.DMA],
        compiler_params=pltpu.CompilerParams(vmem_limit_bytes=VMEM_LIMIT),
        cost_estimate=pl.CostEstimate(flops=0, bytes_accessed=2 * array.size * 2, transcendentals=0),
        name="hold",
    )(array)


def project_kernel(parts, rows, first, *refs):
    att, weights, outs = refs[:parts], refs[parts : 2 * parts], refs[2 * parts :]
    columns = outs[-1].shape[1]
    tile = math.gcd(columns, 256)
    for t in range(0, columns, tile):
        total = None
        for a, w in zip(att, weights):
            term = jnp.dot(
                a[...], w[:, first + t : first + t + tile], preferred_element_type=jnp.float32
            )
            total = term if total is None else total + term
        for i, out in enumerate(outs):
            out[:, t : t + tile] = total[i * rows : (i + 1) * rows].astype(out.dtype)


def project(att, weights, rows, first, columns):
    parts = len(att)
    all_rows, depth = att[0].shape
    send = jax.ShapeDtypeStruct((rows, columns), jnp.bfloat16)
    keep = jax.ShapeDtypeStruct((rows, columns), jnp.float32)
    blocks = all_rows // rows
    return pl.pallas_call(
        functools.partial(project_kernel, parts, rows, first),
        out_shape=(send,) * (blocks - 1) + (keep,),
        in_specs=[VMEM_SPEC] * (2 * parts),
        out_specs=(VMEM_SPEC,) * blocks,
        compiler_params=pltpu.CompilerParams(vmem_limit_bytes=VMEM_LIMIT),
        cost_estimate=pl.CostEstimate(
            flops=2 * parts * all_rows * depth * columns,
            bytes_accessed=2 * parts * depth * columns,
            transcendentals=0,
        ),
        name="project",
    )(*att, *weights)


def combine_kernel(first, level, latents_ref, gate_ref, keep_ref, *refs):
    others, out_ref = refs[:-1], refs[-1]
    part = slice(first, first + keep_ref.shape[1])
    total = keep_ref[...]
    for other in others:
        total += other[...].astype(jnp.float32)
    gate = gate_ref[pl.ds(level[0], 1), part]
    out_ref[...] = (latents_ref[:, part].astype(jnp.float32) + gate * total).astype(out_ref.dtype)


def combine(level, latents, gates, keep, others, first):
    rows, columns = keep.shape
    return pl.pallas_call(
        functools.partial(combine_kernel, first),
        out_shape=jax.ShapeDtypeStruct((rows, columns), latents.dtype),
        in_specs=[SMEM_SPEC] + [VMEM_SPEC] * (3 + len(others)),
        out_specs=VMEM_SPEC,
        compiler_params=pltpu.CompilerParams(vmem_limit_bytes=VMEM_LIMIT),
        cost_estimate=pl.CostEstimate(
            flops=4 * rows * columns, bytes_accessed=12 * rows * columns, transcendentals=0
        ),
        name="combine",
    )(level, latents, gates, keep, *others)


def rotate(value, axis, steps):
    count = lax.axis_size(axis)
    return lax.ppermute(value, axis, [(i, (i + steps) % count) for i in range(count)])


def shards(queries, keys_values, latents, out_weight, gate_table, level_index, pair_window):
    sections, spans, cores = (lax.axis_size(a) for a in ("section", "span", "mp"))
    section_id = lax.axis_index("section")
    rows = latents.shape[1]
    final_pair = pair_window.shape[0] - 1
    prev_width = jnp.where(section_id > 0, pair_window[jnp.clip(section_id - 1, 0, final_pair)], 0)
    next_width = jnp.where(
        section_id < sections - 1, pair_window[jnp.clip(section_id, 0, final_pair)], 0
    )
    up = [(i, i + 1) for i in range(sections - 1)]
    down = [(j, i) for i, j in up]
    before = lax.ppermute(keys_values, "section", up)
    after = lax.ppermute(keys_values, "section", down)
    weights = [hold(out_weight)]
    weights += [hold(rotate(out_weight, "mp", l)) for l in range(1, cores)]
    own_latents = latents[0]
    span_tok = queries.shape[1]
    span_id, core_id = lax.axis_index("span"), lax.axis_index("mp")
    blocks = queries[0].reshape(spans * cores, rows, -1)
    order = []
    for l in range(cores - 1, -1, -1):
        for k in range(spans - 1, -1, -1):
            block = (span_id + k) % spans * cores + (core_id + l) % cores
            order.append(lax.dynamic_index_in_dim(blocks, block, keepdims=False))
    own_queries = jnp.concatenate(order, axis=0)
    col = jnp.arange(span_tok, dtype=jnp.int32)[None]
    prev_mask = jnp.where(col >= span_tok - prev_width, 0.0, NEG_BIG).astype(jnp.float32)
    next_mask = jnp.where(col < next_width, 0.0, NEG_BIG).astype(jnp.float32)

    state = attend_own(own_queries, keys_values)
    state, weights = lax.optimization_barrier((state, weights))
    state = attend_halo(own_queries, before, prev_mask, state, 0, span_tok, False)
    per_core = spans * rows
    att = []
    for l in range(cores - 1, -1, -1):
        start = (cores - 1 - l) * per_core
        (out,) = attend_halo(own_queries, after, next_mask, state, start, per_core, True)
        att.insert(0, out if l == 0 else rotate(out, "mp", l))

    columns = latents.shape[2] // CHUNKS
    pieces = []
    for first in range(0, latents.shape[2], columns):
        *send, keep = project(att, weights, rows, first, columns)
        others = [rotate(send[spans - 1 - k], "span", k) for k in range(1, spans)]
        updated = combine(level_index, own_latents, gate_table, keep, others, first)
        pieces.append(rotate(updated, "section", 1))
    return jnp.concatenate(pieces, axis=1)[None]


def solution(mesh):
    in_specs = (
        P(("group", "section"), None, ("span", "mp")),
        P(None, ("group", "section"), None, ("span", "mp")),
        P(("group", "section"), ("span", "mp"), None),
        P(("span", "mp"), None),
        P(),
        P(("group", "section")),
        P("group"),
    )
    out_specs = P(("group", "section"), ("span", "mp"), None)
    return jax.shard_map(shards, mesh=mesh, in_specs=in_specs, out_specs=out_specs, check_vma=False)
```

time: 81.4 us -> 62.6 us (0.77)
  waiting for transfers between devices: 31 us -> 18.3 us
  Pallas kernels: 25.8 us -> 14.2 us
  local copies, waits for them, and re-layouts: 3.68 us -> 9.8 us
    pallas_call x4, Pallas kernels: 19.5 us -> 3.45 us  [project(): pl.pallas_call(functools.partial(project_kernel, parts, rows, first), out...]
    ppermute x1, waiting for transfers between devices: 19.2 us -> 5.01 us  [shards(): before = lax.ppermute(keys_values, 'section', up)]
    unnamed x10 -> x18, local copies, waits for them, and re-layouts: 2.28 us -> 8.01 us
    pallas_call x3 -> x6, Pallas kernels: 6.02 us -> 10.5 us  [the longest x2 4.84 us: hold(): pl.pallas_call(hold_kernel, out_shape=jax.ShapeDtypeStruct(array.shape, a...]
    ppermute x1, waiting for transfers between devices: 0.01 us -> 1.72 us  [shards(): after = lax.ppermute(keys_values, 'section', down)]
    squeeze x0 -> x1, local copies, waits for them, and re-layouts: none -> 1.14 us  [shards(): order.append(lax.dynamic_index_in_dim(blocks, block, keepdims=False))]
  transfers between devices with their start and end apart: 12 -> 12, of which waited for: 5 -> 9; matrix products, arithmetic and copies ran while one was open for 2% -> 3% of each run, Pallas kernels for 26% -> 19%
where the time goes in v3:
time: 62.6 us; the launch traced here: 62.4 us
  waiting for transfers between devices  18.3 us (29%)
  starting transfers between devices  16.9 us (27%)
  Pallas kernels  14.2 us (23%)
  local copies, waits for them, and re-layouts  9.8 us (16%)
  between operations  2.22 us (4%)
  other arithmetic  0.93 us (1%)
    ppermute x10, waiting for transfers between devices, rotate(): lax.ppermute(value, axis, [(i, (i + steps) % count) for i in range(count)])  11.5 us
    ppermute x10, starting transfers between devices, rotate(): lax.ppermute(value, axis, [(i, (i + steps) % count) for i in range(count)])  11.1 us
    unnamed x18, local copies, waits for them, and re-layouts  8.01 us
    ppermute x1, waiting for transfers between devices, shards(): before = lax.ppermute(keys_values, 'section', up)  5.01 us
    pallas_call x2, Pallas kernels, hold(): pl.pallas_call(hold_kernel, out_shape=jax.ShapeDtypeStruct(array.shape, a...  4.84 us
    pallas_call x3, Pallas kernels, attend_halo(): pl.pallas_call(functools.partial(halo_kernel, first, last), out_shape=out...  4.76 us
    ppermute x1, starting transfers between devices, shards(): before = lax.ppermute(keys_values, 'section', up)  4.53 us
    pallas_call x4, Pallas kernels, project(): pl.pallas_call(functools.partial(project_kernel, parts, rows, first), out...  3.45 us
  transfers between devices with their start and end apart: 12, of which 9 were waited for; matrix products, arithmetic and copies ran while one was open for 3% of the time, Pallas kernels for 19%

profile of v3, /device:TPU:0, one launch (start us, length us, event | category | flops | bytes accessed | tf_op | source)
XLA Modules:
  0.0 62.4 jit_solution(6320874207139700127)
XLA Ops:
  0.5 4.5 %collective-permute-start.1 = (bf16[2,1,256,1024]{3,2,1,0:T(8,128)(2,1)}, bf16[2,1,256,1024]{3,2,1,0:T(8,128)(2,1)S(1)}, u32[]{:S(2)}, u32[]{:S(2)}) collective-permute-start(bf16[2,1,256,1024]{3,2,1,0:T(8,128)(2,1)} %own_ref.1), channel_id=1, source_target_pairs={{0,4},{4,8},{8,12},{1,5},{5,9},{9,13},{2,6},{6,10},{10,14},{3,7},{... | collective-permute-start | bytes 3145736 | tf_op jit(solution)/shard_map/ppermute | solution.py:208
  5.0 1.3 %collective-permute-start = (bf16[2,1,256,1024]{3,2,1,0:T(8,128)(2,1)}, bf16[2,1,256,1024]{3,2,1,0:T(8,128)(2,1)S(1)}, u32[]{:S(2)}, u32[]{:S(2)}) collective-permute-start(bf16[2,1,256,1024]{3,2,1,0:T(8,128)(2,1)} %own_ref.1), channel_id=1, source_target_pairs={{4,0},{8,4},{12,8},{5,1},{9,5},{13,9},{6,2},{10,6},{14,10},{7,3},{... | collective-permute-start | bytes 3145736 | tf_op jit(solution)/shard_map/ppermute | solution.py:209
  6.4 4.0 %copy-done.1 = bf16[1024,5120]{1,0:T(8,128)(2,1)S(1)} copy-done((bf16[1024,5120]{1,0:T(8,128)(2,1)S(1)}, bf16[1024,5120]{1,0:T(8,128)(2,1)}, u32[]{:S(2)}) %copy-start.1) | copy-done | bytes 10485784
  10.3 0.7 %hold.2.refs_2_ = bf16[1024,5120]{1,0:T(8,128)(2,1)S(1)} custom-call(bf16[1024,5120]{1,0:T(8,128)(2,1)S(1)} %copy-done.1), custom_call_target="tpu_custom_call" | custom-call | bytes 20971520 | tf_op jit(solution)/shard_map/hold/pallas_call | solution.py:119
  11.0 4.0 %copy-done = bf16[1024,5120]{1,0:T(8,128)(2,1)} copy-done((bf16[1024,5120]{1,0:T(8,128)(2,1)}, bf16[1024,5120]{1,0:T(8,128)(2,1)S(1)}, u32[]{:S(2)}) %copy-start) | copy-done | bytes 10485784
  15.1 0.7 %fusion = (s32[1]{0:T(128)}, s32[1]{0:T(128)}) fusion(s32[3]{0:T(128)S(1)} %copy-done.5, s32[]{:T(128)S(6)} %min.8, s32[]{:T(128)S(6)} %min.7), kind=kLoop, calls=%fused_computation.8 | loop fusion | bytes 24 | tf_op jit(solution)/shard_map/dynamic_slice | solution.py:202
  17.0 1.1 %dynamic-slice_bitcast_fusion.3 = (bf16[64,1024]{1,0:T(8,128)(2,1)S(1)}, bf16[64,1024]{1,0:T(8,128)(2,1)S(1)}, bf16[64,1024]{1,0:T(8,128)(2,1)S(1)}, bf16[64,1024]{1,0:T(8,128)(2,1)S(1)}) fusion(bf16[4,64,1024]{2,1,0:T(8,128)(2,1)} %bitcast.20, s32[]{:T(128)S(6)} %select_n.58, s32[]{:T(128)S(6)} %select_n.63, s32[]{:T(128)S(6)} %select_n.62, s32[]{:T(128)S(6)} %select_n.60), kind=kLoop, calls=%fused_computation.5 | loop fusion | bytes 1048592 | tf_op jit(solution)/shard_map/jit(dynamic_index_in_dim)/squeeze | solution.py:220
  18.2 0.9 %attend_own.1 = (f32[256,1024]{1,0:T(8,128)S(1)}, f32[256,1024]{1,0:T(8,128)S(1)}, f32[256,1024]{1,0:T(8,128)S(1)}) custom-call(bf16[256,1024]{1,0:T(8,128)(2,1)S(1)} %pad_maximum_fusion.q_ref, bf16[2,1,256,1024]{3,2,1,0:T(8,128)(2,1)S(1)} %copy-done.4), custom_call_target="tpu_custom_call" | custom-call | flops 268435456 | bytes 4718592 | tf_op jit(solution)/shard_map/attend_own/pallas_call | solution.py:75
  19.2 4.1 %hold.3.refs_3_ = bf16[1024,5120]{1,0:T(8,128)(2,1)S(1)} custom-call(bf16[1024,5120]{1,0:T(8,128)(2,1)} %collective-permute-done.2.src_ref), custom_call_target="tpu_custom_call" | custom-call | bytes 20971520 | tf_op jit(solution)/shard_map/hold/pallas_call | solution.py:119
  23.3 5.0 %collective-permute-done.1.halo_ref = bf16[2,1,256,1024]{3,2,1,0:T(8,128)(2,1)S(1)} collective-permute-done((bf16[2,1,256,1024]{3,2,1,0:T(8,128)(2,1)}, bf16[2,1,256,1024]{3,2,1,0:T(8,128)(2,1)S(1)}, u32[]{:S(2)}, u32[]{:S(2)}) %collective-permute-start.1) | collective-permute-done | bytes 1048608 | tf_op jit(solution)/shard_map/ppermute | solution.py:208
  28.3 2.4 %attend_halo.3 = (f32[256,1024]{1,0:T(8,128)S(1)}, f32[256,1024]{1,0:T(8,128)S(1)}, f32[256,1024]{1,0:T(8,128)S(1)}) custom-call(bf16[256,1024]{1,0:T(8,128)(2,1)S(1)} %pad_maximum_fusion.q_ref, bf16[2,1,256,1024]{3,2,1,0:T(8,128)(2,1)S(1)} %collective-permute-done.1.halo_ref, f32[1,256]{1,0:T(1,128)S(1)} %compare_select_fusion.mask_ref, ...), custom_call_target="tpu_custom_call" | custom-call | flops 268435456 | bytes 5242880 | tf_op jit(solution)/shard_map/attend_halo/pallas_call | solution.py:97
  30.7 1.7 %collective-permute-done.halo_ref = bf16[2,1,256,1024]{3,2,1,0:T(8,128)(2,1)S(1)} collective-permute-done((bf16[2,1,256,1024]{3,2,1,0:T(8,128)(2,1)}, bf16[2,1,256,1024]{3,2,1,0:T(8,128)(2,1)S(1)}, u32[]{:S(2)}, u32[]{:S(2)}) %collective-permute-start) | collective-permute-done | bytes 1048608 | tf_op jit(solution)/shard_map/ppermute | solution.py:209
  32.4 1.2 %attend_halo.5 = bf16[128,1024]{1,0:T(8,128)(2,1)S(1)} custom-call(bf16[256,1024]{1,0:T(8,128)(2,1)S(1)} %pad_maximum_fusion.q_ref, bf16[2,1,256,1024]{3,2,1,0:T(8,128)(2,1)S(1)} %collective-permute-done.halo_ref, f32[1,256]{1,0:T(1,128)S(1)} %compare_select_fusion.1.mask_ref, f32[256,1024]{1,0:T(8,128)S(1)} %get-tuple-element.30.acc_ref, ...), custom_call_target="tpu_custom_call" | custom-call | flops 134217728 | bytes 2621440 | tf_op jit(solution)/shard_map/attend_halo/pallas_call | solution.py:97
  33.7 1.2 %attend_halo.4.refs_0_ = bf16[128,1024]{1,0:T(8,128)(2,1)S(1)} custom-call(bf16[256,1024]{1,0:T(8,128)(2,1)S(1)} %pad_maximum_fusion.q_ref, bf16[2,1,256,1024]{3,2,1,0:T(8,128)(2,1)S(1)} %collective-permute-done.halo_ref, f32[1,256]{1,0:T(1,128)S(1)} %compare_select_fusion.1.mask_ref, f32[256,1024]{1,0:T(8,128)S(1)} %get-tuple-element.30.acc_ref, ...), custom_call_target="tpu_custom_call" | custom-call | flops 134217728 | bytes 2621440 | tf_op jit(solution)/shard_map/attend_halo/pallas_call | solution.py:97
  35.2 0.9 %project.4 = (bf16[64,1280]{1,0:T(8,128)(2,1)S(1)}, f32[64,1280]{1,0:T(8,128)S(1)}) custom-call(bf16[128,1024]{1,0:T(8,128)(2,1)S(1)} %attend_halo.4.refs_0_, bf16[128,1024]{1,0:T(8,128)(2,1)S(1)} %collective-permute-done.3.refs_1_, bf16[1024,5120]{1,0:T(8,128)(2,1)S(1)} %bitcast.15, bf16[1024,5120]{1,0:T(8,128)(2,1)S(1)} %hold.3.refs_3_), custom_call_target="tpu_custom_call" | custom-call | flops 671088640 | bytes 5242880 | tf_op jit(solution)/shard_map/project/pallas_call | solution.py:152
  36.1 1.6 %collective-permute-start.4 = (bf16[64,1280]{1,0:T(8,128)(2,1)S(1)}, bf16[64,1280]{1,0:T(8,128)(2,1)S(1)}, u32[]{:S(2)}, u32[]{:S(2)}) collective-permute-start(bf16[64,1280]{1,0:T(8,128)(2,1)S(1)} %get-tuple-element.36), channel_id=1, source_target_pairs={{0,2},{2,0},{1,3},{3,1},{4,6},{6,4},{5,7},{7,5},{8,10},{10,8},{9,1... | collective-permute-start | bytes 491528 | tf_op jit(solution)/shard_map/ppermute | solution.py:194
  37.6 0.9 %project.5 = (bf16[64,1280]{1,0:T(8,128)(2,1)S(1)}, f32[64,1280]{1,0:T(8,128)S(1)}) custom-call(bf16[128,1024]{1,0:T(8,128)(2,1)S(1)} %attend_halo.4.refs_0_, bf16[128,1024]{1,0:T(8,128)(2,1)S(1)} %collective-permute-done.3.refs_1_, bf16[1024,5120]{1,0:T(8,128)(2,1)S(1)} %bitcast.15, bf16[1024,5120]{1,0:T(8,128)(2,1)S(1)} %hold.3.refs_3_), custom_call_target="tpu_custom_call" | custom-call | flops 671088640 | bytes 5242880 | tf_op jit(solution)/shard_map/project/pallas_call | solution.py:152
  39.1 0.9 %project.6 = (bf16[64,1280]{1,0:T(8,128)(2,1)S(1)}, f32[64,1280]{1,0:T(8,128)S(1)}) custom-call(bf16[128,1024]{1,0:T(8,128)(2,1)S(1)} %attend_halo.4.refs_0_, bf16[128,1024]{1,0:T(8,128)(2,1)S(1)} %collective-permute-done.3.refs_1_, bf16[1024,5120]{1,0:T(8,128)(2,1)S(1)} %bitcast.15, bf16[1024,5120]{1,0:T(8,128)(2,1)S(1)} %hold.3.refs_3_), custom_call_target="tpu_custom_call" | custom-call | flops 671088640 | bytes 5242880 | tf_op jit(solution)/shard_map/project/pallas_call | solution.py:152
  40.0 1.5 %collective-permute-start.8 = (bf16[64,1280]{1,0:T(8,128)(2,1)S(1)}, bf16[64,1280]{1,0:T(8,128)(2,1)S(1)}, u32[]{:S(2)}, u32[]{:S(2)}) collective-permute-start(bf16[64,1280]{1,0:T(8,128)(2,1)S(1)} %get-tuple-element.40), channel_id=1, source_target_pairs={{0,2},{2,0},{1,3},{3,1},{4,6},{6,4},{5,7},{7,5},{8,10},{10,8},{9,1... | collective-permute-start | bytes 491528 | tf_op jit(solution)/shard_map/ppermute | solution.py:194
  41.5 0.9 %project.7 = (bf16[64,1280]{1,0:T(8,128)(2,1)S(1)}, f32[64,1280]{1,0:T(8,128)S(1)}) custom-call(bf16[128,1024]{1,0:T(8,128)(2,1)S(1)} %attend_halo.4.refs_0_, bf16[128,1024]{1,0:T(8,128)(2,1)S(1)} %collective-permute-done.3.refs_1_, bf16[1024,5120]{1,0:T(8,128)(2,1)S(1)} %bitcast.15, bf16[1024,5120]{1,0:T(8,128)(2,1)S(1)} %hold.3.refs_3_), custom_call_target="tpu_custom_call" | custom-call | flops 671088640 | bytes 5242880 | tf_op jit(solution)/shard_map/project/pallas_call | solution.py:152
  42.4 0.6 collective-permute-start.10
  43.8 1.6 %collective-permute-start.5 = (bf16[64,1280]{1,0:T(8,128)(2,1)S(1)}, bf16[64,1280]{1,0:T(8,128)(2,1)S(1)}, u32[]{:S(2)}, u32[]{:S(2)}) collective-permute-start(bf16[64,1280]{1,0:T(8,128)(2,1)S(1)} %combine.4), channel_id=1, source_target_pairs={{0,4},{4,8},{8,12},{12,0},{1,5},{5,9},{9,13},{13,1},{2,6},{6,10},{... | collective-permute-start | bytes 491528 | tf_op jit(solution)/shard_map/ppermute | solution.py:194
  45.3 1.3 %collective-permute-done.6.refs_0_ = bf16[64,1280]{1,0:T(8,128)(2,1)S(1)} collective-permute-done((bf16[64,1280]{1,0:T(8,128)(2,1)S(1)}, bf16[64,1280]{1,0:T(8,128)(2,1)S(1)}, u32[]{:S(2)}, u32[]{:S(2)}) %collective-permute-start.6) | collective-permute-done | bytes 163872 | tf_op jit(solution)/shard_map/ppermute | solution.py:194
  46.8 1.6 %collective-permute-start.7 = (bf16[64,1280]{1,0:T(8,128)(2,1)S(1)}, bf16[64,1280]{1,0:T(8,128)(2,1)S(1)}, u32[]{:S(2)}, u32[]{:S(2)}) collective-permute-start(bf16[64,1280]{1,0:T(8,128)(2,1)S(1)} %combine.5), channel_id=1, source_target_pairs={{0,4},{4,8},{8,12},{12,0},{1,5},{5,9},{9,13},{13,1},{2,6},{6,10},{... | collective-permute-start | bytes 491528 | tf_op jit(solution)/shard_map/ppermute | solution.py:194
  48.3 1.9 %collective-permute-done.8.refs_0_ = bf16[64,1280]{1,0:T(8,128)(2,1)S(1)} collective-permute-done((bf16[64,1280]{1,0:T(8,128)(2,1)S(1)}, bf16[64,1280]{1,0:T(8,128)(2,1)S(1)}, u32[]{:S(2)}, u32[]{:S(2)}) %collective-permute-start.8) | collective-permute-done | bytes 163872 | tf_op jit(solution)/shard_map/ppermute | solution.py:194
  50.3 1.6 %collective-permute-start.9 = (bf16[64,1280]{1,0:T(8,128)(2,1)S(1)}, bf16[64,1280]{1,0:T(8,128)(2,1)S(1)}, u32[]{:S(2)}, u32[]{:S(2)}) collective-permute-start(bf16[64,1280]{1,0:T(8,128)(2,1)S(1)} %combine.6), channel_id=1, source_target_pairs={{0,4},{4,8},{8,12},{12,0},{1,5},{5,9},{9,13},{13,1},{2,6},{6,10},{... | collective-permute-start | bytes 491528 | tf_op jit(solution)/shard_map/ppermute | solution.py:194
  51.8 1.1 %collective-permute-done.10.refs_0_ = bf16[64,1280]{1,0:T(8,128)(2,1)S(1)} collective-permute-done((bf16[64,1280]{1,0:T(8,128)(2,1)S(1)}, bf16[64,1280]{1,0:T(8,128)(2,1)S(1)}, u32[]{:S(2)}, u32[]{:S(2)}) %collective-permute-start.10) | collective-permute-done | bytes 163872 | tf_op jit(solution)/shard_map/ppermute | solution.py:194
  53.0 1.6 %collective-permute-start.11 = (bf16[64,1280]{1,0:T(8,128)(2,1)S(1)}, bf16[64,1280]{1,0:T(8,128)(2,1)S(1)}, u32[]{:S(2)}, u32[]{:S(2)}) collective-permute-start(bf16[64,1280]{1,0:T(8,128)(2,1)S(1)} %combine.7), channel_id=1, source_target_pairs={{0,4},{4,8},{8,12},{12,0},{1,5},{5,9},{9,13},{13,1},{2,6},{6,10},{... | collective-permute-start | bytes 491528 | tf_op jit(solution)/shard_map/ppermute | solution.py:194
  54.6 0.9 %collective-permute-done.7 = bf16[64,1280]{1,0:T(8,128)(2,1)S(1)} collective-permute-done((bf16[64,1280]{1,0:T(8,128)(2,1)S(1)}, bf16[64,1280]{1,0:T(8,128)(2,1)S(1)}, u32[]{:S(2)}, u32[]{:S(2)}) %collective-permute-start.7) | collective-permute-done | bytes 163872 | tf_op jit(solution)/shard_map/ppermute | solution.py:194
  55.5 3.5 %collective-permute-done.9 = bf16[64,1280]{1,0:T(8,128)(2,1)S(1)} collective-permute-done((bf16[64,1280]{1,0:T(8,128)(2,1)S(1)}, bf16[64,1280]{1,0:T(8,128)(2,1)S(1)}, u32[]{:S(2)}, u32[]{:S(2)}) %collective-permute-start.9) | collective-permute-done | bytes 163872 | tf_op jit(solution)/shard_map/ppermute | solution.py:194
  59.1 2.4 %collective-permute-done.11 = bf16[64,1280]{1,0:T(8,128)(2,1)S(1)} collective-permute-done((bf16[64,1280]{1,0:T(8,128)(2,1)S(1)}, bf16[64,1280]{1,0:T(8,128)(2,1)S(1)}, u32[]{:S(2)}, u32[]{:S(2)}) %collective-permute-start.11) | collective-permute-done | bytes 163872 | tf_op jit(solution)/shard_map/ppermute | solution.py:194
  61.5 0.9 %maximum_bitcast_fusion = bf16[1,64,5120]{2,1,0:T(8,128)(2,1)} fusion(bf16[64,1280]{1,0:T(8,128)(2,1)S(1)} %collective-permute-done.11, bf16[64,1280]{1,0:T(8,128)(2,1)S(1)} %collective-permute-done.9, bf16[64,1280]{1,0:T(8,128)(2,1)S(1)} %collective-permute-done.7, bf16[64,1280]{1,0:T(8,128)(2,1)S(1)} %collective-permute-done.5), kind=kLoop, calls=%fused_computation | loop fusion | flops 2621440 | bytes 1310720 | tf_op jit(solution)/shard_map/broadcast_in_dim | solution.py:243
  (31 shorter events, 1.8 us)
Async XLA Ops:
  0.0 19.1 %collective-permute-start.2 = (bf16[1024,5120]{1,0:T(8,128)(2,1)}, bf16[1024,5120]{1,0:T(8,128)(2,1)}, u32[]{:S(2)}, u32[]{:S(2)}) collective-permute-start(bf16[1024,5120]{1,0:T(8,128)(2,1)} %src_ref.1), channel_id=1, source_target_pairs={{0,1},{1,0},{2,3},{3,2},{4,5},{5,4},{6,7},{7,6},{8,9},{9,8},{10,11... | collective-permute-start | bytes 31457288 | tf_op jit(solution)/shard_map/ppermute | solution.py:194
  0.5 27.9 %collective-permute-start.1 = (bf16[2,1,256,1024]{3,2,1,0:T(8,128)(2,1)}, bf16[2,1,256,1024]{3,2,1,0:T(8,128)(2,1)S(1)}, u32[]{:S(2)}, u32[]{:S(2)}) collective-permute-start(bf16[2,1,256,1024]{3,2,1,0:T(8,128)(2,1)} %own_ref.1), channel_id=1, source_target_pairs={{0,4},{4,8},{8,12},{1,5},{5,9},{9,13},{2,6},{6,10},{10,14},{3,7},{... | collective-permute-start | bytes 3145736 | tf_op jit(solution)/shard_map/ppermute | solution.py:208
  5.0 27.4 %collective-permute-start = (bf16[2,1,256,1024]{3,2,1,0:T(8,128)(2,1)}, bf16[2,1,256,1024]{3,2,1,0:T(8,128)(2,1)S(1)}, u32[]{:S(2)}, u32[]{:S(2)}) collective-permute-start(bf16[2,1,256,1024]{3,2,1,0:T(8,128)(2,1)} %own_ref.1), channel_id=1, source_target_pairs={{4,0},{8,4},{12,8},{5,1},{9,5},{13,9},{6,2},{10,6},{14,10},{7,3},{... | collective-permute-start | bytes 3145736 | tf_op jit(solution)/shard_map/ppermute | solution.py:209
  6.3 4.0 %copy-start.1 = (bf16[1024,5120]{1,0:T(8,128)(2,1)S(1)}, bf16[1024,5120]{1,0:T(8,128)(2,1)}, u32[]{:S(2)}) copy-start(bf16[1024,5120]{1,0:T(8,128)(2,1)} %src_ref.1) | copy-start | bytes 31457284
  10.3 4.7 %copy-start.5 = (s32[3]{0:T(128)S(1)}, s32[3]{0:T(128)}, u32[]{:S(2)}) copy-start(s32[3]{0:T(128)} %param.13) | copy-start | bytes 40
  11.0 4.0 %copy-start = (bf16[1024,5120]{1,0:T(8,128)(2,1)}, bf16[1024,5120]{1,0:T(8,128)(2,1)S(1)}, u32[]{:S(2)}) copy-start(bf16[1024,5120]{1,0:T(8,128)(2,1)S(1)} %hold.2.refs_2_) | copy-start | bytes 31457284
  15.1 3.1 %copy-start.4 = (bf16[2,1,256,1024]{3,2,1,0:T(8,128)(2,1)S(1)}, bf16[2,1,256,1024]{3,2,1,0:T(8,128)(2,1)}, u32[]{:S(2)}) copy-start(bf16[2,1,256,1024]{3,2,1,0:T(8,128)(2,1)} %own_ref.1) | copy-start | bytes 3145732
  19.1 16.0 %slice-start = ((s8[10485760]{0:T(1024)(128)(4,1)}), s8[4194304]{0:T(1024)(128)(4,1)S(1)}, s32[]{:S(2)}) async-start(s8[10485760]{0:T(1024)(128)(4,1)} %bitcast.14), calls=%async_computation | async-start | bytes 8388608
  19.1 16.0 %slice-start.1 = ((s8[10485760]{0:T(1024)(128)(4,1)}), s8[4194304]{0:T(1024)(128)(4,1)S(1)}, s32[]{:S(2)}) async-start(s8[10485760]{0:T(1024)(128)(4,1)} %bitcast.14), calls=%async_computation.1 | async-start | bytes 8388608
  23.3 11.9 %slice-start.2 = ((s8[10485760]{0:T(1024)(128)(4,1)}), s8[2097152]{0:T(1024)(128)(4,1)S(1)}, s32[]{:S(2)}) async-start(s8[10485760]{0:T(1024)(128)(4,1)} %bitcast.14), calls=%async_computation.2 | async-start | bytes 4194304
  33.6 1.6 %collective-permute-start.3 = (bf16[128,1024]{1,0:T(8,128)(2,1)S(1)}, bf16[128,1024]{1,0:T(8,128)(2,1)S(1)}, u32[]{:S(2)}, u32[]{:S(2)}) collective-permute-start(bf16[128,1024]{1,0:T(8,128)(2,1)S(1)} %attend_halo.5), channel_id=1, source_target_pairs={{0,1},{1,0},{2,3},{3,2},{4,5},{5,4},{6,7},{7,6},{8,9},{9,8},{10,11... | collective-permute-start | bytes 786440 | tf_op jit(solution)/shard_map/ppermute | solution.py:194
  36.1 7.6 %collective-permute-start.4 = (bf16[64,1280]{1,0:T(8,128)(2,1)S(1)}, bf16[64,1280]{1,0:T(8,128)(2,1)S(1)}, u32[]{:S(2)}, u32[]{:S(2)}) collective-permute-start(bf16[64,1280]{1,0:T(8,128)(2,1)S(1)} %get-tuple-element.36), channel_id=1, source_target_pairs={{0,2},{2,0},{1,3},{3,1},{4,6},{6,4},{5,7},{7,5},{8,10},{10,8},{9,1... | collective-permute-start | bytes 491528 | tf_op jit(solution)/shard_map/ppermute | solution.py:194
  38.5 8.2 %collective-permute-start.6 = (bf16[64,1280]{1,0:T(8,128)(2,1)S(1)}, bf16[64,1280]{1,0:T(8,128)(2,1)S(1)}, u32[]{:S(2)}, u32[]{:S(2)}) collective-permute-start(bf16[64,1280]{1,0:T(8,128)(2,1)S(1)} %get-tuple-element.38), channel_id=1, source_target_pairs={{0,2},{2,0},{1,3},{3,1},{4,6},{6,4},{5,7},{7,5},{8,10},{10,8},{9,1... | collective-permute-start | bytes 491528 | tf_op jit(solution)/shard_map/ppermute | solution.py:194
  40.0 3.7 %copy-start.2 = (bf16[1,64,5120]{2,1,0:T(8,128)(2,1)S(1)}, bf16[1,64,5120]{2,1,0:T(8,128)(2,1)}, u32[]{:S(2)}) copy-start(bf16[1,64,5120]{2,1,0:T(8,128)(2,1)} %param.9) | copy-start | bytes 1966084
  40.0 3.7 %copy-start.3 = (f32[8,5120]{1,0:T(8,128)S(1)}, f32[8,5120]{1,0:T(8,128)}, u32[]{:S(2)}) copy-start(f32[8,5120]{1,0:T(8,128)} %gate_ref.7) | copy-start | bytes 491524
  40.0 10.2 %collective-permute-start.8 = (bf16[64,1280]{1,0:T(8,128)(2,1)S(1)}, bf16[64,1280]{1,0:T(8,128)(2,1)S(1)}, u32[]{:S(2)}, u32[]{:S(2)}) collective-permute-start(bf16[64,1280]{1,0:T(8,128)(2,1)S(1)} %get-tuple-element.40), channel_id=1, source_target_pairs={{0,2},{2,0},{1,3},{3,1},{4,6},{6,4},{5,7},{7,5},{8,10},{10,8},{9,1... | collective-permute-start | bytes 491528 | tf_op jit(solution)/shard_map/ppermute | solution.py:194
  42.4 10.6 %collective-permute-start.10 = (bf16[64,1280]{1,0:T(8,128)(2,1)S(1)}, bf16[64,1280]{1,0:T(8,128)(2,1)S(1)}, u32[]{:S(2)}, u32[]{:S(2)}) collective-permute-start(bf16[64,1280]{1,0:T(8,128)(2,1)S(1)} %get-tuple-element.42), channel_id=1, source_target_pairs={{0,2},{2,0},{1,3},{3,1},{4,6},{6,4},{5,7},{7,5},{8,10},{10,8},{9,1... | collective-permute-start | bytes 491528 | tf_op jit(solution)/shard_map/ppermute | solution.py:194
  43.8 10.8 %collective-permute-start.5 = (bf16[64,1280]{1,0:T(8,128)(2,1)S(1)}, bf16[64,1280]{1,0:T(8,128)(2,1)S(1)}, u32[]{:S(2)}, u32[]{:S(2)}) collective-permute-start(bf16[64,1280]{1,0:T(8,128)(2,1)S(1)} %combine.4), channel_id=1, source_target_pairs={{0,4},{4,8},{8,12},{12,0},{1,5},{5,9},{9,13},{13,1},{2,6},{6,10},{... | collective-permute-start | bytes 491528 | tf_op jit(solution)/shard_map/ppermute | solution.py:194
  46.8 8.8 %collective-permute-start.7 = (bf16[64,1280]{1,0:T(8,128)(2,1)S(1)}, bf16[64,1280]{1,0:T(8,128)(2,1)S(1)}, u32[]{:S(2)}, u32[]{:S(2)}) collective-permute-start(bf16[64,1280]{1,0:T(8,128)(2,1)S(1)} %combine.5), channel_id=1, source_target_pairs={{0,4},{4,8},{8,12},{12,0},{1,5},{5,9},{9,13},{13,1},{2,6},{6,10},{... | collective-permute-start | bytes 491528 | tf_op jit(solution)/shard_map/ppermute | solution.py:194
  50.3 8.8 %collective-permute-start.9 = (bf16[64,1280]{1,0:T(8,128)(2,1)S(1)}, bf16[64,1280]{1,0:T(8,128)(2,1)S(1)}, u32[]{:S(2)}, u32[]{:S(2)}) collective-permute-start(bf16[64,1280]{1,0:T(8,128)(2,1)S(1)} %combine.6), channel_id=1, source_target_pairs={{0,4},{4,8},{8,12},{12,0},{1,5},{5,9},{9,13},{13,1},{2,6},{6,10},{... | collective-permute-start | bytes 491528 | tf_op jit(solution)/shard_map/ppermute | solution.py:194
  53.0 8.4 %collective-permute-start.11 = (bf16[64,1280]{1,0:T(8,128)(2,1)S(1)}, bf16[64,1280]{1,0:T(8,128)(2,1)S(1)}, u32[]{:S(2)}, u32[]{:S(2)}) collective-permute-start(bf16[64,1280]{1,0:T(8,128)(2,1)S(1)} %combine.7), channel_id=1, source_target_pairs={{0,4},{4,8},{8,12},{12,0},{1,5},{5,9},{9,13},{13,1},{2,6},{6,10},{... | collective-permute-start | bytes 491528 | tf_op jit(solution)/shard_map/ppermute | solution.py:194

commit v4 on v3

v4 whole, which is shorter than its diff:
```python
import functools
import math

import jax
import jax.numpy as jnp
from jax import lax
from jax.experimental import pallas as pl
from jax.experimental.pallas import tpu as pltpu
from jax.sharding import PartitionSpec as P

HD = 128
CHUNKS = 4
NEG_BIG = -1e30
VMEM_LIMIT = 4 * 1024 * 1024


def scores_of(q, keys):
    return lax.dot_general(
        q, keys, (((1,), (1,)), ((), ())), preferred_element_type=jnp.float32
    )


FACTOR = math.log2(math.e) / math.sqrt(HD)


def exponentials(scores, top):
    wide = jnp.concatenate([top] * (scores.shape[1] // HD), axis=1)
    return jnp.exp2((scores - wide) * FACTOR).astype(jnp.bfloat16)


def own_kernel(q_ref, own_ref, acc_ref, den_ref, top_ref):
    rows, width = q_ref.shape
    ones = jnp.ones((own_ref.shape[2], HD), jnp.bfloat16)
    for h in range(width // HD):
        head = slice(h * HD, (h + 1) * HD)
        scores = scores_of(q_ref[:, head], own_ref[0, 0, :, head])
        top = jnp.broadcast_to(jnp.max(scores, axis=1, keepdims=True), (rows, HD))
        values = jnp.concatenate([own_ref[1, 0, :, head], ones], axis=1)
        both = jnp.dot(
            exponentials(scores, top), values, preferred_element_type=jnp.float32
        )
        acc_ref[:, head] = both[:, :HD]
        den_ref[:, head] = both[:, HD:]
        top_ref[:, head] = top


def halo_kernel(
    first, last, q_ref, halo_ref, mask_ref, acc_ref, den_ref, top_ref, *outs
):
    rows, width = outs[0].shape
    part = slice(first, first + rows)
    mask = mask_ref[...]
    ones = jnp.ones((halo_ref.shape[2], HD), jnp.bfloat16)
    heads = [slice(h * HD, (h + 1) * HD) for h in range(width // HD)]
    scores = [scores_of(q_ref[part, head], halo_ref[0, 0, :, head]) + mask for head in heads]
    peaks = [jnp.max(s, axis=1, keepdims=True) for s in scores]
    probs, fades = [], []
    for head, s, peak in zip(heads, scores, peaks):
        before = top_ref[part, head]
        top = jnp.maximum(before, jnp.broadcast_to(peak, before.shape))
        probs.append(exponentials(s, top))
        fades.append(jnp.exp2((before - top) * FACTOR))
        if not last:
            outs[2][:, head] = top
    for head, p, fade in zip(heads, probs, fades):
        values = jnp.concatenate([halo_ref[1, 0, :, head], ones], axis=1)
        both = jnp.dot(p, values, preferred_element_type=jnp.float32)
        weighted = acc_ref[part, head] * fade + both[:, :HD]
        total = den_ref[part, head] * fade + both[:, HD:]
        if last:
            outs[0][:, head] = (weighted / total).astype(outs[0].dtype)
        else:
            outs[0][:, head] = weighted
            outs[1][:, head] = total


VMEM_SPEC = pl.BlockSpec(memory_space=pltpu.VMEM)


def attend(kernel, name, out_shape, flops, *operands):
    return pl.pallas_call(
        kernel,
        out_shape=out_shape,
        in_specs=[VMEM_SPEC] * len(operands),
        out_specs=(VMEM_SPEC,) * len(out_shape),
        compiler_params=pltpu.CompilerParams(vmem_limit_bytes=VMEM_LIMIT),
        cost_estimate=pl.CostEstimate(
            flops=flops,
            bytes_accessed=sum(x.size * x.dtype.itemsize for x in operands),
            transcendentals=flops // (4 * HD),
        ),
        name=name,
    )(*operands)


def hold_kernel(src_ref, dst_ref, sem):
    copy = pltpu.make_async_copy(src_ref, dst_ref, sem)
    copy.start()
    copy.wait()


def hold(array):
    return pl.pallas_call(
        hold_kernel,
        out_shape=jax.ShapeDtypeStruct(array.shape, array.dtype),
        in_specs=[pl.BlockSpec(memory_space=pltpu.HBM)],
        out_specs=VMEM_SPEC,
        scratch_shapes=[pltpu.SemaphoreType.DMA],
        compiler_params=pltpu.CompilerParams(vmem_limit_bytes=VMEM_LIMIT),
        cost_estimate=pl.CostEstimate(flops=0, bytes_accessed=1024, transcendentals=0),
        name="hold",
    )(array)


def project_kernel(parts, rows, first, base, *refs):
    att, weights = refs[:parts], refs[parts : 2 * parts]
    outs = refs[2 * parts + (1 if base else 0) :]
    columns = outs[-1].shape[1]
    tile = math.gcd(columns, 256)
    for t in range(0, columns, tile):
        total = refs[2 * parts][:, t : t + tile] if base else None
        for a, w in zip(att, weights):
            term = jnp.dot(
                a[...], w[:, first + t : first + t + tile], preferred_element_type=jnp.float32
            )
            total = term if total is None else total + term
        if len(outs) == 1:
            outs[0][:, t : t + tile] = total
            continue
        for i, out in enumerate(outs):
            out[:, t : t + tile] = total[i * rows : (i + 1) * rows].astype(out.dtype)


def project(att, weights, base, rows, first, columns, split):
    parts = len(att)
    all_rows, depth = att[0].shape
    send = jax.ShapeDtypeStruct((rows, columns), jnp.bfloat16)
    keep = jax.ShapeDtypeStruct((rows, columns), jnp.float32)
    blocks = all_rows // rows
    whole = jax.ShapeDtypeStruct((all_rows, columns), jnp.float32)
    out_shape = (send,) * (blocks - 1) + (keep,) if split else (whole,)
    bases = [] if base is None else [base]
    return pl.pallas_call(
        functools.partial(project_kernel, parts, rows, first, len(bases)),
        out_shape=out_shape,
        in_specs=[VMEM_SPEC] * (2 * parts + len(bases)),
        out_specs=(VMEM_SPEC,) * len(out_shape),
        compiler_params=pltpu.CompilerParams(vmem_limit_bytes=VMEM_LIMIT),
        cost_estimate=pl.CostEstimate(
            flops=2 * parts * all_rows * depth * columns,
            bytes_accessed=2 * parts * depth * columns,
            transcendentals=0,
        ),
        name="project",
    )(*att, *weights, *bases)


def combine_kernel(first, latents_ref, gate_ref, keep_ref, *refs):
    others, out_ref = refs[:-1], refs[-1]
    part = slice(first, first + keep_ref.shape[1])
    total = keep_ref[...]
    for other in others:
        total += other[...].astype(jnp.float32)
    out_ref[...] = (
        latents_ref[:, part].astype(jnp.float32) + gate_ref[:, part] * total
    ).astype(out_ref.dtype)


def combine(latents, gate_row, keep, others, first):
    rows, columns = keep.shape
    return pl.pallas_call(
        functools.partial(combine_kernel, first),
        out_shape=jax.ShapeDtypeStruct((rows, columns), latents.dtype),
        in_specs=[VMEM_SPEC] * (3 + len(others)),
        out_specs=VMEM_SPEC,
        compiler_params=pltpu.CompilerParams(vmem_limit_bytes=VMEM_LIMIT),
        cost_estimate=pl.CostEstimate(
            flops=4 * rows * columns, bytes_accessed=12 * rows * columns, transcendentals=0
        ),
        name="combine",
    )(latents, gate_row, keep, *others)


def rotate(value, axis, steps):
    count = lax.axis_size(axis)
    return lax.ppermute(value, axis, [(i, (i + steps) % count) for i in range(count)])


def shards(queries, keys_values, latents, out_weight, gate_table, level_index, pair_window):
    sections, spans, cores = (lax.axis_size(a) for a in ("section", "span", "mp"))
    section_id = lax.axis_index("section")
    rows = latents.shape[1]
    final_pair = pair_window.shape[0] - 1
    prev_width = jnp.where(section_id > 0, pair_window[jnp.clip(section_id - 1, 0, final_pair)], 0)
    next_width = jnp.where(
        section_id < sections - 1, pair_window[jnp.clip(section_id, 0, final_pair)], 0
    )
    up = [(i, i + 1) for i in range(sections - 1)]
    down = [(j, i) for i, j in up]
    before = lax.ppermute(keys_values, "section", up)
    after = lax.ppermute(keys_values, "section", down)
    weights = [hold(out_weight)]
    weights += [hold(rotate(out_weight, "mp", l)) for l in range(1, cores)]
    own_latents = latents[0]
    span_tok = queries.shape[1]
    span_id, core_id = lax.axis_index("span"), lax.axis_index("mp")
    blocks = queries[0].reshape(spans * cores, rows, -1)
    order = []
    for l in range(cores - 1, -1, -1):
        for k in range(spans - 1, -1, -1):
            block = (span_id + k) % spans * cores + (core_id + l) % cores
            order.append(lax.dynamic_index_in_dim(blocks, block, keepdims=False))
    own_queries = jnp.concatenate(order, axis=0)
    col = jnp.arange(span_tok, dtype=jnp.int32)[None]
    prev_mask = jnp.where(col >= span_tok - prev_width, 0.0, NEG_BIG).astype(jnp.float32)
    next_mask = jnp.where(col < next_width, 0.0, NEG_BIG).astype(jnp.float32)

    gate_row = lax.dynamic_slice_in_dim(gate_table, level_index[0], 1, axis=0)
    width = queries.shape[2]
    wide = jax.ShapeDtypeStruct((span_tok, width), jnp.float32)
    flops = 4 * span_tok * span_tok * width
    state = attend(own_kernel, "attend_own", (wide,) * 3, flops, own_queries, keys_values)
    state, weights, gate_row = lax.optimization_barrier((state, weights, gate_row))
    kernel = functools.partial(halo_kernel, 0, False)
    state = attend(
        kernel, "attend_after", (wide,) * 3, flops, own_queries, after, next_mask, *state
    )
    per_core = spans * rows
    out_shape = (jax.ShapeDtypeStruct((per_core, width), jnp.bfloat16),)
    att = []
    for l in range(cores - 1, -1, -1):
        kernel = functools.partial(halo_kernel, (cores - 1 - l) * per_core, True)
        (out,) = attend(
            kernel, "attend_before", out_shape, flops // cores,
            own_queries, before, prev_mask, *state,
        )
        att.insert(0, out if l == 0 else rotate(out, "mp", l))

    columns = latents.shape[2] // CHUNKS
    updates = []
    for c in range(CHUNKS):
        first = c * columns
        if c == 0:
            (base,) = project(att[:1], weights[:1], None, rows, first, columns, False)
            *send, keep = project(att[1:], weights[1:], base, rows, first, columns, True)
            att, keep = lax.optimization_barrier((att, keep))
        else:
            *send, keep = project(att, weights, None, rows, first, columns, True)
        others = [rotate(send[spans - 1 - k], "span", k) for k in range(1, spans)]
        updates.append(combine(own_latents, gate_row, keep, others, first))
    pieces = [rotate(update, "section", 1) for update in updates]
    early = jnp.pad(jnp.concatenate(pieces[:-1], axis=1), ((0, 0), (0, columns)))
    early, late = lax.optimization_barrier((early, pieces[-1]))
    return lax.dynamic_update_slice(early, late, (0, latents.shape[2] - columns))[None]


def solution(mesh):
    in_specs = (
        P(("group", "section"), None, ("span", "mp")),
        P(None, ("group", "section"), None, ("span", "mp")),
        P(("group", "section"), ("span", "mp"), None),
        P(("span", "mp"), None),
        P(),
        P(("group", "section")),
        P("group"),
    )
    out_specs = P(("group", "section"), ("span", "mp"), None)
    return jax.shard_map(shards, mesh=mesh, in_specs=in_specs, out_specs=out_specs, check_vma=False)
```

time: 62.6 us -> 59.7 us (0.954)
  waiting for transfers between devices: 18.3 us -> 12.3 us
  starting transfers between devices: 16.9 us -> 21.2 us
  Pallas kernels: 14.2 us -> 12.3 us
  local copies, waits for them, and re-layouts: 9.8 us -> 10.5 us
    ppermute x1, waiting for transfers between devices: 5.01 us -> 0.04 us  [shards(): before = lax.ppermute(keys_values, 'section', up)]
    ppermute x10, starting transfers between devices: 11.1 us -> 14.5 us  [rotate(): lax.ppermute(value, axis, [(i, (i + steps) % count) for i in range(count)])]
    ppermute x10, waiting for transfers between devices: 11.5 us -> 8.16 us  [rotate(): lax.ppermute(value, axis, [(i, (i + steps) % count) for i in range(count)])]
    ppermute x1, waiting for transfers between devices: 1.72 us -> 4.13 us  [shards(): after = lax.ppermute(keys_values, 'section', down)]
    pallas_call x8 -> x9, Pallas kernels: 9.1 us -> 7.18 us  [the longest x5 3.8 us: project(): pl.pallas_call(functools.partial(project_kernel, parts, rows, first, len(...]
    concatenate x0 -> x1, other arithmetic: none -> 0.89 us  [shards(): jnp.concatenate(pieces[:-1], axis=1)]
    broadcast_in_dim x1 -> x0, other arithmetic: 0.88 us -> none  [shards(): return jnp.concatenate(pieces, axis=1)[None]]
    ppermute x1, starting transfers between devices: 4.53 us -> 5.34 us  [shards(): before = lax.ppermute(keys_values, 'section', up)]
  transfers between devices with their start and end apart: 12 -> 12, of which waited for: 9 -> 7; matrix products, arithmetic and copies ran while one was open for 3% -> 5% of each run, Pallas kernels for 19% -> 19%
where the time goes in v4:
time: 59.7 us; the launch traced here: 59.5 us
  starting transfers between devices  21.2 us (36%)
  Pallas kernels  12.3 us (21%)
  waiting for transfers between devices  12.3 us (21%)
  local copies, waits for them, and re-layouts  10.5 us (18%)
  between operations  2.28 us (4%)
  other arithmetic  0.94 us (2%)
    ppermute x10, starting transfers between devices, rotate(): lax.ppermute(value, axis, [(i, (i + steps) % count) for i in range(count)])  14.5 us
    ppermute x10, waiting for transfers between devices, rotate(): lax.ppermute(value, axis, [(i, (i + steps) % count) for i in range(count)])  8.16 us
    unnamed x18, local copies, waits for them, and re-layouts  8.01 us
    ppermute x1, starting transfers between devices, shards(): before = lax.ppermute(keys_values, 'section', up)  5.34 us
    pallas_call x2, Pallas kernels, hold(): pl.pallas_call(hold_kernel, out_shape=jax.ShapeDtypeStruct(array.shape, a...  4.84 us
    ppermute x1, waiting for transfers between devices, shards(): after = lax.ppermute(keys_values, 'section', down)  4.13 us
    pallas_call x5, Pallas kernels, project(): pl.pallas_call(functools.partial(project_kernel, parts, rows, first, len(...  3.8 us
    pallas_call x4, Pallas kernels, attend(): pl.pallas_call(kernel, out_shape=out_shape, in_specs=[VMEM_SPEC] * len(op...  3.39 us
  transfers between devices with their start and end apart: 12, of which 7 were waited for; matrix products, arithmetic and copies ran while one was open for 5% of the time, Pallas kernels for 19%

profile of v4, /device:TPU:0, one launch (start us, length us, event | category | flops | bytes accessed | tf_op | source)
XLA Modules:
  0.0 59.5 jit_solution(11308057966280346180)
XLA Ops:
  0.5 1.3 %collective-permute-start.2 = (bf16[2,1,256,1024]{3,2,1,0:T(8,128)(2,1)}, bf16[2,1,256,1024]{3,2,1,0:T(8,128)(2,1)S(1)}, u32[]{:S(2)}, u32[]{:S(2)}) collective-permute-start(bf16[2,1,256,1024]{3,2,1,0:T(8,128)(2,1)} %own_ref.1), channel_id=1, source_target_pairs={{4,0},{8,4},{12,8},{5,1},{9,5},{13,9},{6,2},{10,6},{14,10},{7,3},{... | collective-permute-start | bytes 3145736 | tf_op jit(solution)/shard_map/ppermute | solution.py:201
  1.7 5.3 %collective-permute-start.1 = (bf16[2,1,256,1024]{3,2,1,0:T(8,128)(2,1)}, bf16[2,1,256,1024]{3,2,1,0:T(8,128)(2,1)S(1)}, u32[]{:S(2)}, u32[]{:S(2)}) collective-permute-start(bf16[2,1,256,1024]{3,2,1,0:T(8,128)(2,1)} %own_ref.1), channel_id=1, source_target_pairs={{0,4},{4,8},{8,12},{1,5},{5,9},{9,13},{2,6},{6,10},{10,14},{3,7},{... | collective-permute-start | bytes 3145736 | tf_op jit(solution)/shard_map/ppermute | solution.py:200
  7.1 4.0 %copy-done.2 = bf16[1024,5120]{1,0:T(8,128)(2,1)S(1)} copy-done((bf16[1024,5120]{1,0:T(8,128)(2,1)S(1)}, bf16[1024,5120]{1,0:T(8,128)(2,1)}, u32[]{:S(2)}) %copy-start.2) | copy-done | bytes 10485784
  11.1 0.7 %hold.2.refs_1_.refs_2_ = bf16[1024,5120]{1,0:T(8,128)(2,1)S(1)} custom-call(bf16[1024,5120]{1,0:T(8,128)(2,1)S(1)} %copy-done.2), custom_call_target="tpu_custom_call" | custom-call | bytes 1024 | tf_op jit(solution)/shard_map/hold/pallas_call | solution.py:103
  11.8 4.0 %copy-done.1 = bf16[1024,5120]{1,0:T(8,128)(2,1)} copy-done((bf16[1024,5120]{1,0:T(8,128)(2,1)}, bf16[1024,5120]{1,0:T(8,128)(2,1)S(1)}, u32[]{:S(2)}) %copy-start.1) | copy-done | bytes 10485784
  16.6 0.7 %fusion.5 = (s32[1]{0:T(128)}, s32[1]{0:T(128)}) fusion(s32[3]{0:T(128)S(1)} %copy-done.5, s32[]{:T(128)S(6)} %min.8, s32[]{:T(128)S(6)} %min.7), kind=kLoop, calls=%fused_computation.15 | loop fusion | bytes 24 | tf_op jit(solution)/shard_map/dynamic_slice | solution.py:196
  18.5 1.1 %dynamic-slice_bitcast_fusion.3 = (bf16[64,1024]{1,0:T(8,128)(2,1)S(1)}, bf16[64,1024]{1,0:T(8,128)(2,1)S(1)}, bf16[64,1024]{1,0:T(8,128)(2,1)S(1)}, bf16[64,1024]{1,0:T(8,128)(2,1)S(1)}) fusion(bf16[4,64,1024]{2,1,0:T(8,128)(2,1)} %bitcast.26, s32[]{:T(128)S(6)} %select_n.61, s32[]{:T(128)S(6)} %select_n.66, s32[]{:T(128)S(6)} %select_n.65, s32[]{:T(128)S(6)} %select_n.63), kind=kLoop, calls=%fused_computation.11 | loop fusion | bytes 1048592 | tf_op jit(solution)/shard_map/jit(dynamic_index_in_dim)/squeeze | solution.py:212
  19.7 0.9 %attend_own.1 = (f32[256,1024]{1,0:T(8,128)S(1)}, f32[256,1024]{1,0:T(8,128)S(1)}, f32[256,1024]{1,0:T(8,128)S(1)}) custom-call(bf16[256,1024]{1,0:T(8,128)(2,1)S(1)} %pad_maximum_fusion.q_ref, bf16[2,1,256,1024]{3,2,1,0:T(8,128)(2,1)S(1)} %copy-done.4), custom_call_target="tpu_custom_call" | custom-call | flops 268435456 | bytes 1572864 | tf_op jit(solution)/shard_map/attend_own/pallas_call | solution.py:81
  20.7 4.1 %hold.3.refs_1_.refs_3_ = bf16[1024,5120]{1,0:T(8,128)(2,1)S(1)} custom-call(bf16[1024,5120]{1,0:T(8,128)(2,1)} %collective-permute-done.src_ref), custom_call_target="tpu_custom_call" | custom-call | bytes 1024 | tf_op jit(solution)/shard_map/hold/pallas_call | solution.py:103
  24.8 4.1 %collective-permute-done.2.halo_ref = bf16[2,1,256,1024]{3,2,1,0:T(8,128)(2,1)S(1)} collective-permute-done((bf16[2,1,256,1024]{3,2,1,0:T(8,128)(2,1)}, bf16[2,1,256,1024]{3,2,1,0:T(8,128)(2,1)S(1)}, u32[]{:S(2)}, u32[]{:S(2)}) %collective-permute-start.2) | collective-permute-done | bytes 1048608 | tf_op jit(solution)/shard_map/ppermute | solution.py:201
  29.0 1.2 %attend_after.1 = (f32[256,1024]{1,0:T(8,128)S(1)}, f32[256,1024]{1,0:T(8,128)S(1)}, f32[256,1024]{1,0:T(8,128)S(1)}) custom-call(bf16[256,1024]{1,0:T(8,128)(2,1)S(1)} %pad_maximum_fusion.q_ref, bf16[2,1,256,1024]{3,2,1,0:T(8,128)(2,1)S(1)} %collective-permute-done.2.halo_ref, f32[1,256]{1,0:T(1,128)S(1)} %compare_select_fusion.mask_ref, ...), custom_call_target="tpu_custom_call" | custom-call | flops 268435456 | bytes 4719616 | tf_op jit(solution)/shard_map/attend_after/pallas_call | solution.py:81
  30.3 0.6 %attend_before.3 = bf16[128,1024]{1,0:T(8,128)(2,1)S(1)} custom-call(bf16[256,1024]{1,0:T(8,128)(2,1)S(1)} %pad_maximum_fusion.q_ref, bf16[2,1,256,1024]{3,2,1,0:T(8,128)(2,1)S(1)} %collective-permute-done.1.halo_ref, f32[1,256]{1,0:T(1,128)S(1)} %compare_select_fusion.1.mask_ref, f32[256,1024]{1,0:T(8,128)S(1)} %get-tuple-element.37.acc_ref, ...), custom_call_target="tpu_custom_call" | custom-call | flops 134217728 | bytes 4719616 | tf_op jit(solution)/shard_map/attend_before/pallas_call | solution.py:81
  31.0 0.6 %attend_before.2.refs_0_ = bf16[128,1024]{1,0:T(8,128)(2,1)S(1)} custom-call(bf16[256,1024]{1,0:T(8,128)(2,1)S(1)} %pad_maximum_fusion.q_ref, bf16[2,1,256,1024]{3,2,1,0:T(8,128)(2,1)S(1)} %collective-permute-done.1.halo_ref, f32[1,256]{1,0:T(1,128)S(1)} %compare_select_fusion.1.mask_ref, f32[256,1024]{1,0:T(8,128)S(1)} %get-tuple-element.37.acc_ref, ...), custom_call_target="tpu_custom_call" | custom-call | flops 134217728 | bytes 4719616 | tf_op jit(solution)/shard_map/attend_before/pallas_call | solution.py:81
  31.6 0.5 project.5.refs_2_
  32.5 0.6 project.6
  33.0 1.7 %collective-permute-start.4 = (bf16[64,1280]{1,0:T(8,128)(2,1)S(1)}, bf16[64,1280]{1,0:T(8,128)(2,1)S(1)}, u32[]{:S(2)}, u32[]{:S(2)}) collective-permute-start(bf16[64,1280]{1,0:T(8,128)(2,1)S(1)} %get-tuple-element.44), channel_id=1, source_target_pairs={{0,2},{2,0},{1,3},{3,1},{4,6},{6,4},{5,7},{7,5},{8,10},{10,8},{9,1... | collective-permute-start | bytes 491528 | tf_op jit(solution)/shard_map/ppermute | solution.py:186
  34.8 0.9 %project.7 = (bf16[64,1280]{1,0:T(8,128)(2,1)S(1)}, f32[64,1280]{1,0:T(8,128)S(1)}) custom-call(bf16[128,1024]{1,0:T(8,128)(2,1)S(1)} %attend_before.2.refs_0_, bf16[128,1024]{1,0:T(8,128)(2,1)S(1)} %collective-permute-done.3.refs_0_.refs_1_, bf16[1024,5120]{1,0:T(8,128)(2,1)S(1)} %bitcast.20, bf16[1024,5120]{1,0:T(8,128)(2,1)S(1)} %hold.3.refs_1_.refs_3_), custom_call_target="tpu_custom_call" | custom-call | flops 671088640 | bytes 5242880 | tf_op jit(solution)/shard_map/project/pallas_call | solution.py:143
  35.7 0.5 collective-permute-start.6
  36.1 0.9 %project.8 = (bf16[64,1280]{1,0:T(8,128)(2,1)S(1)}, f32[64,1280]{1,0:T(8,128)S(1)}) custom-call(bf16[128,1024]{1,0:T(8,128)(2,1)S(1)} %attend_before.2.refs_0_, bf16[128,1024]{1,0:T(8,128)(2,1)S(1)} %collective-permute-done.3.refs_0_.refs_1_, bf16[1024,5120]{1,0:T(8,128)(2,1)S(1)} %bitcast.20, bf16[1024,5120]{1,0:T(8,128)(2,1)S(1)} %hold.3.refs_1_.refs_3_), custom_call_target="tpu_custom_call" | custom-call | flops 671088640 | bytes 5242880 | tf_op jit(solution)/shard_map/project/pallas_call | solution.py:143
  37.0 1.7 %collective-permute-start.8 = (bf16[64,1280]{1,0:T(8,128)(2,1)S(1)}, bf16[64,1280]{1,0:T(8,128)(2,1)S(1)}, u32[]{:S(2)}, u32[]{:S(2)}) collective-permute-start(bf16[64,1280]{1,0:T(8,128)(2,1)S(1)} %get-tuple-element.50), channel_id=1, source_target_pairs={{0,2},{2,0},{1,3},{3,1},{4,6},{6,4},{5,7},{7,5},{8,10},{10,8},{9,1... | collective-permute-start | bytes 491528 | tf_op jit(solution)/shard_map/ppermute | solution.py:186
  38.7 0.9 %project.9 = (bf16[64,1280]{1,0:T(8,128)(2,1)S(1)}, f32[64,1280]{1,0:T(8,128)S(1)}) custom-call(bf16[128,1024]{1,0:T(8,128)(2,1)S(1)} %attend_before.2.refs_0_, bf16[128,1024]{1,0:T(8,128)(2,1)S(1)} %collective-permute-done.3.refs_0_.refs_1_, bf16[1024,5120]{1,0:T(8,128)(2,1)S(1)} %bitcast.20, bf16[1024,5120]{1,0:T(8,128)(2,1)S(1)} %hold.3.refs_1_.refs_3_), custom_call_target="tpu_custom_call" | custom-call | flops 671088640 | bytes 5242880 | tf_op jit(solution)/shard_map/project/pallas_call | solution.py:143
  39.6 0.5 collective-permute-start.10
  40.2 2.4 %collective-permute-start.5 = (bf16[64,1280]{1,0:T(8,128)(2,1)S(1)}, bf16[64,1280]{1,0:T(8,128)(2,1)S(1)}, u32[]{:S(2)}, u32[]{:S(2)}) collective-permute-start(bf16[64,1280]{1,0:T(8,128)(2,1)S(1)} %combine.4), channel_id=1, source_target_pairs={{0,4},{4,8},{8,12},{12,0},{1,5},{5,9},{9,13},{13,1},{2,6},{6,10},{... | collective-permute-start | bytes 491528 | tf_op jit(solution)/shard_map/ppermute | solution.py:186
  42.6 1.0 %collective-permute-done.6.refs_0_ = bf16[64,1280]{1,0:T(8,128)(2,1)S(1)} collective-permute-done((bf16[64,1280]{1,0:T(8,128)(2,1)S(1)}, bf16[64,1280]{1,0:T(8,128)(2,1)S(1)}, u32[]{:S(2)}, u32[]{:S(2)}) %collective-permute-start.6) | collective-permute-done | bytes 163872 | tf_op jit(solution)/shard_map/ppermute | solution.py:186
  43.7 2.4 %collective-permute-start.7 = (bf16[64,1280]{1,0:T(8,128)(2,1)S(1)}, bf16[64,1280]{1,0:T(8,128)(2,1)S(1)}, u32[]{:S(2)}, u32[]{:S(2)}) collective-permute-start(bf16[64,1280]{1,0:T(8,128)(2,1)S(1)} %combine.5), channel_id=1, source_target_pairs={{0,4},{4,8},{8,12},{12,0},{1,5},{5,9},{9,13},{13,1},{2,6},{6,10},{... | collective-permute-start | bytes 491528 | tf_op jit(solution)/shard_map/ppermute | solution.py:186
  46.2 1.0 %collective-permute-done.8.refs_0_ = bf16[64,1280]{1,0:T(8,128)(2,1)S(1)} collective-permute-done((bf16[64,1280]{1,0:T(8,128)(2,1)S(1)}, bf16[64,1280]{1,0:T(8,128)(2,1)S(1)}, u32[]{:S(2)}, u32[]{:S(2)}) %collective-permute-start.8) | collective-permute-done | bytes 163872 | tf_op jit(solution)/shard_map/ppermute | solution.py:186
  47.2 2.4 %collective-permute-start.9 = (bf16[64,1280]{1,0:T(8,128)(2,1)S(1)}, bf16[64,1280]{1,0:T(8,128)(2,1)S(1)}, u32[]{:S(2)}, u32[]{:S(2)}) collective-permute-start(bf16[64,1280]{1,0:T(8,128)(2,1)S(1)} %combine.6), channel_id=1, source_target_pairs={{0,4},{4,8},{8,12},{12,0},{1,5},{5,9},{9,13},{13,1},{2,6},{6,10},{... | collective-permute-start | bytes 491528 | tf_op jit(solution)/shard_map/ppermute | solution.py:186
  50.0 2.4 %collective-permute-start.11 = (bf16[64,1280]{1,0:T(8,128)(2,1)S(1)}, bf16[64,1280]{1,0:T(8,128)(2,1)S(1)}, u32[]{:S(2)}, u32[]{:S(2)}) collective-permute-start(bf16[64,1280]{1,0:T(8,128)(2,1)S(1)} %combine.7), channel_id=1, source_target_pairs={{0,4},{4,8},{8,12},{12,0},{1,5},{5,9},{9,13},{13,1},{2,6},{6,10},{... | collective-permute-start | bytes 491528 | tf_op jit(solution)/shard_map/ppermute | solution.py:186
  52.4 3.2 %collective-permute-done.9 = bf16[64,1280]{1,0:T(8,128)(2,1)S(1)} collective-permute-done((bf16[64,1280]{1,0:T(8,128)(2,1)S(1)}, bf16[64,1280]{1,0:T(8,128)(2,1)S(1)}, u32[]{:S(2)}, u32[]{:S(2)}) %collective-permute-start.9) | collective-permute-done | bytes 163872 | tf_op jit(solution)/shard_map/ppermute | solution.py:186
  55.6 0.9 %fusion.4 = bf16[64,5120]{1,0:T(8,128)(2,1)} fusion(bf16[64,1280]{1,0:T(8,128)(2,1)S(1)} %collective-permute-done.9, bf16[64,1280]{1,0:T(8,128)(2,1)S(1)} %collective-permute-done.7, bf16[64,1280]{1,0:T(8,128)(2,1)S(1)} %collective-permute-done.5), kind=kLoop, calls=%fused_computation.5 | loop fusion | flops 3276800 | bytes 1146880 | tf_op jit(solution)/shard_map/concatenate | solution.py:252
  56.5 2.3 %collective-permute-done.11 = bf16[64,1280]{1,0:T(8,128)(2,1)S(1)} collective-permute-done((bf16[64,1280]{1,0:T(8,128)(2,1)S(1)}, bf16[64,1280]{1,0:T(8,128)(2,1)S(1)}, u32[]{:S(2)}, u32[]{:S(2)}) %collective-permute-start.11) | collective-permute-done | bytes 163872 | tf_op jit(solution)/shard_map/ppermute | solution.py:186
  58.8 0.7 %bitcast_dynamic-update-slice_fusion = bf16[1,64,5120]{2,1,0:T(8,128)(2,1)} fusion(bf16[1,64,5120]{2,1,0:T(8,128)(2,1)} %bitcast.25, bf16[64,1280]{1,0:T(8,128)(2,1)S(1)} %collective-permute-done.11), kind=kLoop, calls=%fused_computation.7 | loop fusion | bytes 327680 | tf_op jit(solution)/shard_map/dynamic_update_slice | solution.py:254
  (34 shorter events, 1.6 us)
Async XLA Ops:
  0.0 20.6 %copy-start = (f32[8,5120]{1,0:T(8,128)S(1)}, f32[8,5120]{1,0:T(8,128)}, u32[]{:S(2)}) copy-start(f32[8,5120]{1,0:T(8,128)} %param.11) | copy-start | bytes 491524
  0.0 20.6 %collective-permute-start = (bf16[1024,5120]{1,0:T(8,128)(2,1)}, bf16[1024,5120]{1,0:T(8,128)(2,1)}, u32[]{:S(2)}, u32[]{:S(2)}) collective-permute-start(bf16[1024,5120]{1,0:T(8,128)(2,1)} %src_ref.1), channel_id=1, source_target_pairs={{0,1},{1,0},{2,3},{3,2},{4,5},{5,4},{6,7},{7,6},{8,9},{9,8},{10,11... | collective-permute-start | bytes 31457288 | tf_op jit(solution)/shard_map/ppermute | solution.py:186
  0.5 28.5 %collective-permute-start.2 = (bf16[2,1,256,1024]{3,2,1,0:T(8,128)(2,1)}, bf16[2,1,256,1024]{3,2,1,0:T(8,128)(2,1)S(1)}, u32[]{:S(2)}, u32[]{:S(2)}) collective-permute-start(bf16[2,1,256,1024]{3,2,1,0:T(8,128)(2,1)} %own_ref.1), channel_id=1, source_target_pairs={{4,0},{8,4},{12,8},{5,1},{9,5},{13,9},{6,2},{10,6},{14,10},{7,3},{... | collective-permute-start | bytes 3145736 | tf_op jit(solution)/shard_map/ppermute | solution.py:201
  1.7 28.5 %collective-permute-start.1 = (bf16[2,1,256,1024]{3,2,1,0:T(8,128)(2,1)}, bf16[2,1,256,1024]{3,2,1,0:T(8,128)(2,1)S(1)}, u32[]{:S(2)}, u32[]{:S(2)}) collective-permute-start(bf16[2,1,256,1024]{3,2,1,0:T(8,128)(2,1)} %own_ref.1), channel_id=1, source_target_pairs={{0,4},{4,8},{8,12},{1,5},{5,9},{9,13},{2,6},{6,10},{10,14},{3,7},{... | collective-permute-start | bytes 3145736 | tf_op jit(solution)/shard_map/ppermute | solution.py:200
  7.1 4.0 %copy-start.2 = (bf16[1024,5120]{1,0:T(8,128)(2,1)S(1)}, bf16[1024,5120]{1,0:T(8,128)(2,1)}, u32[]{:S(2)}) copy-start(bf16[1024,5120]{1,0:T(8,128)(2,1)} %src_ref.1) | copy-start | bytes 31457284
  11.1 5.5 %copy-start.5 = (s32[3]{0:T(128)S(1)}, s32[3]{0:T(128)}, u32[]{:S(2)}) copy-start(s32[3]{0:T(128)} %param.13) | copy-start | bytes 40
  11.8 4.0 %copy-start.1 = (bf16[1024,5120]{1,0:T(8,128)(2,1)}, bf16[1024,5120]{1,0:T(8,128)(2,1)S(1)}, u32[]{:S(2)}) copy-start(bf16[1024,5120]{1,0:T(8,128)(2,1)S(1)} %hold.2.refs_1_.refs_2_) | copy-start | bytes 31457284
  15.8 3.8 %copy-start.4 = (bf16[2,1,256,1024]{3,2,1,0:T(8,128)(2,1)S(1)}, bf16[2,1,256,1024]{3,2,1,0:T(8,128)(2,1)}, u32[]{:S(2)}) copy-start(bf16[2,1,256,1024]{3,2,1,0:T(8,128)(2,1)} %own_ref.1) | copy-start | bytes 3145732
  20.7 10.9 %slice-start = ((s8[10485760]{0:T(1024)(128)(4,1)}), s8[4194304]{0:T(1024)(128)(4,1)S(1)}, s32[]{:S(2)}) async-start(s8[10485760]{0:T(1024)(128)(4,1)} %bitcast.19), calls=%async_computation | async-start | bytes 8388608
  20.7 10.9 %slice-start.1 = ((s8[10485760]{0:T(1024)(128)(4,1)}), s8[4194304]{0:T(1024)(128)(4,1)S(1)}, s32[]{:S(2)}) async-start(s8[10485760]{0:T(1024)(128)(4,1)} %bitcast.19), calls=%async_computation.1 | async-start | bytes 8388608
  24.8 6.8 %slice-start.2 = ((s8[10485760]{0:T(1024)(128)(4,1)}), s8[2097152]{0:T(1024)(128)(4,1)S(1)}, s32[]{:S(2)}) async-start(s8[10485760]{0:T(1024)(128)(4,1)} %bitcast.19), calls=%async_computation.2 | async-start | bytes 4194304
  30.9 1.6 %collective-permute-start.3 = (bf16[128,1024]{1,0:T(8,128)(2,1)S(1)}, bf16[128,1024]{1,0:T(8,128)(2,1)S(1)}, u32[]{:S(2)}, u32[]{:S(2)}) collective-permute-start(bf16[128,1024]{1,0:T(8,128)(2,1)S(1)} %attend_before.3), channel_id=1, source_target_pairs={{0,1},{1,0},{2,3},{3,2},{4,5},{5,4},{6,7},{7,6},{8,9},{9,8},{10,11... | collective-permute-start | bytes 786440 | tf_op jit(solution)/shard_map/ppermute | solution.py:186
  33.0 7.1 %collective-permute-start.4 = (bf16[64,1280]{1,0:T(8,128)(2,1)S(1)}, bf16[64,1280]{1,0:T(8,128)(2,1)S(1)}, u32[]{:S(2)}, u32[]{:S(2)}) collective-permute-start(bf16[64,1280]{1,0:T(8,128)(2,1)S(1)} %get-tuple-element.44), channel_id=1, source_target_pairs={{0,2},{2,0},{1,3},{3,1},{4,6},{6,4},{5,7},{7,5},{8,10},{10,8},{9,1... | collective-permute-start | bytes 491528 | tf_op jit(solution)/shard_map/ppermute | solution.py:186
  35.7 8.0 %collective-permute-start.6 = (bf16[64,1280]{1,0:T(8,128)(2,1)S(1)}, bf16[64,1280]{1,0:T(8,128)(2,1)S(1)}, u32[]{:S(2)}, u32[]{:S(2)}) collective-permute-start(bf16[64,1280]{1,0:T(8,128)(2,1)S(1)} %get-tuple-element.48), channel_id=1, source_target_pairs={{0,2},{2,0},{1,3},{3,1},{4,6},{6,4},{5,7},{7,5},{8,10},{10,8},{9,1... | collective-permute-start | bytes 491528 | tf_op jit(solution)/shard_map/ppermute | solution.py:186
  37.0 3.1 %copy-start.3 = (bf16[1,64,5120]{2,1,0:T(8,128)(2,1)S(1)}, bf16[1,64,5120]{2,1,0:T(8,128)(2,1)}, u32[]{:S(2)}) copy-start(bf16[1,64,5120]{2,1,0:T(8,128)(2,1)} %param.9) | copy-start | bytes 1966084
  37.0 10.1 %collective-permute-start.8 = (bf16[64,1280]{1,0:T(8,128)(2,1)S(1)}, bf16[64,1280]{1,0:T(8,128)(2,1)S(1)}, u32[]{:S(2)}, u32[]{:S(2)}) collective-permute-start(bf16[64,1280]{1,0:T(8,128)(2,1)S(1)} %get-tuple-element.50), channel_id=1, source_target_pairs={{0,2},{2,0},{1,3},{3,1},{4,6},{6,4},{5,7},{7,5},{8,10},{10,8},{9,1... | collective-permute-start | bytes 491528 | tf_op jit(solution)/shard_map/ppermute | solution.py:186
  39.6 10.3 %collective-permute-start.10 = (bf16[64,1280]{1,0:T(8,128)(2,1)S(1)}, bf16[64,1280]{1,0:T(8,128)(2,1)S(1)}, u32[]{:S(2)}, u32[]{:S(2)}) collective-permute-start(bf16[64,1280]{1,0:T(8,128)(2,1)S(1)} %get-tuple-element.52), channel_id=1, source_target_pairs={{0,2},{2,0},{1,3},{3,1},{4,6},{6,4},{5,7},{7,5},{8,10},{10,8},{9,1... | collective-permute-start | bytes 491528 | tf_op jit(solution)/shard_map/ppermute | solution.py:186
  40.2 12.2 %collective-permute-start.5 = (bf16[64,1280]{1,0:T(8,128)(2,1)S(1)}, bf16[64,1280]{1,0:T(8,128)(2,1)S(1)}, u32[]{:S(2)}, u32[]{:S(2)}) collective-permute-start(bf16[64,1280]{1,0:T(8,128)(2,1)S(1)} %combine.4), channel_id=1, source_target_pairs={{0,4},{4,8},{8,12},{12,0},{1,5},{5,9},{9,13},{13,1},{2,6},{6,10},{... | collective-permute-start | bytes 491528 | tf_op jit(solution)/shard_map/ppermute | solution.py:186
  43.7 8.7 %collective-permute-start.7 = (bf16[64,1280]{1,0:T(8,128)(2,1)S(1)}, bf16[64,1280]{1,0:T(8,128)(2,1)S(1)}, u32[]{:S(2)}, u32[]{:S(2)}) collective-permute-start(bf16[64,1280]{1,0:T(8,128)(2,1)S(1)} %combine.5), channel_id=1, source_target_pairs={{0,4},{4,8},{8,12},{12,0},{1,5},{5,9},{9,13},{13,1},{2,6},{6,10},{... | collective-permute-start | bytes 491528 | tf_op jit(solution)/shard_map/ppermute | solution.py:186
  47.2 8.4 %collective-permute-start.9 = (bf16[64,1280]{1,0:T(8,128)(2,1)S(1)}, bf16[64,1280]{1,0:T(8,128)(2,1)S(1)}, u32[]{:S(2)}, u32[]{:S(2)}) collective-permute-start(bf16[64,1280]{1,0:T(8,128)(2,1)S(1)} %combine.6), channel_id=1, source_target_pairs={{0,4},{4,8},{8,12},{12,0},{1,5},{5,9},{9,13},{13,1},{2,6},{6,10},{... | collective-permute-start | bytes 491528 | tf_op jit(solution)/shard_map/ppermute | solution.py:186
  50.0 8.8 %collective-permute-start.11 = (bf16[64,1280]{1,0:T(8,128)(2,1)S(1)}, bf16[64,1280]{1,0:T(8,128)(2,1)S(1)}, u32[]{:S(2)}, u32[]{:S(2)}) collective-permute-start(bf16[64,1280]{1,0:T(8,128)(2,1)S(1)} %combine.7), channel_id=1, source_target_pairs={{0,4},{4,8},{8,12},{12,0},{1,5},{5,9},{9,13},{13,1},{2,6},{6,10},{... | collective-permute-start | bytes 491528 | tf_op jit(solution)/shard_map/ppermute | solution.py:186

commit v5 on v4

--- a/solution.py
+++ b/solution.py
@@ -195,10 +195,11 @@
     next_width = jnp.where(
         section_id < sections - 1, pair_window[jnp.clip(section_id, 0, final_pair)], 0
     )
-    up = [(i, i + 1) for i in range(sections - 1)]
-    down = [(j, i) for i, j in up]
-    before = lax.ppermute(keys_values, "section", up)
-    after = lax.ppermute(keys_values, "section", down)
+    swaps = [
+        [pair for i in range(odd, sections - 1, 2) for pair in ((i, i + 1), (i + 1, i))]
+        for odd in (0, 1)
+    ]
+    first_halo, second_halo = (lax.ppermute(keys_values, "section", pairs) for pairs in swaps)
     weights = [hold(out_weight)]
     weights += [hold(rotate(out_weight, "mp", l)) for l in range(1, cores)]
     own_latents = latents[0]
@@ -212,8 +213,10 @@
             order.append(lax.dynamic_index_in_dim(blocks, block, keepdims=False))
     own_queries = jnp.concatenate(order, axis=0)
     col = jnp.arange(span_tok, dtype=jnp.int32)[None]
-    prev_mask = jnp.where(col >= span_tok - prev_width, 0.0, NEG_BIG).astype(jnp.float32)
-    next_mask = jnp.where(col < next_width, 0.0, NEG_BIG).astype(jnp.float32)
+    prev_keys, next_keys = col >= span_tok - prev_width, col < next_width
+    from_next = section_id % 2 == 0
+    first_mask = jnp.where(jnp.where(from_next, next_keys, prev_keys), 0.0, NEG_BIG)
+    second_mask = jnp.where(jnp.where(from_next, prev_keys, next_keys), 0.0, NEG_BIG)
 
     gate_row = lax.dynamic_slice_in_dim(gate_table, level_index[0], 1, axis=0)
     width = queries.shape[2]
@@ -223,7 +226,7 @@
     state, weights, gate_row = lax.optimization_barrier((state, weights, gate_row))
     kernel = functools.partial(halo_kernel, 0, False)
     state = attend(
-        kernel, "attend_after", (wide,) * 3, flops, own_queries, after, next_mask, *state
+        kernel, "attend_first", (wide,) * 3, flops, own_queries, first_halo, first_mask, *state
     )
     per_core = spans * rows
     out_shape = (jax.ShapeDtypeStruct((per_core, width), jnp.bfloat16),)
@@ -231,8 +234,8 @@
     for l in range(cores - 1, -1, -1):
         kernel = functools.partial(halo_kernel, (cores - 1 - l) * per_core, True)
         (out,) = attend(
-            kernel, "attend_before", out_shape, flops // cores,
-            own_queries, before, prev_mask, *state,
+            kernel, "attend_second", out_shape, flops // cores,
+            own_queries, second_halo, second_mask, *state,
         )
         att.insert(0, out if l == 0 else rotate(out, "mp", l))
 

time: 59.7 us -> 57 us (0.955)
  waiting for transfers between devices: 12.3 us -> 9.42 us
    ppermute x10, waiting for transfers between devices: 8.16 us -> 3.92 us  [rotate(): lax.ppermute(value, axis, [(i, (i + steps) % count) for i in range(count)])]
    ppermute x10, starting transfers between devices: 14.5 us -> 18 us  [rotate(): lax.ppermute(value, axis, [(i, (i + steps) % count) for i in range(count)])]
    ppermute x2, starting transfers between devices: 6.62 us -> 3.36 us  [shards(): lax.ppermute(keys_values, 'section', pairs)]
    ppermute x2, waiting for transfers between devices: 4.17 us -> 5.5 us  [shards(): lax.ppermute(keys_values, 'section', pairs)]
  transfers between devices with their start and end apart: 12 -> 12, of which waited for: 7 -> 4; matrix products, arithmetic and copies ran while one was open for 5% -> 5% of each run, Pallas kernels for 19% -> 20%
where the time goes in v5:
time: 57 us; the launch traced here: 56.8 us
  starting transfers between devices  21.3 us (37%)
  Pallas kernels  12.3 us (22%)
  local copies, waits for them, and re-layouts  10.5 us (18%)
  waiting for transfers between devices  9.42 us (17%)
  between operations  2.29 us (4%)
  other arithmetic  0.94 us (2%)
    ppermute x10, starting transfers between devices, rotate(): lax.ppermute(value, axis, [(i, (i + steps) % count) for i in range(count)])  18 us
    unnamed x18, local copies, waits for them, and re-layouts  8.01 us
    ppermute x2, waiting for transfers between devices, shards(): lax.ppermute(keys_values, 'section', pairs)  5.5 us
    pallas_call x2, Pallas kernels, hold(): pl.pallas_call(hold_kernel, out_shape=jax.ShapeDtypeStruct(array.shape, a...  4.84 us
    ppermute x10, waiting for transfers between devices, rotate(): lax.ppermute(value, axis, [(i, (i + steps) % count) for i in range(count)])  3.92 us
    pallas_call x5, Pallas kernels, project(): pl.pallas_call(functools.partial(project_kernel, parts, rows, first, len(...  3.8 us
    pallas_call x4, Pallas kernels, attend(): pl.pallas_call(kernel, out_shape=out_shape, in_specs=[VMEM_SPEC] * len(op...  3.38 us
    ppermute x2, starting transfers between devices, shards(): lax.ppermute(keys_values, 'section', pairs)  3.36 us
  transfers between devices with their start and end apart: 12, of which 4 were waited for; matrix products, arithmetic and copies ran while one was open for 5% of the time, Pallas kernels for 20%

profile of v5, /device:TPU:0, one launch (start us, length us, event | category | flops | bytes accessed | tf_op | source)
XLA Modules:
  0.0 56.8 jit_solution(18358327013081759990)
XLA Ops:
  0.0 0.5 collective-permute-start
  0.5 2.6 %collective-permute-start.2 = (bf16[2,1,256,1024]{3,2,1,0:T(8,128)(2,1)}, bf16[2,1,256,1024]{3,2,1,0:T(8,128)(2,1)S(1)}, u32[]{:S(2)}, u32[]{:S(2)}) collective-permute-start(bf16[2,1,256,1024]{3,2,1,0:T(8,128)(2,1)} %own_ref.1), channel_id=1, source_target_pairs={{0,4},{4,0},{8,12},{12,8},{1,5},{5,1},{9,13},{13,9},{2,6},{6,2},{1... | collective-permute-start | bytes 3145736 | tf_op jit(solution)/shard_map/ppermute | solution.py:202
  3.1 0.7 %collective-permute-start.1 = (bf16[2,1,256,1024]{3,2,1,0:T(8,128)(2,1)}, bf16[2,1,256,1024]{3,2,1,0:T(8,128)(2,1)S(1)}, u32[]{:S(2)}, u32[]{:S(2)}) collective-permute-start(bf16[2,1,256,1024]{3,2,1,0:T(8,128)(2,1)} %own_ref.1), channel_id=1, source_target_pairs={{4,8},{8,4},{5,9},{9,5},{6,10},{10,6},{7,11},{11,7},{20,24},{24,20... | collective-permute-start | bytes 3145736 | tf_op jit(solution)/shard_map/ppermute | solution.py:202
  3.9 4.0 %copy-done.2 = bf16[1024,5120]{1,0:T(8,128)(2,1)S(1)} copy-done((bf16[1024,5120]{1,0:T(8,128)(2,1)S(1)}, bf16[1024,5120]{1,0:T(8,128)(2,1)}, u32[]{:S(2)}) %copy-start.2) | copy-done | bytes 10485784
  7.9 0.7 %hold.2.refs_1_.refs_2_ = bf16[1024,5120]{1,0:T(8,128)(2,1)S(1)} custom-call(bf16[1024,5120]{1,0:T(8,128)(2,1)S(1)} %copy-done.2), custom_call_target="tpu_custom_call" | custom-call | bytes 1024 | tf_op jit(solution)/shard_map/hold/pallas_call | solution.py:103
  8.6 4.0 %copy-done.1 = bf16[1024,5120]{1,0:T(8,128)(2,1)} copy-done((bf16[1024,5120]{1,0:T(8,128)(2,1)}, bf16[1024,5120]{1,0:T(8,128)(2,1)S(1)}, u32[]{:S(2)}) %copy-start.1) | copy-done | bytes 10485784
  13.4 0.7 %fusion.5 = (s32[1]{0:T(128)}, s32[1]{0:T(128)}) fusion(s32[3]{0:T(128)S(1)} %copy-done.5, s32[]{:T(128)S(6)} %min.7, s32[]{:T(128)S(6)} %min.8), kind=kLoop, calls=%fused_computation.15 | loop fusion | bytes 24 | tf_op jit(solution)/shard_map/dynamic_slice | solution.py:194
  15.2 1.1 %dynamic-slice_bitcast_fusion.3 = (bf16[64,1024]{1,0:T(8,128)(2,1)S(1)}, bf16[64,1024]{1,0:T(8,128)(2,1)S(1)}, bf16[64,1024]{1,0:T(8,128)(2,1)S(1)}, bf16[64,1024]{1,0:T(8,128)(2,1)S(1)}) fusion(bf16[4,64,1024]{2,1,0:T(8,128)(2,1)} %bitcast.26, s32[]{:T(128)S(6)} %select_n.93, s32[]{:T(128)S(6)} %select_n.98, s32[]{:T(128)S(6)} %select_n.97, s32[]{:T(128)S(6)} %select_n.95), kind=kLoop, calls=%fused_computation.11 | loop fusion | bytes 1048592 | tf_op jit(solution)/shard_map/jit(dynamic_index_in_dim)/squeeze | solution.py:213
  16.4 0.9 %attend_own.1 = (f32[256,1024]{1,0:T(8,128)S(1)}, f32[256,1024]{1,0:T(8,128)S(1)}, f32[256,1024]{1,0:T(8,128)S(1)}) custom-call(bf16[256,1024]{1,0:T(8,128)(2,1)S(1)} %pad_maximum_fusion.q_ref, bf16[2,1,256,1024]{3,2,1,0:T(8,128)(2,1)S(1)} %copy-done.4), custom_call_target="tpu_custom_call" | custom-call | flops 268435456 | bytes 1572864 | tf_op jit(solution)/shard_map/attend_own/pallas_call | solution.py:81
  17.4 4.1 %hold.3.refs_1_.refs_3_ = bf16[1024,5120]{1,0:T(8,128)(2,1)S(1)} custom-call(bf16[1024,5120]{1,0:T(8,128)(2,1)} %collective-permute-done.src_ref), custom_call_target="tpu_custom_call" | custom-call | bytes 1024 | tf_op jit(solution)/shard_map/hold/pallas_call | solution.py:103
  21.6 5.5 %collective-permute-done.2.halo_ref = bf16[2,1,256,1024]{3,2,1,0:T(8,128)(2,1)S(1)} collective-permute-done((bf16[2,1,256,1024]{3,2,1,0:T(8,128)(2,1)}, bf16[2,1,256,1024]{3,2,1,0:T(8,128)(2,1)S(1)}, u32[]{:S(2)}, u32[]{:S(2)}) %collective-permute-start.2) | collective-permute-done | bytes 1048608 | tf_op jit(solution)/shard_map/ppermute | solution.py:202
  27.1 1.2 %attend_first.1 = (f32[256,1024]{1,0:T(8,128)S(1)}, f32[256,1024]{1,0:T(8,128)S(1)}, f32[256,1024]{1,0:T(8,128)S(1)}) custom-call(bf16[256,1024]{1,0:T(8,128)(2,1)S(1)} %pad_maximum_fusion.q_ref, bf16[2,1,256,1024]{3,2,1,0:T(8,128)(2,1)S(1)} %collective-permute-done.2.halo_ref, f32[1,256]{1,0:T(1,128)S(1)} %select_select_fusion.mask_ref, ...), custom_call_target="tpu_custom_call" | custom-call | flops 268435456 | bytes 4719616 | tf_op jit(solution)/shard_map/attend_first/pallas_call | solution.py:81
  28.3 0.6 %attend_second.3 = bf16[128,1024]{1,0:T(8,128)(2,1)S(1)} custom-call(bf16[256,1024]{1,0:T(8,128)(2,1)S(1)} %pad_maximum_fusion.q_ref, bf16[2,1,256,1024]{3,2,1,0:T(8,128)(2,1)S(1)} %collective-permute-done.1.halo_ref, f32[1,256]{1,0:T(1,128)S(1)} %select_select_fusion.1.mask_ref, f32[256,1024]{1,0:T(8,128)S(1)} %get-tuple-element.37.acc_ref, ...), custom_call_target="tpu_custom_call" | custom-call | flops 134217728 | bytes 4719616 | tf_op jit(solution)/shard_map/attend_second/pallas_call | solution.py:81
  29.0 0.6 %attend_second.2.refs_0_ = bf16[128,1024]{1,0:T(8,128)(2,1)S(1)} custom-call(bf16[256,1024]{1,0:T(8,128)(2,1)S(1)} %pad_maximum_fusion.q_ref, bf16[2,1,256,1024]{3,2,1,0:T(8,128)(2,1)S(1)} %collective-permute-done.1.halo_ref, f32[1,256]{1,0:T(1,128)S(1)} %select_select_fusion.1.mask_ref, f32[256,1024]{1,0:T(8,128)S(1)} %get-tuple-element.37.acc_ref, ...), custom_call_target="tpu_custom_call" | custom-call | flops 134217728 | bytes 4719616 | tf_op jit(solution)/shard_map/attend_second/pallas_call | solution.py:81
  29.7 0.5 project.5.refs_2_
  30.2 0.3 collective-permute-done.3.refs_0_.refs_1_
  30.6 0.6 project.6
  31.1 1.7 %collective-permute-start.4 = (bf16[64,1280]{1,0:T(8,128)(2,1)S(1)}, bf16[64,1280]{1,0:T(8,128)(2,1)S(1)}, u32[]{:S(2)}, u32[]{:S(2)}) collective-permute-start(bf16[64,1280]{1,0:T(8,128)(2,1)S(1)} %get-tuple-element.44), channel_id=1, source_target_pairs={{0,2},{2,0},{1,3},{3,1},{4,6},{6,4},{5,7},{7,5},{8,10},{10,8},{9,1... | collective-permute-start | bytes 491528 | tf_op jit(solution)/shard_map/ppermute | solution.py:186
  32.8 0.9 %project.7 = (bf16[64,1280]{1,0:T(8,128)(2,1)S(1)}, f32[64,1280]{1,0:T(8,128)S(1)}) custom-call(bf16[128,1024]{1,0:T(8,128)(2,1)S(1)} %attend_second.2.refs_0_, bf16[128,1024]{1,0:T(8,128)(2,1)S(1)} %collective-permute-done.3.refs_0_.refs_1_, bf16[1024,5120]{1,0:T(8,128)(2,1)S(1)} %bitcast.20, bf16[1024,5120]{1,0:T(8,128)(2,1)S(1)} %hold.3.refs_1_.refs_3_), custom_call_target="tpu_custom_call" | custom-call | flops 671088640 | bytes 5242880 | tf_op jit(solution)/shard_map/project/pallas_call | solution.py:143
  33.8 0.4 collective-permute-start.6
  34.2 0.9 %project.8 = (bf16[64,1280]{1,0:T(8,128)(2,1)S(1)}, f32[64,1280]{1,0:T(8,128)S(1)}) custom-call(bf16[128,1024]{1,0:T(8,128)(2,1)S(1)} %attend_second.2.refs_0_, bf16[128,1024]{1,0:T(8,128)(2,1)S(1)} %collective-permute-done.3.refs_0_.refs_1_, bf16[1024,5120]{1,0:T(8,128)(2,1)S(1)} %bitcast.20, bf16[1024,5120]{1,0:T(8,128)(2,1)S(1)} %hold.3.refs_1_.refs_3_), custom_call_target="tpu_custom_call" | custom-call | flops 671088640 | bytes 5242880 | tf_op jit(solution)/shard_map/project/pallas_call | solution.py:143
  35.1 1.7 %collective-permute-start.8 = (bf16[64,1280]{1,0:T(8,128)(2,1)S(1)}, bf16[64,1280]{1,0:T(8,128)(2,1)S(1)}, u32[]{:S(2)}, u32[]{:S(2)}) collective-permute-start(bf16[64,1280]{1,0:T(8,128)(2,1)S(1)} %get-tuple-element.50), channel_id=1, source_target_pairs={{0,2},{2,0},{1,3},{3,1},{4,6},{6,4},{5,7},{7,5},{8,10},{10,8},{9,1... | collective-permute-start | bytes 491528 | tf_op jit(solution)/shard_map/ppermute | solution.py:186
  36.8 0.9 %project.9 = (bf16[64,1280]{1,0:T(8,128)(2,1)S(1)}, f32[64,1280]{1,0:T(8,128)S(1)}) custom-call(bf16[128,1024]{1,0:T(8,128)(2,1)S(1)} %attend_second.2.refs_0_, bf16[128,1024]{1,0:T(8,128)(2,1)S(1)} %collective-permute-done.3.refs_0_.refs_1_, bf16[1024,5120]{1,0:T(8,128)(2,1)S(1)} %bitcast.20, bf16[1024,5120]{1,0:T(8,128)(2,1)S(1)} %hold.3.refs_1_.refs_3_), custom_call_target="tpu_custom_call" | custom-call | flops 671088640 | bytes 5242880 | tf_op jit(solution)/shard_map/project/pallas_call | solution.py:143
  37.8 0.4 collective-permute-start.10
  38.3 3.6 %collective-permute-start.5 = (bf16[64,1280]{1,0:T(8,128)(2,1)S(1)}, bf16[64,1280]{1,0:T(8,128)(2,1)S(1)}, u32[]{:S(2)}, u32[]{:S(2)}) collective-permute-start(bf16[64,1280]{1,0:T(8,128)(2,1)S(1)} %combine.4), channel_id=1, source_target_pairs={{0,4},{4,8},{8,12},{12,0},{1,5},{5,9},{9,13},{13,1},{2,6},{6,10},{... | collective-permute-start | bytes 491528 | tf_op jit(solution)/shard_map/ppermute | solution.py:186
  41.9 3.4 %collective-permute-start.7 = (bf16[64,1280]{1,0:T(8,128)(2,1)S(1)}, bf16[64,1280]{1,0:T(8,128)(2,1)S(1)}, u32[]{:S(2)}, u32[]{:S(2)}) collective-permute-start(bf16[64,1280]{1,0:T(8,128)(2,1)S(1)} %combine.5), channel_id=1, source_target_pairs={{0,4},{4,8},{8,12},{12,0},{1,5},{5,9},{9,13},{13,1},{2,6},{6,10},{... | collective-permute-start | bytes 491528 | tf_op jit(solution)/shard_map/ppermute | solution.py:186
  45.4 3.4 %collective-permute-start.9 = (bf16[64,1280]{1,0:T(8,128)(2,1)S(1)}, bf16[64,1280]{1,0:T(8,128)(2,1)S(1)}, u32[]{:S(2)}, u32[]{:S(2)}) collective-permute-start(bf16[64,1280]{1,0:T(8,128)(2,1)S(1)} %combine.6), channel_id=1, source_target_pairs={{0,4},{4,8},{8,12},{12,0},{1,5},{5,9},{9,13},{13,1},{2,6},{6,10},{... | collective-permute-start | bytes 491528 | tf_op jit(solution)/shard_map/ppermute | solution.py:186
  48.9 2.7 %collective-permute-start.11 = (bf16[64,1280]{1,0:T(8,128)(2,1)S(1)}, bf16[64,1280]{1,0:T(8,128)(2,1)S(1)}, u32[]{:S(2)}, u32[]{:S(2)}) collective-permute-start(bf16[64,1280]{1,0:T(8,128)(2,1)S(1)} %combine.7), channel_id=1, source_target_pairs={{0,4},{4,8},{8,12},{12,0},{1,5},{5,9},{9,13},{13,1},{2,6},{6,10},{... | collective-permute-start | bytes 491528 | tf_op jit(solution)/shard_map/ppermute | solution.py:186
  51.7 1.3 %collective-permute-done.9 = bf16[64,1280]{1,0:T(8,128)(2,1)S(1)} collective-permute-done((bf16[64,1280]{1,0:T(8,128)(2,1)S(1)}, bf16[64,1280]{1,0:T(8,128)(2,1)S(1)}, u32[]{:S(2)}, u32[]{:S(2)}) %collective-permute-start.9) | collective-permute-done | bytes 163872 | tf_op jit(solution)/shard_map/ppermute | solution.py:186
  53.0 0.9 %fusion.4 = bf16[64,5120]{1,0:T(8,128)(2,1)} fusion(bf16[64,1280]{1,0:T(8,128)(2,1)S(1)} %collective-permute-done.9, bf16[64,1280]{1,0:T(8,128)(2,1)S(1)} %collective-permute-done.7, bf16[64,1280]{1,0:T(8,128)(2,1)S(1)} %collective-permute-done.5), kind=kLoop, calls=%fused_computation.5 | loop fusion | flops 3276800 | bytes 1146880 | tf_op jit(solution)/shard_map/concatenate | solution.py:255
  53.9 2.2 %collective-permute-done.11 = bf16[64,1280]{1,0:T(8,128)(2,1)S(1)} collective-permute-done((bf16[64,1280]{1,0:T(8,128)(2,1)S(1)}, bf16[64,1280]{1,0:T(8,128)(2,1)S(1)}, u32[]{:S(2)}, u32[]{:S(2)}) %collective-permute-start.11) | collective-permute-done | bytes 163872 | tf_op jit(solution)/shard_map/ppermute | solution.py:186
  56.1 0.7 %bitcast_dynamic-update-slice_fusion = bf16[1,64,5120]{2,1,0:T(8,128)(2,1)} fusion(bf16[1,64,5120]{2,1,0:T(8,128)(2,1)} %bitcast.25, bf16[64,1280]{1,0:T(8,128)(2,1)S(1)} %collective-permute-done.11), kind=kLoop, calls=%fused_computation.7 | loop fusion | bytes 327680 | tf_op jit(solution)/shard_map/dynamic_update_slice | solution.py:257
  (34 shorter events, 0.5 us)
Async XLA Ops:
  0.0 17.3 %copy-start = (f32[8,5120]{1,0:T(8,128)S(1)}, f32[8,5120]{1,0:T(8,128)}, u32[]{:S(2)}) copy-start(f32[8,5120]{1,0:T(8,128)} %param.11) | copy-start | bytes 491524
  0.0 17.4 %collective-permute-start = (bf16[1024,5120]{1,0:T(8,128)(2,1)}, bf16[1024,5120]{1,0:T(8,128)(2,1)}, u32[]{:S(2)}, u32[]{:S(2)}) collective-permute-start(bf16[1024,5120]{1,0:T(8,128)(2,1)} %src_ref.1), channel_id=1, source_target_pairs={{0,1},{1,0},{2,3},{3,2},{4,5},{5,4},{6,7},{7,6},{8,9},{9,8},{10,11... | collective-permute-start | bytes 31457288 | tf_op jit(solution)/shard_map/ppermute | solution.py:186
  0.5 26.6 %collective-permute-start.2 = (bf16[2,1,256,1024]{3,2,1,0:T(8,128)(2,1)}, bf16[2,1,256,1024]{3,2,1,0:T(8,128)(2,1)S(1)}, u32[]{:S(2)}, u32[]{:S(2)}) collective-permute-start(bf16[2,1,256,1024]{3,2,1,0:T(8,128)(2,1)} %own_ref.1), channel_id=1, source_target_pairs={{0,4},{4,0},{8,12},{12,8},{1,5},{5,1},{9,13},{13,9},{2,6},{6,2},{1... | collective-permute-start | bytes 3145736 | tf_op jit(solution)/shard_map/ppermute | solution.py:202
  3.1 25.2 %collective-permute-start.1 = (bf16[2,1,256,1024]{3,2,1,0:T(8,128)(2,1)}, bf16[2,1,256,1024]{3,2,1,0:T(8,128)(2,1)S(1)}, u32[]{:S(2)}, u32[]{:S(2)}) collective-permute-start(bf16[2,1,256,1024]{3,2,1,0:T(8,128)(2,1)} %own_ref.1), channel_id=1, source_target_pairs={{4,8},{8,4},{5,9},{9,5},{6,10},{10,6},{7,11},{11,7},{20,24},{24,20... | collective-permute-start | bytes 3145736 | tf_op jit(solution)/shard_map/ppermute | solution.py:202
  3.9 4.0 %copy-start.2 = (bf16[1024,5120]{1,0:T(8,128)(2,1)S(1)}, bf16[1024,5120]{1,0:T(8,128)(2,1)}, u32[]{:S(2)}) copy-start(bf16[1024,5120]{1,0:T(8,128)(2,1)} %src_ref.1) | copy-start | bytes 31457284
  7.8 5.5 %copy-start.5 = (s32[3]{0:T(128)S(1)}, s32[3]{0:T(128)}, u32[]{:S(2)}) copy-start(s32[3]{0:T(128)} %param.13) | copy-start | bytes 40
  8.6 4.0 %copy-start.1 = (bf16[1024,5120]{1,0:T(8,128)(2,1)}, bf16[1024,5120]{1,0:T(8,128)(2,1)S(1)}, u32[]{:S(2)}) copy-start(bf16[1024,5120]{1,0:T(8,128)(2,1)S(1)} %hold.2.refs_1_.refs_2_) | copy-start | bytes 31457284
  12.6 3.8 %copy-start.4 = (bf16[2,1,256,1024]{3,2,1,0:T(8,128)(2,1)S(1)}, bf16[2,1,256,1024]{3,2,1,0:T(8,128)(2,1)}, u32[]{:S(2)}) copy-start(bf16[2,1,256,1024]{3,2,1,0:T(8,128)(2,1)} %own_ref.1) | copy-start | bytes 3145732
  17.4 12.3 %slice-start = ((s8[10485760]{0:T(1024)(128)(4,1)}), s8[4194304]{0:T(1024)(128)(4,1)S(1)}, s32[]{:S(2)}) async-start(s8[10485760]{0:T(1024)(128)(4,1)} %bitcast.19), calls=%async_computation | async-start | bytes 8388608
  17.4 12.3 %slice-start.1 = ((s8[10485760]{0:T(1024)(128)(4,1)}), s8[4194304]{0:T(1024)(128)(4,1)S(1)}, s32[]{:S(2)}) async-start(s8[10485760]{0:T(1024)(128)(4,1)} %bitcast.19), calls=%async_computation.1 | async-start | bytes 8388608
  21.6 8.1 %slice-start.2 = ((s8[10485760]{0:T(1024)(128)(4,1)}), s8[2097152]{0:T(1024)(128)(4,1)S(1)}, s32[]{:S(2)}) async-start(s8[10485760]{0:T(1024)(128)(4,1)} %bitcast.19), calls=%async_computation.2 | async-start | bytes 4194304
  29.0 1.6 %collective-permute-start.3 = (bf16[128,1024]{1,0:T(8,128)(2,1)S(1)}, bf16[128,1024]{1,0:T(8,128)(2,1)S(1)}, u32[]{:S(2)}, u32[]{:S(2)}) collective-permute-start(bf16[128,1024]{1,0:T(8,128)(2,1)S(1)} %attend_second.3), channel_id=1, source_target_pairs={{0,1},{1,0},{2,3},{3,2},{4,5},{5,4},{6,7},{7,6},{8,9},{9,8},{10,11... | collective-permute-start | bytes 786440 | tf_op jit(solution)/shard_map/ppermute | solution.py:186
  31.1 7.1 %collective-permute-start.4 = (bf16[64,1280]{1,0:T(8,128)(2,1)S(1)}, bf16[64,1280]{1,0:T(8,128)(2,1)S(1)}, u32[]{:S(2)}, u32[]{:S(2)}) collective-permute-start(bf16[64,1280]{1,0:T(8,128)(2,1)S(1)} %get-tuple-element.44), channel_id=1, source_target_pairs={{0,2},{2,0},{1,3},{3,1},{4,6},{6,4},{5,7},{7,5},{8,10},{10,8},{9,1... | collective-permute-start | bytes 491528 | tf_op jit(solution)/shard_map/ppermute | solution.py:186
  33.8 8.1 %collective-permute-start.6 = (bf16[64,1280]{1,0:T(8,128)(2,1)S(1)}, bf16[64,1280]{1,0:T(8,128)(2,1)S(1)}, u32[]{:S(2)}, u32[]{:S(2)}) collective-permute-start(bf16[64,1280]{1,0:T(8,128)(2,1)S(1)} %get-tuple-element.48), channel_id=1, source_target_pairs={{0,2},{2,0},{1,3},{3,1},{4,6},{6,4},{5,7},{7,5},{8,10},{10,8},{9,1... | collective-permute-start | bytes 491528 | tf_op jit(solution)/shard_map/ppermute | solution.py:186
  35.1 3.1 %copy-start.3 = (bf16[1,64,5120]{2,1,0:T(8,128)(2,1)S(1)}, bf16[1,64,5120]{2,1,0:T(8,128)(2,1)}, u32[]{:S(2)}) copy-start(bf16[1,64,5120]{2,1,0:T(8,128)(2,1)} %param.9) | copy-start | bytes 1966084
  35.1 10.2 %collective-permute-start.8 = (bf16[64,1280]{1,0:T(8,128)(2,1)S(1)}, bf16[64,1280]{1,0:T(8,128)(2,1)S(1)}, u32[]{:S(2)}, u32[]{:S(2)}) collective-permute-start(bf16[64,1280]{1,0:T(8,128)(2,1)S(1)} %get-tuple-element.50), channel_id=1, source_target_pairs={{0,2},{2,0},{1,3},{3,1},{4,6},{6,4},{5,7},{7,5},{8,10},{10,8},{9,1... | collective-permute-start | bytes 491528 | tf_op jit(solution)/shard_map/ppermute | solution.py:186
  37.8 11.1 %collective-permute-start.10 = (bf16[64,1280]{1,0:T(8,128)(2,1)S(1)}, bf16[64,1280]{1,0:T(8,128)(2,1)S(1)}, u32[]{:S(2)}, u32[]{:S(2)}) collective-permute-start(bf16[64,1280]{1,0:T(8,128)(2,1)S(1)} %get-tuple-element.52), channel_id=1, source_target_pairs={{0,2},{2,0},{1,3},{3,1},{4,6},{6,4},{5,7},{7,5},{8,10},{10,8},{9,1... | collective-permute-start | bytes 491528 | tf_op jit(solution)/shard_map/ppermute | solution.py:186
  38.3 13.4 %collective-permute-start.5 = (bf16[64,1280]{1,0:T(8,128)(2,1)S(1)}, bf16[64,1280]{1,0:T(8,128)(2,1)S(1)}, u32[]{:S(2)}, u32[]{:S(2)}) collective-permute-start(bf16[64,1280]{1,0:T(8,128)(2,1)S(1)} %combine.4), channel_id=1, source_target_pairs={{0,4},{4,8},{8,12},{12,0},{1,5},{5,9},{9,13},{13,1},{2,6},{6,10},{... | collective-permute-start | bytes 491528 | tf_op jit(solution)/shard_map/ppermute | solution.py:186
  41.9 9.7 %collective-permute-start.7 = (bf16[64,1280]{1,0:T(8,128)(2,1)S(1)}, bf16[64,1280]{1,0:T(8,128)(2,1)S(1)}, u32[]{:S(2)}, u32[]{:S(2)}) collective-permute-start(bf16[64,1280]{1,0:T(8,128)(2,1)S(1)} %combine.5), channel_id=1, source_target_pairs={{0,4},{4,8},{8,12},{12,0},{1,5},{5,9},{9,13},{13,1},{2,6},{6,10},{... | collective-permute-start | bytes 491528 | tf_op jit(solution)/shard_map/ppermute | solution.py:186
  45.4 7.6 %collective-permute-start.9 = (bf16[64,1280]{1,0:T(8,128)(2,1)S(1)}, bf16[64,1280]{1,0:T(8,128)(2,1)S(1)}, u32[]{:S(2)}, u32[]{:S(2)}) collective-permute-start(bf16[64,1280]{1,0:T(8,128)(2,1)S(1)} %combine.6), channel_id=1, source_target_pairs={{0,4},{4,8},{8,12},{12,0},{1,5},{5,9},{9,13},{13,1},{2,6},{6,10},{... | collective-permute-start | bytes 491528 | tf_op jit(solution)/shard_map/ppermute | solution.py:186
  48.9 7.2 %collective-permute-start.11 = (bf16[64,1280]{1,0:T(8,128)(2,1)S(1)}, bf16[64,1280]{1,0:T(8,128)(2,1)S(1)}, u32[]{:S(2)}, u32[]{:S(2)}) collective-permute-start(bf16[64,1280]{1,0:T(8,128)(2,1)S(1)} %combine.7), channel_id=1, source_target_pairs={{0,4},{4,8},{8,12},{12,0},{1,5},{5,9},{9,13},{13,1},{2,6},{6,10},{... | collective-permute-start | bytes 491528 | tf_op jit(solution)/shard_map/ppermute | solution.py:186

commit v6 on v5

--- a/solution.py
+++ b/solution.py
@@ -44,34 +44,55 @@
         top_ref[:, head] = top
 
 
-def halo_kernel(
-    first, last, q_ref, halo_ref, mask_ref, acc_ref, den_ref, top_ref, *outs
-):
+def halo_kernel(halos, q_first, s_first, last, *refs):
+    q_ref, refs = refs[0], refs[1:]
+    halo_refs, mask_refs, refs = refs[:halos], refs[halos : 2 * halos], refs[2 * halos :]
+    (acc_ref, den_ref, top_ref), outs = refs[:3], refs[3:]
     rows, width = outs[0].shape
-    part = slice(first, first + rows)
-    mask = mask_ref[...]
-    ones = jnp.ones((halo_ref.shape[2], HD), jnp.bfloat16)
+    q_part, s_part = slice(q_first, q_first + rows), slice(s_first, s_first + rows)
     heads = [slice(h * HD, (h + 1) * HD) for h in range(width // HD)]
-    scores = [scores_of(q_ref[part, head], halo_ref[0, 0, :, head]) + mask for head in heads]
-    peaks = [jnp.max(s, axis=1, keepdims=True) for s in scores]
-    probs, fades = [], []
-    for head, s, peak in zip(heads, scores, peaks):
-        before = top_ref[part, head]
-        top = jnp.maximum(before, jnp.broadcast_to(peak, before.shape))
-        probs.append(exponentials(s, top))
-        fades.append(jnp.exp2((before - top) * FACTOR))
-        if not last:
-            outs[2][:, head] = top
-    for head, p, fade in zip(heads, probs, fades):
-        values = jnp.concatenate([halo_ref[1, 0, :, head], ones], axis=1)
-        both = jnp.dot(p, values, preferred_element_type=jnp.float32)
-        weighted = acc_ref[part, head] * fade + both[:, :HD]
-        total = den_ref[part, head] * fade + both[:, HD:]
-        if last:
-            outs[0][:, head] = (weighted / total).astype(outs[0].dtype)
-        else:
-            outs[0][:, head] = weighted
-            outs[1][:, head] = total
+    masks = [mask_ref[...] for mask_ref in mask_refs]
+
+    def visit():
+        ones = jnp.ones((halos * halo_refs[0].shape[2], HD), jnp.bfloat16)
+        scores = []
+        for head in heads:
+            q = q_ref[q_part, head]
+            pieces = [scores_of(q, k[0, 0, :, head]) + m for k, m in zip(halo_refs, masks)]
+            scores.append(jnp.concatenate(pieces, axis=1))
+        peaks = [jnp.max(s, axis=1, keepdims=True) for s in scores]
+        probs, fades = [], []
+        for head, s, peak in zip(heads, scores, peaks):
+            before = top_ref[s_part, head]
+            top = jnp.maximum(before, jnp.broadcast_to(peak, before.shape))
+            probs.append(exponentials(s, top))
+            fades.append(jnp.exp2((before - top) * FACTOR))
+            if not last:
+                outs[2][:, head] = top
+        for head, p, fade in zip(heads, probs, fades):
+            values = jnp.concatenate([v[1, 0, :, head] for v in halo_refs], axis=0)
+            values = jnp.concatenate([values, ones], axis=1)
+            both = jnp.dot(p, values, preferred_element_type=jnp.float32)
+            weighted = acc_ref[s_part, head] * fade + both[:, :HD]
+            total = den_ref[s_part, head] * fade + both[:, HD:]
+            if last:
+                outs[0][:, head] = (weighted / total).astype(outs[0].dtype)
+            else:
+                outs[0][:, head] = weighted
+                outs[1][:, head] = total
+
+    if not (last and halos == 1):
+        visit()
+        return
+    anything = jnp.max(masks[0]) == 0.0
+    pl.when(anything)(visit)
+
+    @pl.when(jnp.logical_not(anything))
+    def _():
+        for head in heads:
+            outs[0][:, head] = (acc_ref[s_part, head] / den_ref[s_part, head]).astype(
+                outs[0].dtype
+            )
 
 
 VMEM_SPEC = pl.BlockSpec(memory_space=pltpu.VMEM)
@@ -224,20 +245,30 @@
     flops = 4 * span_tok * span_tok * width
     state = attend(own_kernel, "attend_own", (wide,) * 3, flops, own_queries, keys_values)
     state, weights, gate_row = lax.optimization_barrier((state, weights, gate_row))
-    kernel = functools.partial(halo_kernel, 0, False)
-    state = attend(
-        kernel, "attend_first", (wide,) * 3, flops, own_queries, first_halo, first_mask, *state
-    )
     per_core = spans * rows
+    some = jax.ShapeDtypeStruct((per_core, width), jnp.float32)
     out_shape = (jax.ShapeDtypeStruct((per_core, width), jnp.bfloat16),)
     att = []
-    for l in range(cores - 1, -1, -1):
-        kernel = functools.partial(halo_kernel, (cores - 1 - l) * per_core, True)
+    for l in range(cores - 1, 0, -1):
+        start = (cores - 1 - l) * per_core
+        kernel = functools.partial(halo_kernel, 1, start, start, False)
+        part = attend(
+            kernel, "attend_first", (some,) * 3, flops // cores,
+            own_queries, first_halo, first_mask, *state,
+        )
+        kernel = functools.partial(halo_kernel, 1, start, 0, True)
         (out,) = attend(
             kernel, "attend_second", out_shape, flops // cores,
-            own_queries, second_halo, second_mask, *state,
+            own_queries, second_halo, second_mask, *part,
         )
-        att.insert(0, out if l == 0 else rotate(out, "mp", l))
+        att.insert(0, rotate(out, "mp", l))
+    start = (cores - 1) * per_core
+    kernel = functools.partial(halo_kernel, 2, start, start, True)
+    (out,) = attend(
+        kernel, "attend_both", out_shape, 2 * flops // cores,
+        own_queries, first_halo, second_halo, first_mask, second_mask, *state,
+    )
+    att.insert(0, out)
 
     columns = latents.shape[2] // CHUNKS
     updates = []

time: 57 us -> 57.1 us (level)
  starting transfers between devices: 21.3 us -> 22.8 us
    ppermute x10, starting transfers between devices: 18 us -> 19.4 us  [rotate(): lax.ppermute(value, axis, [(i, (i + steps) % count) for i in range(count)])]
    ppermute x10, waiting for transfers between devices: 3.92 us -> 3.26 us  [rotate(): lax.ppermute(value, axis, [(i, (i + steps) % count) for i in range(count)])]
  transfers between devices with their start and end apart: 12 -> 12, of which waited for: 4 -> 3; matrix products, arithmetic and copies ran while one was open for 5% -> 5% of each run, Pallas kernels for 20% -> 19%
where the time goes in v6:
time: 57.1 us; the launch traced here: 57.2 us
  starting transfers between devices  22.8 us (40%)
  Pallas kernels  11.9 us (21%)
  local copies, waits for them, and re-layouts  10.4 us (18%)
  waiting for transfers between devices  8.93 us (16%)
  between operations  2.21 us (4%)
  other arithmetic  0.94 us (2%)
    ppermute x10, starting transfers between devices, rotate(): lax.ppermute(value, axis, [(i, (i + steps) % count) for i in range(count)])  19.4 us
    unnamed x18, local copies, waits for them, and re-layouts  8 us
    ppermute x2, waiting for transfers between devices, shards(): lax.ppermute(keys_values, 'section', pairs)  5.66 us
    pallas_call x2, Pallas kernels, hold(): pl.pallas_call(hold_kernel, out_shape=jax.ShapeDtypeStruct(array.shape, a...  4.84 us
    pallas_call x5, Pallas kernels, project(): pl.pallas_call(functools.partial(project_kernel, parts, rows, first, len(...  3.8 us
    ppermute x2, starting transfers between devices, shards(): lax.ppermute(keys_values, 'section', pairs)  3.36 us
    ppermute x10, waiting for transfers between devices, rotate(): lax.ppermute(value, axis, [(i, (i + steps) % count) for i in range(count)])  3.26 us
    pallas_call x4, Pallas kernels, attend(): pl.pallas_call(kernel, out_shape=out_shape, in_specs=[VMEM_SPEC] * len(op...  2.95 us
  transfers between devices with their start and end apart: 12, of which 3 were waited for; matrix products, arithmetic and copies ran while one was open for 5% of the time, Pallas kernels for 19%

profile of v6, /device:TPU:0, one launch (start us, length us, event | category | flops | bytes accessed | tf_op | source)
XLA Modules:
  0.0 57.2 jit_solution(4793481785133329368)
XLA Ops:
  0.0 0.5 collective-permute-start
  0.5 2.6 %collective-permute-start.1 = (bf16[2,1,256,1024]{3,2,1,0:T(8,128)(2,1)}, bf16[2,1,256,1024]{3,2,1,0:T(8,128)(2,1)S(1)}, u32[]{:S(2)}, u32[]{:S(2)}) collective-permute-start(bf16[2,1,256,1024]{3,2,1,0:T(8,128)(2,1)} %own_ref.1), channel_id=1, source_target_pairs={{0,4},{4,0},{8,12},{12,8},{1,5},{5,1},{9,13},{13,9},{2,6},{6,2},{1... | collective-permute-start | bytes 3145736 | tf_op jit(solution)/shard_map/ppermute | solution.py:223
  3.1 0.7 %collective-permute-start.2 = (bf16[2,1,256,1024]{3,2,1,0:T(8,128)(2,1)}, bf16[2,1,256,1024]{3,2,1,0:T(8,128)(2,1)S(1)}, u32[]{:S(2)}, u32[]{:S(2)}) collective-permute-start(bf16[2,1,256,1024]{3,2,1,0:T(8,128)(2,1)} %own_ref.1), channel_id=1, source_target_pairs={{4,8},{8,4},{5,9},{9,5},{6,10},{10,6},{7,11},{11,7},{20,24},{24,20... | collective-permute-start | bytes 3145736 | tf_op jit(solution)/shard_map/ppermute | solution.py:223
  3.9 4.0 %copy-done.2 = bf16[1024,5120]{1,0:T(8,128)(2,1)S(1)} copy-done((bf16[1024,5120]{1,0:T(8,128)(2,1)S(1)}, bf16[1024,5120]{1,0:T(8,128)(2,1)}, u32[]{:S(2)}) %copy-start.2) | copy-done | bytes 10485784
  7.9 0.7 %hold.2.refs_1_.refs_2_ = bf16[1024,5120]{1,0:T(8,128)(2,1)S(1)} custom-call(bf16[1024,5120]{1,0:T(8,128)(2,1)S(1)} %copy-done.2), custom_call_target="tpu_custom_call" | custom-call | bytes 1024 | tf_op jit(solution)/shard_map/hold/pallas_call | solution.py:124
  8.6 4.0 %copy-done.1 = bf16[1024,5120]{1,0:T(8,128)(2,1)} copy-done((bf16[1024,5120]{1,0:T(8,128)(2,1)}, bf16[1024,5120]{1,0:T(8,128)(2,1)S(1)}, u32[]{:S(2)}) %copy-start.1) | copy-done | bytes 10485784
  13.4 0.6 %fusion.5 = (s32[1]{0:T(128)}, s32[1]{0:T(128)}) fusion(s32[3]{0:T(128)S(1)} %copy-done.5, s32[]{:T(128)S(6)} %min.7, s32[]{:T(128)S(6)} %min.8), kind=kLoop, calls=%fused_computation.15 | loop fusion | bytes 24 | tf_op jit(solution)/shard_map/dynamic_slice | solution.py:217
  15.1 1.1 %dynamic-slice_bitcast_fusion.3 = (bf16[64,1024]{1,0:T(8,128)(2,1)S(1)}, bf16[64,1024]{1,0:T(8,128)(2,1)S(1)}, bf16[64,1024]{1,0:T(8,128)(2,1)S(1)}, bf16[64,1024]{1,0:T(8,128)(2,1)S(1)}) fusion(bf16[4,64,1024]{2,1,0:T(8,128)(2,1)} %bitcast.26, s32[]{:T(128)S(6)} %select_n.93, s32[]{:T(128)S(6)} %select_n.98, s32[]{:T(128)S(6)} %select_n.97, s32[]{:T(128)S(6)} %select_n.95), kind=kLoop, calls=%fused_computation.11 | loop fusion | bytes 1048592 | tf_op jit(solution)/shard_map/jit(dynamic_index_in_dim)/squeeze | solution.py:234
  16.3 0.9 %attend_own.1 = (f32[256,1024]{1,0:T(8,128)S(1)}, f32[256,1024]{1,0:T(8,128)S(1)}, f32[256,1024]{1,0:T(8,128)S(1)}) custom-call(bf16[256,1024]{1,0:T(8,128)(2,1)S(1)} %pad_maximum_fusion.q_ref.refs_0_, bf16[2,1,256,1024]{3,2,1,0:T(8,128)(2,1)S(1)} %copy-done.4), custom_call_target="tpu_custom_call" | custom-call | flops 268435456 | bytes 1572864 | tf_op jit(solution)/shard_map/attend_own/pallas_call | solution.py:102
  17.3 4.1 %hold.3.refs_1_.refs_3_ = bf16[1024,5120]{1,0:T(8,128)(2,1)S(1)} custom-call(bf16[1024,5120]{1,0:T(8,128)(2,1)} %collective-permute-done.src_ref), custom_call_target="tpu_custom_call" | custom-call | bytes 1024 | tf_op jit(solution)/shard_map/hold/pallas_call | solution.py:124
  21.4 5.7 %collective-permute-done.1.refs_1_ = bf16[2,1,256,1024]{3,2,1,0:T(8,128)(2,1)S(1)} collective-permute-done((bf16[2,1,256,1024]{3,2,1,0:T(8,128)(2,1)}, bf16[2,1,256,1024]{3,2,1,0:T(8,128)(2,1)S(1)}, u32[]{:S(2)}, u32[]{:S(2)}) %collective-permute-start.1) | collective-permute-done | bytes 1048608 | tf_op jit(solution)/shard_map/ppermute | solution.py:223
  27.1 0.7 %attend_first.1 = (f32[128,1024]{1,0:T(8,128)S(1)}, f32[128,1024]{1,0:T(8,128)S(1)}, f32[128,1024]{1,0:T(8,128)S(1)}) custom-call(bf16[256,1024]{1,0:T(8,128)(2,1)S(1)} %pad_maximum_fusion.q_ref.refs_0_, bf16[2,1,256,1024]{3,2,1,0:T(8,128)(2,1)S(1)} %collective-permute-done.1.refs_1_, f32[1,256]{1,0:T(1,128)S(1)} %get-tuple-element.62.refs_3_.refs_2_, ...), custom_call_target="tpu_custom_call" | custom-call | flops 134217728 | bytes 4719616 | tf_op jit(solution)/shard_map/attend_first/pallas_call | solution.py:102
  27.7 0.2 attend_second.1
  28.0 0.1 collective-permute-start.3
  28.0 1.2 %attend_both.1.refs_0_ = bf16[128,1024]{1,0:T(8,128)(2,1)S(1)} custom-call(bf16[256,1024]{1,0:T(8,128)(2,1)S(1)} %pad_maximum_fusion.q_ref.refs_0_, bf16[2,1,256,1024]{3,2,1,0:T(8,128)(2,1)S(1)} %collective-permute-done.1.refs_1_, bf16[2,1,256,1024]{3,2,1,0:T(8,128)(2,1)S(1)} %collective-permute-done.2.refs_2_.refs_1_, ...), custom_call_target="tpu_custom_call" | custom-call | flops 268435456 | bytes 5769216 | tf_op jit(solution)/shard_map/attend_both/pallas_call | solution.py:102
  29.3 0.5 project.5.refs_2_
  29.8 0.6 project.6
  30.4 1.7 %collective-permute-start.4 = (bf16[64,1280]{1,0:T(8,128)(2,1)S(1)}, bf16[64,1280]{1,0:T(8,128)(2,1)S(1)}, u32[]{:S(2)}, u32[]{:S(2)}) collective-permute-start(bf16[64,1280]{1,0:T(8,128)(2,1)S(1)} %get-tuple-element.44), channel_id=1, source_target_pairs={{0,2},{2,0},{1,3},{3,1},{4,6},{6,4},{5,7},{7,5},{8,10},{10,8},{9,1... | collective-permute-start | bytes 491528 | tf_op jit(solution)/shard_map/ppermute | solution.py:207
  32.1 0.9 %project.7 = (bf16[64,1280]{1,0:T(8,128)(2,1)S(1)}, f32[64,1280]{1,0:T(8,128)S(1)}) custom-call(bf16[128,1024]{1,0:T(8,128)(2,1)S(1)} %attend_both.1.refs_0_, bf16[128,1024]{1,0:T(8,128)(2,1)S(1)} %collective-permute-done.3.refs_0_.refs_1_, bf16[1024,5120]{1,0:T(8,128)(2,1)S(1)} %bitcast.20, bf16[1024,5120]{1,0:T(8,128)(2,1)S(1)} %hold.3.refs_1_.refs_3_), custom_call_target="tpu_custom_call" | custom-call | flops 671088640 | bytes 5242880 | tf_op jit(solution)/shard_map/project/pallas_call | solution.py:164
  33.0 0.4 collective-permute-start.6
  33.5 0.9 %project.8 = (bf16[64,1280]{1,0:T(8,128)(2,1)S(1)}, f32[64,1280]{1,0:T(8,128)S(1)}) custom-call(bf16[128,1024]{1,0:T(8,128)(2,1)S(1)} %attend_both.1.refs_0_, bf16[128,1024]{1,0:T(8,128)(2,1)S(1)} %collective-permute-done.3.refs_0_.refs_1_, bf16[1024,5120]{1,0:T(8,128)(2,1)S(1)} %bitcast.20, bf16[1024,5120]{1,0:T(8,128)(2,1)S(1)} %hold.3.refs_1_.refs_3_), custom_call_target="tpu_custom_call" | custom-call | flops 671088640 | bytes 5242880 | tf_op jit(solution)/shard_map/project/pallas_call | solution.py:164
  34.4 1.7 %collective-permute-start.8 = (bf16[64,1280]{1,0:T(8,128)(2,1)S(1)}, bf16[64,1280]{1,0:T(8,128)(2,1)S(1)}, u32[]{:S(2)}, u32[]{:S(2)}) collective-permute-start(bf16[64,1280]{1,0:T(8,128)(2,1)S(1)} %get-tuple-element.50), channel_id=1, source_target_pairs={{0,2},{2,0},{1,3},{3,1},{4,6},{6,4},{5,7},{7,5},{8,10},{10,8},{9,1... | collective-permute-start | bytes 491528 | tf_op jit(solution)/shard_map/ppermute | solution.py:207
  36.1 0.9 %project.9 = (bf16[64,1280]{1,0:T(8,128)(2,1)S(1)}, f32[64,1280]{1,0:T(8,128)S(1)}) custom-call(bf16[128,1024]{1,0:T(8,128)(2,1)S(1)} %attend_both.1.refs_0_, bf16[128,1024]{1,0:T(8,128)(2,1)S(1)} %collective-permute-done.3.refs_0_.refs_1_, bf16[1024,5120]{1,0:T(8,128)(2,1)S(1)} %bitcast.20, bf16[1024,5120]{1,0:T(8,128)(2,1)S(1)} %hold.3.refs_1_.refs_3_), custom_call_target="tpu_custom_call" | custom-call | flops 671088640 | bytes 5242880 | tf_op jit(solution)/shard_map/project/pallas_call | solution.py:164
  37.0 0.4 collective-permute-start.10
  37.5 4.7 %collective-permute-start.5 = (bf16[64,1280]{1,0:T(8,128)(2,1)S(1)}, bf16[64,1280]{1,0:T(8,128)(2,1)S(1)}, u32[]{:S(2)}, u32[]{:S(2)}) collective-permute-start(bf16[64,1280]{1,0:T(8,128)(2,1)S(1)} %combine.4), channel_id=1, source_target_pairs={{0,4},{4,8},{8,12},{12,0},{1,5},{5,9},{9,13},{13,1},{2,6},{6,10},{... | collective-permute-start | bytes 491528 | tf_op jit(solution)/shard_map/ppermute | solution.py:207
  42.3 3.4 %collective-permute-start.7 = (bf16[64,1280]{1,0:T(8,128)(2,1)S(1)}, bf16[64,1280]{1,0:T(8,128)(2,1)S(1)}, u32[]{:S(2)}, u32[]{:S(2)}) collective-permute-start(bf16[64,1280]{1,0:T(8,128)(2,1)S(1)} %combine.5), channel_id=1, source_target_pairs={{0,4},{4,8},{8,12},{12,0},{1,5},{5,9},{9,13},{13,1},{2,6},{6,10},{... | collective-permute-start | bytes 491528 | tf_op jit(solution)/shard_map/ppermute | solution.py:207
  45.8 3.4 %collective-permute-start.9 = (bf16[64,1280]{1,0:T(8,128)(2,1)S(1)}, bf16[64,1280]{1,0:T(8,128)(2,1)S(1)}, u32[]{:S(2)}, u32[]{:S(2)}) collective-permute-start(bf16[64,1280]{1,0:T(8,128)(2,1)S(1)} %combine.6), channel_id=1, source_target_pairs={{0,4},{4,8},{8,12},{12,0},{1,5},{5,9},{9,13},{13,1},{2,6},{6,10},{... | collective-permute-start | bytes 491528 | tf_op jit(solution)/shard_map/ppermute | solution.py:207
  49.3 3.0 %collective-permute-start.11 = (bf16[64,1280]{1,0:T(8,128)(2,1)S(1)}, bf16[64,1280]{1,0:T(8,128)(2,1)S(1)}, u32[]{:S(2)}, u32[]{:S(2)}) collective-permute-start(bf16[64,1280]{1,0:T(8,128)(2,1)S(1)} %combine.7), channel_id=1, source_target_pairs={{0,4},{4,8},{8,12},{12,0},{1,5},{5,9},{9,13},{13,1},{2,6},{6,10},{... | collective-permute-start | bytes 491528 | tf_op jit(solution)/shard_map/ppermute | solution.py:207
  52.4 0.7 %collective-permute-done.9 = bf16[64,1280]{1,0:T(8,128)(2,1)S(1)} collective-permute-done((bf16[64,1280]{1,0:T(8,128)(2,1)S(1)}, bf16[64,1280]{1,0:T(8,128)(2,1)S(1)}, u32[]{:S(2)}, u32[]{:S(2)}) %collective-permute-start.9) | collective-permute-done | bytes 163872 | tf_op jit(solution)/shard_map/ppermute | solution.py:207
  53.1 0.9 %fusion.4 = bf16[64,5120]{1,0:T(8,128)(2,1)} fusion(bf16[64,1280]{1,0:T(8,128)(2,1)S(1)} %collective-permute-done.9, bf16[64,1280]{1,0:T(8,128)(2,1)S(1)} %collective-permute-done.7, bf16[64,1280]{1,0:T(8,128)(2,1)S(1)} %collective-permute-done.5), kind=kLoop, calls=%fused_computation.5 | loop fusion | flops 3276800 | bytes 1146880 | tf_op jit(solution)/shard_map/concatenate | solution.py:286
  54.0 2.5 %collective-permute-done.11 = bf16[64,1280]{1,0:T(8,128)(2,1)S(1)} collective-permute-done((bf16[64,1280]{1,0:T(8,128)(2,1)S(1)}, bf16[64,1280]{1,0:T(8,128)(2,1)S(1)}, u32[]{:S(2)}, u32[]{:S(2)}) %collective-permute-start.11) | collective-permute-done | bytes 163872 | tf_op jit(solution)/shard_map/ppermute | solution.py:207
  56.5 0.7 %bitcast_dynamic-update-slice_fusion = bf16[1,64,5120]{2,1,0:T(8,128)(2,1)} fusion(bf16[1,64,5120]{2,1,0:T(8,128)(2,1)} %bitcast.25, bf16[64,1280]{1,0:T(8,128)(2,1)S(1)} %collective-permute-done.11), kind=kLoop, calls=%fused_computation.7 | loop fusion | bytes 327680 | tf_op jit(solution)/shard_map/dynamic_update_slice | solution.py:288
  (33 shorter events, 0.4 us)
Async XLA Ops:
  0.0 17.2 %copy-start = (f32[8,5120]{1,0:T(8,128)S(1)}, f32[8,5120]{1,0:T(8,128)}, u32[]{:S(2)}) copy-start(f32[8,5120]{1,0:T(8,128)} %param.11) | copy-start | bytes 491524
  0.0 17.2 %collective-permute-start = (bf16[1024,5120]{1,0:T(8,128)(2,1)}, bf16[1024,5120]{1,0:T(8,128)(2,1)}, u32[]{:S(2)}, u32[]{:S(2)}) collective-permute-start(bf16[1024,5120]{1,0:T(8,128)(2,1)} %src_ref.1), channel_id=1, source_target_pairs={{0,1},{1,0},{2,3},{3,2},{4,5},{5,4},{6,7},{7,6},{8,9},{9,8},{10,11... | collective-permute-start | bytes 31457288 | tf_op jit(solution)/shard_map/ppermute | solution.py:207
  0.5 26.6 %collective-permute-start.1 = (bf16[2,1,256,1024]{3,2,1,0:T(8,128)(2,1)}, bf16[2,1,256,1024]{3,2,1,0:T(8,128)(2,1)S(1)}, u32[]{:S(2)}, u32[]{:S(2)}) collective-permute-start(bf16[2,1,256,1024]{3,2,1,0:T(8,128)(2,1)} %own_ref.1), channel_id=1, source_target_pairs={{0,4},{4,0},{8,12},{12,8},{1,5},{5,1},{9,13},{13,9},{2,6},{6,2},{1... | collective-permute-start | bytes 3145736 | tf_op jit(solution)/shard_map/ppermute | solution.py:223
  3.1 24.6 %collective-permute-start.2 = (bf16[2,1,256,1024]{3,2,1,0:T(8,128)(2,1)}, bf16[2,1,256,1024]{3,2,1,0:T(8,128)(2,1)S(1)}, u32[]{:S(2)}, u32[]{:S(2)}) collective-permute-start(bf16[2,1,256,1024]{3,2,1,0:T(8,128)(2,1)} %own_ref.1), channel_id=1, source_target_pairs={{4,8},{8,4},{5,9},{9,5},{6,10},{10,6},{7,11},{11,7},{20,24},{24,20... | collective-permute-start | bytes 3145736 | tf_op jit(solution)/shard_map/ppermute | solution.py:223
  3.9 4.0 %copy-start.2 = (bf16[1024,5120]{1,0:T(8,128)(2,1)S(1)}, bf16[1024,5120]{1,0:T(8,128)(2,1)}, u32[]{:S(2)}) copy-start(bf16[1024,5120]{1,0:T(8,128)(2,1)} %src_ref.1) | copy-start | bytes 31457284
  7.8 5.5 %copy-start.5 = (s32[3]{0:T(128)S(1)}, s32[3]{0:T(128)}, u32[]{:S(2)}) copy-start(s32[3]{0:T(128)} %param.13) | copy-start | bytes 40
  8.6 4.0 %copy-start.1 = (bf16[1024,5120]{1,0:T(8,128)(2,1)}, bf16[1024,5120]{1,0:T(8,128)(2,1)S(1)}, u32[]{:S(2)}) copy-start(bf16[1024,5120]{1,0:T(8,128)(2,1)S(1)} %hold.2.refs_1_.refs_2_) | copy-start | bytes 31457284
  12.6 3.7 %copy-start.4 = (bf16[2,1,256,1024]{3,2,1,0:T(8,128)(2,1)S(1)}, bf16[2,1,256,1024]{3,2,1,0:T(8,128)(2,1)}, u32[]{:S(2)}) copy-start(bf16[2,1,256,1024]{3,2,1,0:T(8,128)(2,1)} %own_ref.1) | copy-start | bytes 3145732
  17.2 12.0 %slice-start = ((s8[10485760]{0:T(1024)(128)(4,1)}), s8[4194304]{0:T(1024)(128)(4,1)S(1)}, s32[]{:S(2)}) async-start(s8[10485760]{0:T(1024)(128)(4,1)} %bitcast.19), calls=%async_computation | async-start | bytes 8388608
  17.3 12.0 %slice-start.1 = ((s8[10485760]{0:T(1024)(128)(4,1)}), s8[4194304]{0:T(1024)(128)(4,1)S(1)}, s32[]{:S(2)}) async-start(s8[10485760]{0:T(1024)(128)(4,1)} %bitcast.19), calls=%async_computation.1 | async-start | bytes 8388608
  27.1 2.2 %slice-start.2 = ((s8[10485760]{0:T(1024)(128)(4,1)}), s8[2097152]{0:T(1024)(128)(4,1)S(1)}, s32[]{:S(2)}) async-start(s8[10485760]{0:T(1024)(128)(4,1)} %bitcast.19), calls=%async_computation.2 | async-start | bytes 4194304
  28.0 1.9 %collective-permute-start.3 = (bf16[128,1024]{1,0:T(8,128)(2,1)S(1)}, bf16[128,1024]{1,0:T(8,128)(2,1)S(1)}, u32[]{:S(2)}, u32[]{:S(2)}) collective-permute-start(bf16[128,1024]{1,0:T(8,128)(2,1)S(1)} %attend_second.1), channel_id=1, source_target_pairs={{0,1},{1,0},{2,3},{3,2},{4,5},{5,4},{6,7},{7,6},{8,9},{9,8},{10,11... | collective-permute-start | bytes 786440 | tf_op jit(solution)/shard_map/ppermute | solution.py:207
  30.4 7.1 %collective-permute-start.4 = (bf16[64,1280]{1,0:T(8,128)(2,1)S(1)}, bf16[64,1280]{1,0:T(8,128)(2,1)S(1)}, u32[]{:S(2)}, u32[]{:S(2)}) collective-permute-start(bf16[64,1280]{1,0:T(8,128)(2,1)S(1)} %get-tuple-element.44), channel_id=1, source_target_pairs={{0,2},{2,0},{1,3},{3,1},{4,6},{6,4},{5,7},{7,5},{8,10},{10,8},{9,1... | collective-permute-start | bytes 491528 | tf_op jit(solution)/shard_map/ppermute | solution.py:207
  33.0 9.2 %collective-permute-start.6 = (bf16[64,1280]{1,0:T(8,128)(2,1)S(1)}, bf16[64,1280]{1,0:T(8,128)(2,1)S(1)}, u32[]{:S(2)}, u32[]{:S(2)}) collective-permute-start(bf16[64,1280]{1,0:T(8,128)(2,1)S(1)} %get-tuple-element.48), channel_id=1, source_target_pairs={{0,2},{2,0},{1,3},{3,1},{4,6},{6,4},{5,7},{7,5},{8,10},{10,8},{9,1... | collective-permute-start | bytes 491528 | tf_op jit(solution)/shard_map/ppermute | solution.py:207
  34.4 3.1 %copy-start.3 = (bf16[1,64,5120]{2,1,0:T(8,128)(2,1)S(1)}, bf16[1,64,5120]{2,1,0:T(8,128)(2,1)}, u32[]{:S(2)}) copy-start(bf16[1,64,5120]{2,1,0:T(8,128)(2,1)} %param.9) | copy-start | bytes 1966084
  34.4 11.3 %collective-permute-start.8 = (bf16[64,1280]{1,0:T(8,128)(2,1)S(1)}, bf16[64,1280]{1,0:T(8,128)(2,1)S(1)}, u32[]{:S(2)}, u32[]{:S(2)}) collective-permute-start(bf16[64,1280]{1,0:T(8,128)(2,1)S(1)} %get-tuple-element.50), channel_id=1, source_target_pairs={{0,2},{2,0},{1,3},{3,1},{4,6},{6,4},{5,7},{7,5},{8,10},{10,8},{9,1... | collective-permute-start | bytes 491528 | tf_op jit(solution)/shard_map/ppermute | solution.py:207
  37.0 12.2 %collective-permute-start.10 = (bf16[64,1280]{1,0:T(8,128)(2,1)S(1)}, bf16[64,1280]{1,0:T(8,128)(2,1)S(1)}, u32[]{:S(2)}, u32[]{:S(2)}) collective-permute-start(bf16[64,1280]{1,0:T(8,128)(2,1)S(1)} %get-tuple-element.52), channel_id=1, source_target_pairs={{0,2},{2,0},{1,3},{3,1},{4,6},{6,4},{5,7},{7,5},{8,10},{10,8},{9,1... | collective-permute-start | bytes 491528 | tf_op jit(solution)/shard_map/ppermute | solution.py:207
  37.5 14.8 %collective-permute-start.5 = (bf16[64,1280]{1,0:T(8,128)(2,1)S(1)}, bf16[64,1280]{1,0:T(8,128)(2,1)S(1)}, u32[]{:S(2)}, u32[]{:S(2)}) collective-permute-start(bf16[64,1280]{1,0:T(8,128)(2,1)S(1)} %combine.4), channel_id=1, source_target_pairs={{0,4},{4,8},{8,12},{12,0},{1,5},{5,9},{9,13},{13,1},{2,6},{6,10},{... | collective-permute-start | bytes 491528 | tf_op jit(solution)/shard_map/ppermute | solution.py:207
  42.3 10.1 %collective-permute-start.7 = (bf16[64,1280]{1,0:T(8,128)(2,1)S(1)}, bf16[64,1280]{1,0:T(8,128)(2,1)S(1)}, u32[]{:S(2)}, u32[]{:S(2)}) collective-permute-start(bf16[64,1280]{1,0:T(8,128)(2,1)S(1)} %combine.5), channel_id=1, source_target_pairs={{0,4},{4,8},{8,12},{12,0},{1,5},{5,9},{9,13},{13,1},{2,6},{6,10},{... | collective-permute-start | bytes 491528 | tf_op jit(solution)/shard_map/ppermute | solution.py:207
  45.8 7.3 %collective-permute-start.9 = (bf16[64,1280]{1,0:T(8,128)(2,1)S(1)}, bf16[64,1280]{1,0:T(8,128)(2,1)S(1)}, u32[]{:S(2)}, u32[]{:S(2)}) collective-permute-start(bf16[64,1280]{1,0:T(8,128)(2,1)S(1)} %combine.6), channel_id=1, source_target_pairs={{0,4},{4,8},{8,12},{12,0},{1,5},{5,9},{9,13},{13,1},{2,6},{6,10},{... | collective-permute-start | bytes 491528 | tf_op jit(solution)/shard_map/ppermute | solution.py:207
  49.3 7.2 %collective-permute-start.11 = (bf16[64,1280]{1,0:T(8,128)(2,1)S(1)}, bf16[64,1280]{1,0:T(8,128)(2,1)S(1)}, u32[]{:S(2)}, u32[]{:S(2)}) collective-permute-start(bf16[64,1280]{1,0:T(8,128)(2,1)S(1)} %combine.7), channel_id=1, source_target_pairs={{0,4},{4,8},{8,12},{12,0},{1,5},{5,9},{9,13},{13,1},{2,6},{6,10},{... | collective-permute-start | bytes 491528 | tf_op jit(solution)/shard_map/ppermute | solution.py:207

commit v7 on v5

--- a/solution.py
+++ b/solution.py
@@ -241,6 +241,7 @@
 
     columns = latents.shape[2] // CHUNKS
     updates = []
+    sends, keeps = [], []
     for c in range(CHUNKS):
         first = c * columns
         if c == 0:
@@ -249,8 +250,12 @@
             att, keep = lax.optimization_barrier((att, keep))
         else:
             *send, keep = project(att, weights, None, rows, first, columns, True)
+        sends.append(send)
+        keeps.append(keep)
+    sends[1], keeps[2] = lax.optimization_barrier((sends[1], keeps[2]))
+    for c, (send, keep) in enumerate(zip(sends, keeps)):
         others = [rotate(send[spans - 1 - k], "span", k) for k in range(1, spans)]
-        updates.append(combine(own_latents, gate_row, keep, others, first))
+        updates.append(combine(own_latents, gate_row, keep, others, c * columns))
     pieces = [rotate(update, "section", 1) for update in updates]
     early = jnp.pad(jnp.concatenate(pieces[:-1], axis=1), ((0, 0), (0, columns)))
     early, late = lax.optimization_barrier((early, pieces[-1]))

time: 57 us -> 57 us (level)
  transfers between devices with their start and end apart: 12 -> 12, of which waited for: 4 -> 6; matrix products, arithmetic and copies ran while one was open for 5% -> 5% of each run, Pallas kernels for 20% -> 20%
where the time goes in v7:
time: 57 us; the launch traced here: 56.8 us
  starting transfers between devices  21.2 us (37%)
  Pallas kernels  12.3 us (22%)
  local copies, waits for them, and re-layouts  10.5 us (18%)
  waiting for transfers between devices  9.5 us (17%)
  between operations  2.28 us (4%)
  other arithmetic  0.94 us (2%)
    ppermute x10, starting transfers between devices, rotate(): lax.ppermute(value, axis, [(i, (i + steps) % count) for i in range(count)])  17.9 us
    unnamed x18, local copies, waits for them, and re-layouts  8.01 us
    ppermute x2, waiting for transfers between devices, shards(): lax.ppermute(keys_values, 'section', pairs)  5.5 us
    pallas_call x2, Pallas kernels, hold(): pl.pallas_call(hold_kernel, out_shape=jax.ShapeDtypeStruct(array.shape, a...  4.84 us
    ppermute x10, waiting for transfers between devices, rotate(): lax.ppermute(value, axis, [(i, (i + steps) % count) for i in range(count)])  4 us
    pallas_call x5, Pallas kernels, project(): pl.pallas_call(functools.partial(project_kernel, parts, rows, first, len(...  3.82 us
    pallas_call x4, Pallas kernels, attend(): pl.pallas_call(kernel, out_shape=out_shape, in_specs=[VMEM_SPEC] * len(op...  3.38 us
    ppermute x2, starting transfers between devices, shards(): lax.ppermute(keys_values, 'section', pairs)  3.36 us
  transfers between devices with their start and end apart: 12, of which 6 were waited for; matrix products, arithmetic and copies ran while one was open for 5% of the time, Pallas kernels for 20%

profile of v7, /device:TPU:0, one launch (start us, length us, event | category | flops | bytes accessed | tf_op | source)
XLA Modules:
  0.0 56.8 jit_solution(17289230668545178566)
XLA Ops:
  0.0 0.5 collective-permute-start
  0.5 2.6 %collective-permute-start.2 = (bf16[2,1,256,1024]{3,2,1,0:T(8,128)(2,1)}, bf16[2,1,256,1024]{3,2,1,0:T(8,128)(2,1)S(1)}, u32[]{:S(2)}, u32[]{:S(2)}) collective-permute-start(bf16[2,1,256,1024]{3,2,1,0:T(8,128)(2,1)} %own_ref.1), channel_id=1, source_target_pairs={{0,4},{4,0},{8,12},{12,8},{1,5},{5,1},{9,13},{13,9},{2,6},{6,2},{1... | collective-permute-start | bytes 3145736 | tf_op jit(solution)/shard_map/ppermute | solution.py:202
  3.1 0.7 %collective-permute-start.1 = (bf16[2,1,256,1024]{3,2,1,0:T(8,128)(2,1)}, bf16[2,1,256,1024]{3,2,1,0:T(8,128)(2,1)S(1)}, u32[]{:S(2)}, u32[]{:S(2)}) collective-permute-start(bf16[2,1,256,1024]{3,2,1,0:T(8,128)(2,1)} %own_ref.1), channel_id=1, source_target_pairs={{4,8},{8,4},{5,9},{9,5},{6,10},{10,6},{7,11},{11,7},{20,24},{24,20... | collective-permute-start | bytes 3145736 | tf_op jit(solution)/shard_map/ppermute | solution.py:202
  3.9 4.0 %copy-done.2 = bf16[1024,5120]{1,0:T(8,128)(2,1)S(1)} copy-done((bf16[1024,5120]{1,0:T(8,128)(2,1)S(1)}, bf16[1024,5120]{1,0:T(8,128)(2,1)}, u32[]{:S(2)}) %copy-start.2) | copy-done | bytes 10485784
  7.9 0.7 %hold.2.refs_1_.refs_2_ = bf16[1024,5120]{1,0:T(8,128)(2,1)S(1)} custom-call(bf16[1024,5120]{1,0:T(8,128)(2,1)S(1)} %copy-done.2), custom_call_target="tpu_custom_call" | custom-call | bytes 1024 | tf_op jit(solution)/shard_map/hold/pallas_call | solution.py:103
  8.6 4.0 %copy-done.1 = bf16[1024,5120]{1,0:T(8,128)(2,1)} copy-done((bf16[1024,5120]{1,0:T(8,128)(2,1)}, bf16[1024,5120]{1,0:T(8,128)(2,1)S(1)}, u32[]{:S(2)}) %copy-start.1) | copy-done | bytes 10485784
  13.4 0.7 %fusion.5 = (s32[1]{0:T(128)}, s32[1]{0:T(128)}) fusion(s32[3]{0:T(128)S(1)} %copy-done.5, s32[]{:T(128)S(6)} %min.7, s32[]{:T(128)S(6)} %min.8), kind=kLoop, calls=%fused_computation.15 | loop fusion | bytes 24 | tf_op jit(solution)/shard_map/dynamic_slice | solution.py:194
  15.2 1.1 %dynamic-slice_bitcast_fusion.3 = (bf16[64,1024]{1,0:T(8,128)(2,1)S(1)}, bf16[64,1024]{1,0:T(8,128)(2,1)S(1)}, bf16[64,1024]{1,0:T(8,128)(2,1)S(1)}, bf16[64,1024]{1,0:T(8,128)(2,1)S(1)}) fusion(bf16[4,64,1024]{2,1,0:T(8,128)(2,1)} %bitcast.26, s32[]{:T(128)S(6)} %select_n.93, s32[]{:T(128)S(6)} %select_n.98, s32[]{:T(128)S(6)} %select_n.97, s32[]{:T(128)S(6)} %select_n.95), kind=kLoop, calls=%fused_computation.11 | loop fusion | bytes 1048592 | tf_op jit(solution)/shard_map/jit(dynamic_index_in_dim)/squeeze | solution.py:213
  16.4 0.9 %attend_own.1 = (f32[256,1024]{1,0:T(8,128)S(1)}, f32[256,1024]{1,0:T(8,128)S(1)}, f32[256,1024]{1,0:T(8,128)S(1)}) custom-call(bf16[256,1024]{1,0:T(8,128)(2,1)S(1)} %pad_maximum_fusion.q_ref, bf16[2,1,256,1024]{3,2,1,0:T(8,128)(2,1)S(1)} %copy-done.4), custom_call_target="tpu_custom_call" | custom-call | flops 268435456 | bytes 1572864 | tf_op jit(solution)/shard_map/attend_own/pallas_call | solution.py:81
  17.4 4.1 %hold.3.refs_1_.refs_3_ = bf16[1024,5120]{1,0:T(8,128)(2,1)S(1)} custom-call(bf16[1024,5120]{1,0:T(8,128)(2,1)} %collective-permute-done.src_ref), custom_call_target="tpu_custom_call" | custom-call | bytes 1024 | tf_op jit(solution)/shard_map/hold/pallas_call | solution.py:103
  21.6 5.5 %collective-permute-done.2.halo_ref = bf16[2,1,256,1024]{3,2,1,0:T(8,128)(2,1)S(1)} collective-permute-done((bf16[2,1,256,1024]{3,2,1,0:T(8,128)(2,1)}, bf16[2,1,256,1024]{3,2,1,0:T(8,128)(2,1)S(1)}, u32[]{:S(2)}, u32[]{:S(2)}) %collective-permute-start.2) | collective-permute-done | bytes 1048608 | tf_op jit(solution)/shard_map/ppermute | solution.py:202
  27.1 1.2 %attend_first.1 = (f32[256,1024]{1,0:T(8,128)S(1)}, f32[256,1024]{1,0:T(8,128)S(1)}, f32[256,1024]{1,0:T(8,128)S(1)}) custom-call(bf16[256,1024]{1,0:T(8,128)(2,1)S(1)} %pad_maximum_fusion.q_ref, bf16[2,1,256,1024]{3,2,1,0:T(8,128)(2,1)S(1)} %collective-permute-done.2.halo_ref, f32[1,256]{1,0:T(1,128)S(1)} %select_select_fusion.mask_ref, ...), custom_call_target="tpu_custom_call" | custom-call | flops 268435456 | bytes 4719616 | tf_op jit(solution)/shard_map/attend_first/pallas_call | solution.py:81
  28.3 0.6 %attend_second.3 = bf16[128,1024]{1,0:T(8,128)(2,1)S(1)} custom-call(bf16[256,1024]{1,0:T(8,128)(2,1)S(1)} %pad_maximum_fusion.q_ref, bf16[2,1,256,1024]{3,2,1,0:T(8,128)(2,1)S(1)} %collective-permute-done.1.halo_ref, f32[1,256]{1,0:T(1,128)S(1)} %select_select_fusion.1.mask_ref, f32[256,1024]{1,0:T(8,128)S(1)} %get-tuple-element.39.acc_ref, ...), custom_call_target="tpu_custom_call" | custom-call | flops 134217728 | bytes 4719616 | tf_op jit(solution)/shard_map/attend_second/pallas_call | solution.py:81
  29.0 0.6 %attend_second.2.refs_0_ = bf16[128,1024]{1,0:T(8,128)(2,1)S(1)} custom-call(bf16[256,1024]{1,0:T(8,128)(2,1)S(1)} %pad_maximum_fusion.q_ref, bf16[2,1,256,1024]{3,2,1,0:T(8,128)(2,1)S(1)} %collective-permute-done.1.halo_ref, f32[1,256]{1,0:T(1,128)S(1)} %select_select_fusion.1.mask_ref, f32[256,1024]{1,0:T(8,128)S(1)} %get-tuple-element.39.acc_ref, ...), custom_call_target="tpu_custom_call" | custom-call | flops 134217728 | bytes 4719616 | tf_op jit(solution)/shard_map/attend_second/pallas_call | solution.py:81
  29.7 0.5 project.5.refs_2_
  30.2 0.3 collective-permute-done.3.refs_0_.refs_1_
  30.6 0.6 project.6
  31.1 1.7 %collective-permute-start.4 = (bf16[64,1280]{1,0:T(8,128)(2,1)S(1)}, bf16[64,1280]{1,0:T(8,128)(2,1)S(1)}, u32[]{:S(2)}, u32[]{:S(2)}) collective-permute-start(bf16[64,1280]{1,0:T(8,128)(2,1)S(1)} %get-tuple-element.46), channel_id=1, source_target_pairs={{0,2},{2,0},{1,3},{3,1},{4,6},{6,4},{5,7},{7,5},{8,10},{10,8},{9,1... | collective-permute-start | bytes 491528 | tf_op jit(solution)/shard_map/ppermute | solution.py:186
  32.8 0.9 %project.8 = (bf16[64,1280]{1,0:T(8,128)(2,1)S(1)}, f32[64,1280]{1,0:T(8,128)S(1)}) custom-call(bf16[128,1024]{1,0:T(8,128)(2,1)S(1)} %attend_second.2.refs_0_, bf16[128,1024]{1,0:T(8,128)(2,1)S(1)} %collective-permute-done.3.refs_0_.refs_1_, bf16[1024,5120]{1,0:T(8,128)(2,1)S(1)} %bitcast.20, bf16[1024,5120]{1,0:T(8,128)(2,1)S(1)} %hold.3.refs_1_.refs_3_), custom_call_target="tpu_custom_call" | custom-call | flops 671088640 | bytes 5242880 | tf_op jit(solution)/shard_map/project/pallas_call | solution.py:143
  33.8 0.9 %project.7 = (bf16[64,1280]{1,0:T(8,128)(2,1)S(1)}, f32[64,1280]{1,0:T(8,128)S(1)}) custom-call(bf16[128,1024]{1,0:T(8,128)(2,1)S(1)} %attend_second.2.refs_0_, bf16[128,1024]{1,0:T(8,128)(2,1)S(1)} %collective-permute-done.3.refs_0_.refs_1_, bf16[1024,5120]{1,0:T(8,128)(2,1)S(1)} %bitcast.20, bf16[1024,5120]{1,0:T(8,128)(2,1)S(1)} %hold.3.refs_1_.refs_3_), custom_call_target="tpu_custom_call" | custom-call | flops 671088640 | bytes 5242880 | tf_op jit(solution)/shard_map/project/pallas_call | solution.py:143
  34.7 0.4 collective-permute-start.6
  35.1 1.7 %collective-permute-start.8 = (bf16[64,1280]{1,0:T(8,128)(2,1)S(1)}, bf16[64,1280]{1,0:T(8,128)(2,1)S(1)}, u32[]{:S(2)}, u32[]{:S(2)}) collective-permute-start(bf16[64,1280]{1,0:T(8,128)(2,1)S(1)} %get-tuple-element.54), channel_id=1, source_target_pairs={{0,2},{2,0},{1,3},{3,1},{4,6},{6,4},{5,7},{7,5},{8,10},{10,8},{9,1... | collective-permute-start | bytes 491528 | tf_op jit(solution)/shard_map/ppermute | solution.py:186
  36.8 0.9 %project.9 = (bf16[64,1280]{1,0:T(8,128)(2,1)S(1)}, f32[64,1280]{1,0:T(8,128)S(1)}) custom-call(bf16[128,1024]{1,0:T(8,128)(2,1)S(1)} %attend_second.2.refs_0_, bf16[128,1024]{1,0:T(8,128)(2,1)S(1)} %collective-permute-done.3.refs_0_.refs_1_, bf16[1024,5120]{1,0:T(8,128)(2,1)S(1)} %bitcast.20, bf16[1024,5120]{1,0:T(8,128)(2,1)S(1)} %hold.3.refs_1_.refs_3_), custom_call_target="tpu_custom_call" | custom-call | flops 671088640 | bytes 5242880 | tf_op jit(solution)/shard_map/project/pallas_call | solution.py:143
  37.7 0.4 collective-permute-start.10
  38.2 3.6 %collective-permute-start.5 = (bf16[64,1280]{1,0:T(8,128)(2,1)S(1)}, bf16[64,1280]{1,0:T(8,128)(2,1)S(1)}, u32[]{:S(2)}, u32[]{:S(2)}) collective-permute-start(bf16[64,1280]{1,0:T(8,128)(2,1)S(1)} %combine.4), channel_id=1, source_target_pairs={{0,4},{4,8},{8,12},{12,0},{1,5},{5,9},{9,13},{13,1},{2,6},{6,10},{... | collective-permute-start | bytes 491528 | tf_op jit(solution)/shard_map/ppermute | solution.py:186
  41.9 3.4 %collective-permute-start.7 = (bf16[64,1280]{1,0:T(8,128)(2,1)S(1)}, bf16[64,1280]{1,0:T(8,128)(2,1)S(1)}, u32[]{:S(2)}, u32[]{:S(2)}) collective-permute-start(bf16[64,1280]{1,0:T(8,128)(2,1)S(1)} %combine.5), channel_id=1, source_target_pairs={{0,4},{4,8},{8,12},{12,0},{1,5},{5,9},{9,13},{13,1},{2,6},{6,10},{... | collective-permute-start | bytes 491528 | tf_op jit(solution)/shard_map/ppermute | solution.py:186
  45.4 3.4 %collective-permute-start.9 = (bf16[64,1280]{1,0:T(8,128)(2,1)S(1)}, bf16[64,1280]{1,0:T(8,128)(2,1)S(1)}, u32[]{:S(2)}, u32[]{:S(2)}) collective-permute-start(bf16[64,1280]{1,0:T(8,128)(2,1)S(1)} %combine.6), channel_id=1, source_target_pairs={{0,4},{4,8},{8,12},{12,0},{1,5},{5,9},{9,13},{13,1},{2,6},{6,10},{... | collective-permute-start | bytes 491528 | tf_op jit(solution)/shard_map/ppermute | solution.py:186
  48.9 2.8 %collective-permute-start.11 = (bf16[64,1280]{1,0:T(8,128)(2,1)S(1)}, bf16[64,1280]{1,0:T(8,128)(2,1)S(1)}, u32[]{:S(2)}, u32[]{:S(2)}) collective-permute-start(bf16[64,1280]{1,0:T(8,128)(2,1)S(1)} %combine.7), channel_id=1, source_target_pairs={{0,4},{4,8},{8,12},{12,0},{1,5},{5,9},{9,13},{13,1},{2,6},{6,10},{... | collective-permute-start | bytes 491528 | tf_op jit(solution)/shard_map/ppermute | solution.py:186
  51.7 1.2 %collective-permute-done.9 = bf16[64,1280]{1,0:T(8,128)(2,1)S(1)} collective-permute-done((bf16[64,1280]{1,0:T(8,128)(2,1)S(1)}, bf16[64,1280]{1,0:T(8,128)(2,1)S(1)}, u32[]{:S(2)}, u32[]{:S(2)}) %collective-permute-start.9) | collective-permute-done | bytes 163872 | tf_op jit(solution)/shard_map/ppermute | solution.py:186
  52.9 0.9 %fusion.4 = bf16[64,5120]{1,0:T(8,128)(2,1)} fusion(bf16[64,1280]{1,0:T(8,128)(2,1)S(1)} %collective-permute-done.9, bf16[64,1280]{1,0:T(8,128)(2,1)S(1)} %collective-permute-done.7, bf16[64,1280]{1,0:T(8,128)(2,1)S(1)} %collective-permute-done.5), kind=kLoop, calls=%fused_computation.5 | loop fusion | flops 3276800 | bytes 1146880 | tf_op jit(solution)/shard_map/concatenate | solution.py:260
  53.8 2.3 %collective-permute-done.11 = bf16[64,1280]{1,0:T(8,128)(2,1)S(1)} collective-permute-done((bf16[64,1280]{1,0:T(8,128)(2,1)S(1)}, bf16[64,1280]{1,0:T(8,128)(2,1)S(1)}, u32[]{:S(2)}, u32[]{:S(2)}) %collective-permute-start.11) | collective-permute-done | bytes 163872 | tf_op jit(solution)/shard_map/ppermute | solution.py:186
  56.1 0.7 %bitcast_dynamic-update-slice_fusion = bf16[1,64,5120]{2,1,0:T(8,128)(2,1)} fusion(bf16[1,64,5120]{2,1,0:T(8,128)(2,1)} %bitcast.25, bf16[64,1280]{1,0:T(8,128)(2,1)S(1)} %collective-permute-done.11), kind=kLoop, calls=%fused_computation.7 | loop fusion | bytes 327680 | tf_op jit(solution)/shard_map/dynamic_update_slice | solution.py:262
  (34 shorter events, 0.6 us)
Async XLA Ops:
  0.0 17.3 %copy-start = (f32[8,5120]{1,0:T(8,128)S(1)}, f32[8,5120]{1,0:T(8,128)}, u32[]{:S(2)}) copy-start(f32[8,5120]{1,0:T(8,128)} %param.11) | copy-start | bytes 491524
  0.0 17.4 %collective-permute-start = (bf16[1024,5120]{1,0:T(8,128)(2,1)}, bf16[1024,5120]{1,0:T(8,128)(2,1)}, u32[]{:S(2)}, u32[]{:S(2)}) collective-permute-start(bf16[1024,5120]{1,0:T(8,128)(2,1)} %src_ref.1), channel_id=1, source_target_pairs={{0,1},{1,0},{2,3},{3,2},{4,5},{5,4},{6,7},{7,6},{8,9},{9,8},{10,11... | collective-permute-start | bytes 31457288 | tf_op jit(solution)/shard_map/ppermute | solution.py:186
  0.5 26.6 %collective-permute-start.2 = (bf16[2,1,256,1024]{3,2,1,0:T(8,128)(2,1)}, bf16[2,1,256,1024]{3,2,1,0:T(8,128)(2,1)S(1)}, u32[]{:S(2)}, u32[]{:S(2)}) collective-permute-start(bf16[2,1,256,1024]{3,2,1,0:T(8,128)(2,1)} %own_ref.1), channel_id=1, source_target_pairs={{0,4},{4,0},{8,12},{12,8},{1,5},{5,1},{9,13},{13,9},{2,6},{6,2},{1... | collective-permute-start | bytes 3145736 | tf_op jit(solution)/shard_map/ppermute | solution.py:202
  3.1 25.2 %collective-permute-start.1 = (bf16[2,1,256,1024]{3,2,1,0:T(8,128)(2,1)}, bf16[2,1,256,1024]{3,2,1,0:T(8,128)(2,1)S(1)}, u32[]{:S(2)}, u32[]{:S(2)}) collective-permute-start(bf16[2,1,256,1024]{3,2,1,0:T(8,128)(2,1)} %own_ref.1), channel_id=1, source_target_pairs={{4,8},{8,4},{5,9},{9,5},{6,10},{10,6},{7,11},{11,7},{20,24},{24,20... | collective-permute-start | bytes 3145736 | tf_op jit(solution)/shard_map/ppermute | solution.py:202
  3.9 4.0 %copy-start.2 = (bf16[1024,5120]{1,0:T(8,128)(2,1)S(1)}, bf16[1024,5120]{1,0:T(8,128)(2,1)}, u32[]{:S(2)}) copy-start(bf16[1024,5120]{1,0:T(8,128)(2,1)} %src_ref.1) | copy-start | bytes 31457284
  7.8 5.5 %copy-start.5 = (s32[3]{0:T(128)S(1)}, s32[3]{0:T(128)}, u32[]{:S(2)}) copy-start(s32[3]{0:T(128)} %param.13) | copy-start | bytes 40
  8.6 4.0 %copy-start.1 = (bf16[1024,5120]{1,0:T(8,128)(2,1)}, bf16[1024,5120]{1,0:T(8,128)(2,1)S(1)}, u32[]{:S(2)}) copy-start(bf16[1024,5120]{1,0:T(8,128)(2,1)S(1)} %hold.2.refs_1_.refs_2_) | copy-start | bytes 31457284
  12.6 3.8 %copy-start.4 = (bf16[2,1,256,1024]{3,2,1,0:T(8,128)(2,1)S(1)}, bf16[2,1,256,1024]{3,2,1,0:T(8,128)(2,1)}, u32[]{:S(2)}) copy-start(bf16[2,1,256,1024]{3,2,1,0:T(8,128)(2,1)} %own_ref.1) | copy-start | bytes 3145732
  17.4 12.3 %slice-start = ((s8[10485760]{0:T(1024)(128)(4,1)}), s8[4194304]{0:T(1024)(128)(4,1)S(1)}, s32[]{:S(2)}) async-start(s8[10485760]{0:T(1024)(128)(4,1)} %bitcast.19), calls=%async_computation | async-start | bytes 8388608
  17.4 12.3 %slice-start.1 = ((s8[10485760]{0:T(1024)(128)(4,1)}), s8[4194304]{0:T(1024)(128)(4,1)S(1)}, s32[]{:S(2)}) async-start(s8[10485760]{0:T(1024)(128)(4,1)} %bitcast.19), calls=%async_computation.1 | async-start | bytes 8388608
  21.6 8.1 %slice-start.2 = ((s8[10485760]{0:T(1024)(128)(4,1)}), s8[2097152]{0:T(1024)(128)(4,1)S(1)}, s32[]{:S(2)}) async-start(s8[10485760]{0:T(1024)(128)(4,1)} %bitcast.19), calls=%async_computation.2 | async-start | bytes 4194304
  29.0 1.6 %collective-permute-start.3 = (bf16[128,1024]{1,0:T(8,128)(2,1)S(1)}, bf16[128,1024]{1,0:T(8,128)(2,1)S(1)}, u32[]{:S(2)}, u32[]{:S(2)}) collective-permute-start(bf16[128,1024]{1,0:T(8,128)(2,1)S(1)} %attend_second.3), channel_id=1, source_target_pairs={{0,1},{1,0},{2,3},{3,2},{4,5},{5,4},{6,7},{7,6},{8,9},{9,8},{10,11... | collective-permute-start | bytes 786440 | tf_op jit(solution)/shard_map/ppermute | solution.py:186
  31.1 7.0 %collective-permute-start.4 = (bf16[64,1280]{1,0:T(8,128)(2,1)S(1)}, bf16[64,1280]{1,0:T(8,128)(2,1)S(1)}, u32[]{:S(2)}, u32[]{:S(2)}) collective-permute-start(bf16[64,1280]{1,0:T(8,128)(2,1)S(1)} %get-tuple-element.46), channel_id=1, source_target_pairs={{0,2},{2,0},{1,3},{3,1},{4,6},{6,4},{5,7},{7,5},{8,10},{10,8},{9,1... | collective-permute-start | bytes 491528 | tf_op jit(solution)/shard_map/ppermute | solution.py:186
  34.7 7.1 %collective-permute-start.6 = (bf16[64,1280]{1,0:T(8,128)(2,1)S(1)}, bf16[64,1280]{1,0:T(8,128)(2,1)S(1)}, u32[]{:S(2)}, u32[]{:S(2)}) collective-permute-start(bf16[64,1280]{1,0:T(8,128)(2,1)S(1)} %get-tuple-element.52), channel_id=1, source_target_pairs={{0,2},{2,0},{1,3},{3,1},{4,6},{6,4},{5,7},{7,5},{8,10},{10,8},{9,1... | collective-permute-start | bytes 491528 | tf_op jit(solution)/shard_map/ppermute | solution.py:186
  35.1 3.0 %copy-start.3 = (bf16[1,64,5120]{2,1,0:T(8,128)(2,1)S(1)}, bf16[1,64,5120]{2,1,0:T(8,128)(2,1)}, u32[]{:S(2)}) copy-start(bf16[1,64,5120]{2,1,0:T(8,128)(2,1)} %param.9) | copy-start | bytes 1966084
  35.1 10.2 %collective-permute-start.8 = (bf16[64,1280]{1,0:T(8,128)(2,1)S(1)}, bf16[64,1280]{1,0:T(8,128)(2,1)S(1)}, u32[]{:S(2)}, u32[]{:S(2)}) collective-permute-start(bf16[64,1280]{1,0:T(8,128)(2,1)S(1)} %get-tuple-element.54), channel_id=1, source_target_pairs={{0,2},{2,0},{1,3},{3,1},{4,6},{6,4},{5,7},{7,5},{8,10},{10,8},{9,1... | collective-permute-start | bytes 491528 | tf_op jit(solution)/shard_map/ppermute | solution.py:186
  37.7 11.1 %collective-permute-start.10 = (bf16[64,1280]{1,0:T(8,128)(2,1)S(1)}, bf16[64,1280]{1,0:T(8,128)(2,1)S(1)}, u32[]{:S(2)}, u32[]{:S(2)}) collective-permute-start(bf16[64,1280]{1,0:T(8,128)(2,1)S(1)} %get-tuple-element.56), channel_id=1, source_target_pairs={{0,2},{2,0},{1,3},{3,1},{4,6},{6,4},{5,7},{7,5},{8,10},{10,8},{9,1... | collective-permute-start | bytes 491528 | tf_op jit(solution)/shard_map/ppermute | solution.py:186
  38.2 13.5 %collective-permute-start.5 = (bf16[64,1280]{1,0:T(8,128)(2,1)S(1)}, bf16[64,1280]{1,0:T(8,128)(2,1)S(1)}, u32[]{:S(2)}, u32[]{:S(2)}) collective-permute-start(bf16[64,1280]{1,0:T(8,128)(2,1)S(1)} %combine.4), channel_id=1, source_target_pairs={{0,4},{4,8},{8,12},{12,0},{1,5},{5,9},{9,13},{13,1},{2,6},{6,10},{... | collective-permute-start | bytes 491528 | tf_op jit(solution)/shard_map/ppermute | solution.py:186
  41.9 9.8 %collective-permute-start.7 = (bf16[64,1280]{1,0:T(8,128)(2,1)S(1)}, bf16[64,1280]{1,0:T(8,128)(2,1)S(1)}, u32[]{:S(2)}, u32[]{:S(2)}) collective-permute-start(bf16[64,1280]{1,0:T(8,128)(2,1)S(1)} %combine.5), channel_id=1, source_target_pairs={{0,4},{4,8},{8,12},{12,0},{1,5},{5,9},{9,13},{13,1},{2,6},{6,10},{... | collective-permute-start | bytes 491528 | tf_op jit(solution)/shard_map/ppermute | solution.py:186
  45.4 7.5 %collective-permute-start.9 = (bf16[64,1280]{1,0:T(8,128)(2,1)S(1)}, bf16[64,1280]{1,0:T(8,128)(2,1)S(1)}, u32[]{:S(2)}, u32[]{:S(2)}) collective-permute-start(bf16[64,1280]{1,0:T(8,128)(2,1)S(1)} %combine.6), channel_id=1, source_target_pairs={{0,4},{4,8},{8,12},{12,0},{1,5},{5,9},{9,13},{13,1},{2,6},{6,10},{... | collective-permute-start | bytes 491528 | tf_op jit(solution)/shard_map/ppermute | solution.py:186
  48.9 7.2 %collective-permute-start.11 = (bf16[64,1280]{1,0:T(8,128)(2,1)S(1)}, bf16[64,1280]{1,0:T(8,128)(2,1)S(1)}, u32[]{:S(2)}, u32[]{:S(2)}) collective-permute-start(bf16[64,1280]{1,0:T(8,128)(2,1)S(1)} %combine.7), channel_id=1, source_target_pairs={{0,4},{4,8},{8,12},{12,0},{1,5},{5,9},{9,13},{13,1},{2,6},{6,10},{... | collective-permute-start | bytes 491528 | tf_op jit(solution)/shard_map/ppermute | solution.py:186

commit v8 on v7

--- a/solution.py
+++ b/solution.py
@@ -50,28 +50,41 @@
     rows, width = outs[0].shape
     part = slice(first, first + rows)
     mask = mask_ref[...]
-    ones = jnp.ones((halo_ref.shape[2], HD), jnp.bfloat16)
     heads = [slice(h * HD, (h + 1) * HD) for h in range(width // HD)]
-    scores = [scores_of(q_ref[part, head], halo_ref[0, 0, :, head]) + mask for head in heads]
-    peaks = [jnp.max(s, axis=1, keepdims=True) for s in scores]
-    probs, fades = [], []
-    for head, s, peak in zip(heads, scores, peaks):
-        before = top_ref[part, head]
-        top = jnp.maximum(before, jnp.broadcast_to(peak, before.shape))
-        probs.append(exponentials(s, top))
-        fades.append(jnp.exp2((before - top) * FACTOR))
-        if not last:
-            outs[2][:, head] = top
-    for head, p, fade in zip(heads, probs, fades):
-        values = jnp.concatenate([halo_ref[1, 0, :, head], ones], axis=1)
-        both = jnp.dot(p, values, preferred_element_type=jnp.float32)
-        weighted = acc_ref[part, head] * fade + both[:, :HD]
-        total = den_ref[part, head] * fade + both[:, HD:]
-        if last:
-            outs[0][:, head] = (weighted / total).astype(outs[0].dtype)
-        else:
-            outs[0][:, head] = weighted
-            outs[1][:, head] = total
+
+    def visit():
+        ones = jnp.ones((halo_ref.shape[2], HD), jnp.bfloat16)
+        scores = [scores_of(q_ref[part, head], halo_ref[0, 0, :, head]) + mask for head in heads]
+        peaks = [jnp.max(s, axis=1, keepdims=True) for s in scores]
+        probs, fades = [], []
+        for head, s, peak in zip(heads, scores, peaks):
+            before = top_ref[part, head]
+            top = jnp.maximum(before, jnp.broadcast_to(peak, before.shape))
+            probs.append(exponentials(s, top))
+            fades.append(jnp.exp2((before - top) * FACTOR))
+            if not last:
+                outs[2][:, head] = top
+        for head, p, fade in zip(heads, probs, fades):
+            values = jnp.concatenate([halo_ref[1, 0, :, head], ones], axis=1)
+            both = jnp.dot(p, values, preferred_element_type=jnp.float32)
+            weighted = acc_ref[part, head] * fade + both[:, :HD]
+            total = den_ref[part, head] * fade + both[:, HD:]
+            if last:
+                outs[0][:, head] = (weighted / total).astype(outs[0].dtype)
+            else:
+                outs[0][:, head] = weighted
+                outs[1][:, head] = total
+
+    if not last:
+        visit()
+        return
+    anything = jnp.max(mask) == 0.0
+    pl.when(anything)(visit)
+
+    @pl.when(jnp.logical_not(anything))
+    def _():
+        for head in heads:
+            outs[0][:, head] = (acc_ref[part, head] / den_ref[part, head]).astype(outs[0].dtype)
 
 
 VMEM_SPEC = pl.BlockSpec(memory_space=pltpu.VMEM)

time: 57 us -> 57 us (level)
  Pallas kernels: 12.3 us -> 11.5 us
  starting transfers between devices: 21.2 us -> 22 us
    pallas_call x4, Pallas kernels: 3.38 us -> 2.55 us  [attend(): pl.pallas_call(kernel, out_shape=out_shape, in_specs=[VMEM_SPEC] * len(op...]
    ppermute x10, starting transfers between devices: 17.9 us -> 18.7 us  [rotate(): lax.ppermute(value, axis, [(i, (i + steps) % count) for i in range(count)])]
  transfers between devices with their start and end apart: 12 -> 12, of which waited for: 6 -> 4; matrix products, arithmetic and copies ran while one was open for 5% -> 5% of each run, Pallas kernels for 20% -> 19%
where the time goes in v8:
time: 57 us; the launch traced here: 56.8 us
  starting transfers between devices  22 us (39%)
  Pallas kernels  11.5 us (20%)
  local copies, waits for them, and re-layouts  10.5 us (18%)
  waiting for transfers between devices  9.57 us (17%)
  between operations  2.29 us (4%)
  other arithmetic  0.94 us (2%)
    ppermute x10, starting transfers between devices, rotate(): lax.ppermute(value, axis, [(i, (i + steps) % count) for i in range(count)])  18.7 us
    unnamed x18, local copies, waits for them, and re-layouts  8.01 us
    ppermute x2, waiting for transfers between devices, shards(): lax.ppermute(keys_values, 'section', pairs)  5.5 us
    pallas_call x2, Pallas kernels, hold(): pl.pallas_call(hold_kernel, out_shape=jax.ShapeDtypeStruct(array.shape, a...  4.84 us
    ppermute x10, waiting for transfers between devices, rotate(): lax.ppermute(value, axis, [(i, (i + steps) % count) for i in range(count)])  4.07 us
    pallas_call x5, Pallas kernels, project(): pl.pallas_call(functools.partial(project_kernel, parts, rows, first, len(...  3.83 us
    ppermute x2, starting transfers between devices, shards(): lax.ppermute(keys_values, 'section', pairs)  3.36 us
    pallas_call x4, Pallas kernels, attend(): pl.pallas_call(kernel, out_shape=out_shape, in_specs=[VMEM_SPEC] * len(op...  2.55 us
  transfers between devices with their start and end apart: 12, of which 4 were waited for; matrix products, arithmetic and copies ran while one was open for 5% of the time, Pallas kernels for 19%

profile of v8, /device:TPU:0, one launch (start us, length us, event | category | flops | bytes accessed | tf_op | source)
XLA Modules:
  0.0 56.8 jit_solution(1912760332988442238)
XLA Ops:
  0.0 0.5 collective-permute-start
  0.5 2.6 %collective-permute-start.2 = (bf16[2,1,256,1024]{3,2,1,0:T(8,128)(2,1)}, bf16[2,1,256,1024]{3,2,1,0:T(8,128)(2,1)S(1)}, u32[]{:S(2)}, u32[]{:S(2)}) collective-permute-start(bf16[2,1,256,1024]{3,2,1,0:T(8,128)(2,1)} %own_ref.1), channel_id=1, source_target_pairs={{0,4},{4,0},{8,12},{12,8},{1,5},{5,1},{9,13},{13,9},{2,6},{6,2},{1... | collective-permute-start | bytes 3145736 | tf_op jit(solution)/shard_map/ppermute | solution.py:215
  3.1 0.7 %collective-permute-start.1 = (bf16[2,1,256,1024]{3,2,1,0:T(8,128)(2,1)}, bf16[2,1,256,1024]{3,2,1,0:T(8,128)(2,1)S(1)}, u32[]{:S(2)}, u32[]{:S(2)}) collective-permute-start(bf16[2,1,256,1024]{3,2,1,0:T(8,128)(2,1)} %own_ref.1), channel_id=1, source_target_pairs={{4,8},{8,4},{5,9},{9,5},{6,10},{10,6},{7,11},{11,7},{20,24},{24,20... | collective-permute-start | bytes 3145736 | tf_op jit(solution)/shard_map/ppermute | solution.py:215
  3.9 4.0 %copy-done.2 = bf16[1024,5120]{1,0:T(8,128)(2,1)S(1)} copy-done((bf16[1024,5120]{1,0:T(8,128)(2,1)S(1)}, bf16[1024,5120]{1,0:T(8,128)(2,1)}, u32[]{:S(2)}) %copy-start.2) | copy-done | bytes 10485784
  7.9 0.7 %hold.2.refs_1_.refs_2_ = bf16[1024,5120]{1,0:T(8,128)(2,1)S(1)} custom-call(bf16[1024,5120]{1,0:T(8,128)(2,1)S(1)} %copy-done.2), custom_call_target="tpu_custom_call" | custom-call | bytes 1024 | tf_op jit(solution)/shard_map/hold/pallas_call | solution.py:116
  8.6 4.0 %copy-done.1 = bf16[1024,5120]{1,0:T(8,128)(2,1)} copy-done((bf16[1024,5120]{1,0:T(8,128)(2,1)}, bf16[1024,5120]{1,0:T(8,128)(2,1)S(1)}, u32[]{:S(2)}) %copy-start.1) | copy-done | bytes 10485784
  13.4 0.7 %fusion.5 = (s32[1]{0:T(128)}, s32[1]{0:T(128)}) fusion(s32[3]{0:T(128)S(1)} %copy-done.5, s32[]{:T(128)S(6)} %min.7, s32[]{:T(128)S(6)} %min.8), kind=kLoop, calls=%fused_computation.15 | loop fusion | bytes 24 | tf_op jit(solution)/shard_map/dynamic_slice | solution.py:207
  15.2 1.1 %dynamic-slice_bitcast_fusion.3 = (bf16[64,1024]{1,0:T(8,128)(2,1)S(1)}, bf16[64,1024]{1,0:T(8,128)(2,1)S(1)}, bf16[64,1024]{1,0:T(8,128)(2,1)S(1)}, bf16[64,1024]{1,0:T(8,128)(2,1)S(1)}) fusion(bf16[4,64,1024]{2,1,0:T(8,128)(2,1)} %bitcast.26, s32[]{:T(128)S(6)} %select_n.93, s32[]{:T(128)S(6)} %select_n.98, s32[]{:T(128)S(6)} %select_n.97, s32[]{:T(128)S(6)} %select_n.95), kind=kLoop, calls=%fused_computation.11 | loop fusion | bytes 1048592 | tf_op jit(solution)/shard_map/jit(dynamic_index_in_dim)/squeeze | solution.py:226
  16.4 0.9 %attend_own.1 = (f32[256,1024]{1,0:T(8,128)S(1)}, f32[256,1024]{1,0:T(8,128)S(1)}, f32[256,1024]{1,0:T(8,128)S(1)}) custom-call(bf16[256,1024]{1,0:T(8,128)(2,1)S(1)} %pad_maximum_fusion.q_ref, bf16[2,1,256,1024]{3,2,1,0:T(8,128)(2,1)S(1)} %copy-done.4), custom_call_target="tpu_custom_call" | custom-call | flops 268435456 | bytes 1572864 | tf_op jit(solution)/shard_map/attend_own/pallas_call | solution.py:94
  17.4 4.1 %hold.3.refs_1_.refs_3_ = bf16[1024,5120]{1,0:T(8,128)(2,1)S(1)} custom-call(bf16[1024,5120]{1,0:T(8,128)(2,1)} %collective-permute-done.src_ref), custom_call_target="tpu_custom_call" | custom-call | bytes 1024 | tf_op jit(solution)/shard_map/hold/pallas_call | solution.py:116
  21.6 5.5 %collective-permute-done.2.halo_ref = bf16[2,1,256,1024]{3,2,1,0:T(8,128)(2,1)S(1)} collective-permute-done((bf16[2,1,256,1024]{3,2,1,0:T(8,128)(2,1)}, bf16[2,1,256,1024]{3,2,1,0:T(8,128)(2,1)S(1)}, u32[]{:S(2)}, u32[]{:S(2)}) %collective-permute-start.2) | collective-permute-done | bytes 1048608 | tf_op jit(solution)/shard_map/ppermute | solution.py:215
  27.1 1.2 %attend_first.1 = (f32[256,1024]{1,0:T(8,128)S(1)}, f32[256,1024]{1,0:T(8,128)S(1)}, f32[256,1024]{1,0:T(8,128)S(1)}) custom-call(bf16[256,1024]{1,0:T(8,128)(2,1)S(1)} %pad_maximum_fusion.q_ref, bf16[2,1,256,1024]{3,2,1,0:T(8,128)(2,1)S(1)} %collective-permute-done.2.halo_ref, f32[1,256]{1,0:T(1,128)S(1)} %select_select_fusion.mask_ref, ...), custom_call_target="tpu_custom_call" | custom-call | flops 268435456 | bytes 4719616 | tf_op jit(solution)/shard_map/attend_first/pallas_call | solution.py:94
  28.3 0.2 attend_second.3
  28.6 0.2 attend_second.2.refs_0_
  28.9 0.5 project.5.refs_2_
  29.4 0.7 %collective-permute-done.3.refs_0_.refs_1_ = bf16[128,1024]{1,0:T(8,128)(2,1)S(1)} collective-permute-done((bf16[128,1024]{1,0:T(8,128)(2,1)S(1)}, bf16[128,1024]{1,0:T(8,128)(2,1)S(1)}, u32[]{:S(2)}, u32[]{:S(2)}) %collective-permute-start.3) | collective-permute-done | bytes 262176 | tf_op jit(solution)/shard_map/ppermute | solution.py:199
  30.1 0.6 project.6
  30.7 1.7 %collective-permute-start.4 = (bf16[64,1280]{1,0:T(8,128)(2,1)S(1)}, bf16[64,1280]{1,0:T(8,128)(2,1)S(1)}, u32[]{:S(2)}, u32[]{:S(2)}) collective-permute-start(bf16[64,1280]{1,0:T(8,128)(2,1)S(1)} %get-tuple-element.46), channel_id=1, source_target_pairs={{0,2},{2,0},{1,3},{3,1},{4,6},{6,4},{5,7},{7,5},{8,10},{10,8},{9,1... | collective-permute-start | bytes 491528 | tf_op jit(solution)/shard_map/ppermute | solution.py:199
  32.4 0.9 %project.8 = (bf16[64,1280]{1,0:T(8,128)(2,1)S(1)}, f32[64,1280]{1,0:T(8,128)S(1)}) custom-call(bf16[128,1024]{1,0:T(8,128)(2,1)S(1)} %attend_second.2.refs_0_, bf16[128,1024]{1,0:T(8,128)(2,1)S(1)} %collective-permute-done.3.refs_0_.refs_1_, bf16[1024,5120]{1,0:T(8,128)(2,1)S(1)} %bitcast.20, bf16[1024,5120]{1,0:T(8,128)(2,1)S(1)} %hold.3.refs_1_.refs_3_), custom_call_target="tpu_custom_call" | custom-call | flops 671088640 | bytes 5242880 | tf_op jit(solution)/shard_map/project/pallas_call | solution.py:156
  33.4 0.9 %project.7 = (bf16[64,1280]{1,0:T(8,128)(2,1)S(1)}, f32[64,1280]{1,0:T(8,128)S(1)}) custom-call(bf16[128,1024]{1,0:T(8,128)(2,1)S(1)} %attend_second.2.refs_0_, bf16[128,1024]{1,0:T(8,128)(2,1)S(1)} %collective-permute-done.3.refs_0_.refs_1_, bf16[1024,5120]{1,0:T(8,128)(2,1)S(1)} %bitcast.20, bf16[1024,5120]{1,0:T(8,128)(2,1)S(1)} %hold.3.refs_1_.refs_3_), custom_call_target="tpu_custom_call" | custom-call | flops 671088640 | bytes 5242880 | tf_op jit(solution)/shard_map/project/pallas_call | solution.py:156
  34.3 0.4 collective-permute-start.6
  34.7 1.7 %collective-permute-start.8 = (bf16[64,1280]{1,0:T(8,128)(2,1)S(1)}, bf16[64,1280]{1,0:T(8,128)(2,1)S(1)}, u32[]{:S(2)}, u32[]{:S(2)}) collective-permute-start(bf16[64,1280]{1,0:T(8,128)(2,1)S(1)} %get-tuple-element.54), channel_id=1, source_target_pairs={{0,2},{2,0},{1,3},{3,1},{4,6},{6,4},{5,7},{7,5},{8,10},{10,8},{9,1... | collective-permute-start | bytes 491528 | tf_op jit(solution)/shard_map/ppermute | solution.py:199
  36.4 0.9 %project.9 = (bf16[64,1280]{1,0:T(8,128)(2,1)S(1)}, f32[64,1280]{1,0:T(8,128)S(1)}) custom-call(bf16[128,1024]{1,0:T(8,128)(2,1)S(1)} %attend_second.2.refs_0_, bf16[128,1024]{1,0:T(8,128)(2,1)S(1)} %collective-permute-done.3.refs_0_.refs_1_, bf16[1024,5120]{1,0:T(8,128)(2,1)S(1)} %bitcast.20, bf16[1024,5120]{1,0:T(8,128)(2,1)S(1)} %hold.3.refs_1_.refs_3_), custom_call_target="tpu_custom_call" | custom-call | flops 671088640 | bytes 5242880 | tf_op jit(solution)/shard_map/project/pallas_call | solution.py:156
  37.3 0.4 collective-permute-start.10
  37.8 4.1 %collective-permute-start.5 = (bf16[64,1280]{1,0:T(8,128)(2,1)S(1)}, bf16[64,1280]{1,0:T(8,128)(2,1)S(1)}, u32[]{:S(2)}, u32[]{:S(2)}) collective-permute-start(bf16[64,1280]{1,0:T(8,128)(2,1)S(1)} %combine.4), channel_id=1, source_target_pairs={{0,4},{4,8},{8,12},{12,0},{1,5},{5,9},{9,13},{13,1},{2,6},{6,10},{... | collective-permute-start | bytes 491528 | tf_op jit(solution)/shard_map/ppermute | solution.py:199
  41.9 3.4 %collective-permute-start.7 = (bf16[64,1280]{1,0:T(8,128)(2,1)S(1)}, bf16[64,1280]{1,0:T(8,128)(2,1)S(1)}, u32[]{:S(2)}, u32[]{:S(2)}) collective-permute-start(bf16[64,1280]{1,0:T(8,128)(2,1)S(1)} %combine.5), channel_id=1, source_target_pairs={{0,4},{4,8},{8,12},{12,0},{1,5},{5,9},{9,13},{13,1},{2,6},{6,10},{... | collective-permute-start | bytes 491528 | tf_op jit(solution)/shard_map/ppermute | solution.py:199
  45.5 3.4 %collective-permute-start.9 = (bf16[64,1280]{1,0:T(8,128)(2,1)S(1)}, bf16[64,1280]{1,0:T(8,128)(2,1)S(1)}, u32[]{:S(2)}, u32[]{:S(2)}) collective-permute-start(bf16[64,1280]{1,0:T(8,128)(2,1)S(1)} %combine.6), channel_id=1, source_target_pairs={{0,4},{4,8},{8,12},{12,0},{1,5},{5,9},{9,13},{13,1},{2,6},{6,10},{... | collective-permute-start | bytes 491528 | tf_op jit(solution)/shard_map/ppermute | solution.py:199
  49.0 2.9 %collective-permute-start.11 = (bf16[64,1280]{1,0:T(8,128)(2,1)S(1)}, bf16[64,1280]{1,0:T(8,128)(2,1)S(1)}, u32[]{:S(2)}, u32[]{:S(2)}) collective-permute-start(bf16[64,1280]{1,0:T(8,128)(2,1)S(1)} %combine.7), channel_id=1, source_target_pairs={{0,4},{4,8},{8,12},{12,0},{1,5},{5,9},{9,13},{13,1},{2,6},{6,10},{... | collective-permute-start | bytes 491528 | tf_op jit(solution)/shard_map/ppermute | solution.py:199
  51.9 1.1 %collective-permute-done.9 = bf16[64,1280]{1,0:T(8,128)(2,1)S(1)} collective-permute-done((bf16[64,1280]{1,0:T(8,128)(2,1)S(1)}, bf16[64,1280]{1,0:T(8,128)(2,1)S(1)}, u32[]{:S(2)}, u32[]{:S(2)}) %collective-permute-start.9) | collective-permute-done | bytes 163872 | tf_op jit(solution)/shard_map/ppermute | solution.py:199
  53.0 0.9 %fusion.4 = bf16[64,5120]{1,0:T(8,128)(2,1)} fusion(bf16[64,1280]{1,0:T(8,128)(2,1)S(1)} %collective-permute-done.9, bf16[64,1280]{1,0:T(8,128)(2,1)S(1)} %collective-permute-done.7, bf16[64,1280]{1,0:T(8,128)(2,1)S(1)} %collective-permute-done.5), kind=kLoop, calls=%fused_computation.5 | loop fusion | flops 3276800 | bytes 1146880 | tf_op jit(solution)/shard_map/concatenate | solution.py:273
  53.9 2.3 %collective-permute-done.11 = bf16[64,1280]{1,0:T(8,128)(2,1)S(1)} collective-permute-done((bf16[64,1280]{1,0:T(8,128)(2,1)S(1)}, bf16[64,1280]{1,0:T(8,128)(2,1)S(1)}, u32[]{:S(2)}, u32[]{:S(2)}) %collective-permute-start.11) | collective-permute-done | bytes 163872 | tf_op jit(solution)/shard_map/ppermute | solution.py:199
  56.1 0.7 %bitcast_dynamic-update-slice_fusion = bf16[1,64,5120]{2,1,0:T(8,128)(2,1)} fusion(bf16[1,64,5120]{2,1,0:T(8,128)(2,1)} %bitcast.25, bf16[64,1280]{1,0:T(8,128)(2,1)S(1)} %collective-permute-done.11), kind=kLoop, calls=%fused_computation.7 | loop fusion | bytes 327680 | tf_op jit(solution)/shard_map/dynamic_update_slice | solution.py:275
  (34 shorter events, 0.5 us)
Async XLA Ops:
  0.0 17.3 %copy-start = (f32[8,5120]{1,0:T(8,128)S(1)}, f32[8,5120]{1,0:T(8,128)}, u32[]{:S(2)}) copy-start(f32[8,5120]{1,0:T(8,128)} %param.11) | copy-start | bytes 491524
  0.0 17.4 %collective-permute-start = (bf16[1024,5120]{1,0:T(8,128)(2,1)}, bf16[1024,5120]{1,0:T(8,128)(2,1)}, u32[]{:S(2)}, u32[]{:S(2)}) collective-permute-start(bf16[1024,5120]{1,0:T(8,128)(2,1)} %src_ref.1), channel_id=1, source_target_pairs={{0,1},{1,0},{2,3},{3,2},{4,5},{5,4},{6,7},{7,6},{8,9},{9,8},{10,11... | collective-permute-start | bytes 31457288 | tf_op jit(solution)/shard_map/ppermute | solution.py:199
  0.5 26.6 %collective-permute-start.2 = (bf16[2,1,256,1024]{3,2,1,0:T(8,128)(2,1)}, bf16[2,1,256,1024]{3,2,1,0:T(8,128)(2,1)S(1)}, u32[]{:S(2)}, u32[]{:S(2)}) collective-permute-start(bf16[2,1,256,1024]{3,2,1,0:T(8,128)(2,1)} %own_ref.1), channel_id=1, source_target_pairs={{0,4},{4,0},{8,12},{12,8},{1,5},{5,1},{9,13},{13,9},{2,6},{6,2},{1... | collective-permute-start | bytes 3145736 | tf_op jit(solution)/shard_map/ppermute | solution.py:215
  3.1 25.2 %collective-permute-start.1 = (bf16[2,1,256,1024]{3,2,1,0:T(8,128)(2,1)}, bf16[2,1,256,1024]{3,2,1,0:T(8,128)(2,1)S(1)}, u32[]{:S(2)}, u32[]{:S(2)}) collective-permute-start(bf16[2,1,256,1024]{3,2,1,0:T(8,128)(2,1)} %own_ref.1), channel_id=1, source_target_pairs={{4,8},{8,4},{5,9},{9,5},{6,10},{10,6},{7,11},{11,7},{20,24},{24,20... | collective-permute-start | bytes 3145736 | tf_op jit(solution)/shard_map/ppermute | solution.py:215
  3.9 4.0 %copy-start.2 = (bf16[1024,5120]{1,0:T(8,128)(2,1)S(1)}, bf16[1024,5120]{1,0:T(8,128)(2,1)}, u32[]{:S(2)}) copy-start(bf16[1024,5120]{1,0:T(8,128)(2,1)} %src_ref.1) | copy-start | bytes 31457284
  7.8 5.5 %copy-start.5 = (s32[3]{0:T(128)S(1)}, s32[3]{0:T(128)}, u32[]{:S(2)}) copy-start(s32[3]{0:T(128)} %param.13) | copy-start | bytes 40
  8.6 4.0 %copy-start.1 = (bf16[1024,5120]{1,0:T(8,128)(2,1)}, bf16[1024,5120]{1,0:T(8,128)(2,1)S(1)}, u32[]{:S(2)}) copy-start(bf16[1024,5120]{1,0:T(8,128)(2,1)S(1)} %hold.2.refs_1_.refs_2_) | copy-start | bytes 31457284
  12.6 3.8 %copy-start.4 = (bf16[2,1,256,1024]{3,2,1,0:T(8,128)(2,1)S(1)}, bf16[2,1,256,1024]{3,2,1,0:T(8,128)(2,1)}, u32[]{:S(2)}) copy-start(bf16[2,1,256,1024]{3,2,1,0:T(8,128)(2,1)} %own_ref.1) | copy-start | bytes 3145732
  17.4 11.4 %slice-start = ((s8[10485760]{0:T(1024)(128)(4,1)}), s8[4194304]{0:T(1024)(128)(4,1)S(1)}, s32[]{:S(2)}) async-start(s8[10485760]{0:T(1024)(128)(4,1)} %bitcast.19), calls=%async_computation | async-start | bytes 8388608
  17.4 11.4 %slice-start.1 = ((s8[10485760]{0:T(1024)(128)(4,1)}), s8[4194304]{0:T(1024)(128)(4,1)S(1)}, s32[]{:S(2)}) async-start(s8[10485760]{0:T(1024)(128)(4,1)} %bitcast.19), calls=%async_computation.1 | async-start | bytes 8388608
  21.6 7.3 %slice-start.2 = ((s8[10485760]{0:T(1024)(128)(4,1)}), s8[2097152]{0:T(1024)(128)(4,1)S(1)}, s32[]{:S(2)}) async-start(s8[10485760]{0:T(1024)(128)(4,1)} %bitcast.19), calls=%async_computation.2 | async-start | bytes 4194304
  28.5 1.6 %collective-permute-start.3 = (bf16[128,1024]{1,0:T(8,128)(2,1)S(1)}, bf16[128,1024]{1,0:T(8,128)(2,1)S(1)}, u32[]{:S(2)}, u32[]{:S(2)}) collective-permute-start(bf16[128,1024]{1,0:T(8,128)(2,1)S(1)} %attend_second.3), channel_id=1, source_target_pairs={{0,1},{1,0},{2,3},{3,2},{4,5},{5,4},{6,7},{7,6},{8,9},{9,8},{10,11... | collective-permute-start | bytes 786440 | tf_op jit(solution)/shard_map/ppermute | solution.py:199
  30.7 7.0 %collective-permute-start.4 = (bf16[64,1280]{1,0:T(8,128)(2,1)S(1)}, bf16[64,1280]{1,0:T(8,128)(2,1)S(1)}, u32[]{:S(2)}, u32[]{:S(2)}) collective-permute-start(bf16[64,1280]{1,0:T(8,128)(2,1)S(1)} %get-tuple-element.46), channel_id=1, source_target_pairs={{0,2},{2,0},{1,3},{3,1},{4,6},{6,4},{5,7},{7,5},{8,10},{10,8},{9,1... | collective-permute-start | bytes 491528 | tf_op jit(solution)/shard_map/ppermute | solution.py:199
  34.3 7.6 %collective-permute-start.6 = (bf16[64,1280]{1,0:T(8,128)(2,1)S(1)}, bf16[64,1280]{1,0:T(8,128)(2,1)S(1)}, u32[]{:S(2)}, u32[]{:S(2)}) collective-permute-start(bf16[64,1280]{1,0:T(8,128)(2,1)S(1)} %get-tuple-element.52), channel_id=1, source_target_pairs={{0,2},{2,0},{1,3},{3,1},{4,6},{6,4},{5,7},{7,5},{8,10},{10,8},{9,1... | collective-permute-start | bytes 491528 | tf_op jit(solution)/shard_map/ppermute | solution.py:199
  34.7 3.0 %copy-start.3 = (bf16[1,64,5120]{2,1,0:T(8,128)(2,1)S(1)}, bf16[1,64,5120]{2,1,0:T(8,128)(2,1)}, u32[]{:S(2)}) copy-start(bf16[1,64,5120]{2,1,0:T(8,128)(2,1)} %param.9) | copy-start | bytes 1966084
  34.7 10.7 %collective-permute-start.8 = (bf16[64,1280]{1,0:T(8,128)(2,1)S(1)}, bf16[64,1280]{1,0:T(8,128)(2,1)S(1)}, u32[]{:S(2)}, u32[]{:S(2)}) collective-permute-start(bf16[64,1280]{1,0:T(8,128)(2,1)S(1)} %get-tuple-element.54), channel_id=1, source_target_pairs={{0,2},{2,0},{1,3},{3,1},{4,6},{6,4},{5,7},{7,5},{8,10},{10,8},{9,1... | collective-permute-start | bytes 491528 | tf_op jit(solution)/shard_map/ppermute | solution.py:199
  37.3 11.6 %collective-permute-start.10 = (bf16[64,1280]{1,0:T(8,128)(2,1)S(1)}, bf16[64,1280]{1,0:T(8,128)(2,1)S(1)}, u32[]{:S(2)}, u32[]{:S(2)}) collective-permute-start(bf16[64,1280]{1,0:T(8,128)(2,1)S(1)} %get-tuple-element.56), channel_id=1, source_target_pairs={{0,2},{2,0},{1,3},{3,1},{4,6},{6,4},{5,7},{7,5},{8,10},{10,8},{9,1... | collective-permute-start | bytes 491528 | tf_op jit(solution)/shard_map/ppermute | solution.py:199
  37.8 14.1 %collective-permute-start.5 = (bf16[64,1280]{1,0:T(8,128)(2,1)S(1)}, bf16[64,1280]{1,0:T(8,128)(2,1)S(1)}, u32[]{:S(2)}, u32[]{:S(2)}) collective-permute-start(bf16[64,1280]{1,0:T(8,128)(2,1)S(1)} %combine.4), channel_id=1, source_target_pairs={{0,4},{4,8},{8,12},{12,0},{1,5},{5,9},{9,13},{13,1},{2,6},{6,10},{... | collective-permute-start | bytes 491528 | tf_op jit(solution)/shard_map/ppermute | solution.py:199
  41.9 10.0 %collective-permute-start.7 = (bf16[64,1280]{1,0:T(8,128)(2,1)S(1)}, bf16[64,1280]{1,0:T(8,128)(2,1)S(1)}, u32[]{:S(2)}, u32[]{:S(2)}) collective-permute-start(bf16[64,1280]{1,0:T(8,128)(2,1)S(1)} %combine.5), channel_id=1, source_target_pairs={{0,4},{4,8},{8,12},{12,0},{1,5},{5,9},{9,13},{13,1},{2,6},{6,10},{... | collective-permute-start | bytes 491528 | tf_op jit(solution)/shard_map/ppermute | solution.py:199
  45.5 7.5 %collective-permute-start.9 = (bf16[64,1280]{1,0:T(8,128)(2,1)S(1)}, bf16[64,1280]{1,0:T(8,128)(2,1)S(1)}, u32[]{:S(2)}, u32[]{:S(2)}) collective-permute-start(bf16[64,1280]{1,0:T(8,128)(2,1)S(1)} %combine.6), channel_id=1, source_target_pairs={{0,4},{4,8},{8,12},{12,0},{1,5},{5,9},{9,13},{13,1},{2,6},{6,10},{... | collective-permute-start | bytes 491528 | tf_op jit(solution)/shard_map/ppermute | solution.py:199
  49.0 7.2 %collective-permute-start.11 = (bf16[64,1280]{1,0:T(8,128)(2,1)S(1)}, bf16[64,1280]{1,0:T(8,128)(2,1)S(1)}, u32[]{:S(2)}, u32[]{:S(2)}) collective-permute-start(bf16[64,1280]{1,0:T(8,128)(2,1)S(1)} %combine.7), channel_id=1, source_target_pairs={{0,4},{4,8},{8,12},{12,0},{1,5},{5,9},{9,13},{13,1},{2,6},{6,10},{... | collective-permute-start | bytes 491528 | tf_op jit(solution)/shard_map/ppermute | solution.py:199

commit v9 on v7

--- a/solution.py
+++ b/solution.py
@@ -200,7 +200,7 @@
         for odd in (0, 1)
     ]
     first_halo, second_halo = (lax.ppermute(keys_values, "section", pairs) for pairs in swaps)
-    weights = [hold(out_weight)]
+    weights = [out_weight]
     weights += [hold(rotate(out_weight, "mp", l)) for l in range(1, cores)]
     own_latents = latents[0]
     span_tok = queries.shape[1]
@@ -223,7 +223,7 @@
     wide = jax.ShapeDtypeStruct((span_tok, width), jnp.float32)
     flops = 4 * span_tok * span_tok * width
     state = attend(own_kernel, "attend_own", (wide,) * 3, flops, own_queries, keys_values)
-    state, weights, gate_row = lax.optimization_barrier((state, weights, gate_row))
+    state, weights[1:], gate_row = lax.optimization_barrier((state, weights[1:], gate_row))
     kernel = functools.partial(halo_kernel, 0, False)
     state = attend(
         kernel, "attend_first", (wide,) * 3, flops, own_queries, first_halo, first_mask, *state

time: 57 us -> 60.9 us (1.068)
  waiting for transfers between devices: 9.5 us -> 25 us
  local copies, waits for them, and re-layouts: 10.5 us -> 3.21 us
  starting transfers between devices: 21.2 us -> 18.1 us
  Pallas kernels: 12.3 us -> 11.3 us
    ppermute x10, waiting for transfers between devices: 4 us -> 15.4 us  [rotate(): lax.ppermute(value, axis, [(i, (i + steps) % count) for i in range(count)])]
    unnamed x18 -> x12, local copies, waits for them, and re-layouts: 8.01 us -> 0.03 us
    ppermute x10, starting transfers between devices: 17.9 us -> 11.8 us  [rotate(): lax.ppermute(value, axis, [(i, (i + steps) % count) for i in range(count)])]
    ppermute x2, waiting for transfers between devices: 5.5 us -> 9.6 us  [shards(): lax.ppermute(keys_values, 'section', pairs)]
    ppermute x2, starting transfers between devices: 3.36 us -> 6.26 us  [shards(): lax.ppermute(keys_values, 'section', pairs)]
    pallas_call x2 -> x1, Pallas kernels: 4.84 us -> 4.14 us  [hold(): pl.pallas_call(hold_kernel, out_shape=jax.ShapeDtypeStruct(array.shape, a...]
    dynamic_slice x1, local copies, waits for them, and re-layouts: 0.65 us -> 1.35 us  [shards(): pair_window[jnp.clip(section_id - 1, 0, final_pair)]]
  transfers between devices with their start and end apart: 12 -> 12, of which waited for: 6 -> 9; matrix products, arithmetic and copies ran while one was open for 5% -> 6% of each run, Pallas kernels for 20% -> 15%
where the time goes in v9:
time: 60.9 us; the launch traced here: 60.7 us
  waiting for transfers between devices  25 us (41%)
  starting transfers between devices  18.1 us (30%)
  Pallas kernels  11.3 us (19%)
  local copies, waits for them, and re-layouts  3.21 us (5%)
  between operations  2.08 us (3%)
  other arithmetic  0.94 us (2%)
    ppermute x10, waiting for transfers between devices, rotate(): lax.ppermute(value, axis, [(i, (i + steps) % count) for i in range(count)])  15.4 us
    ppermute x10, starting transfers between devices, rotate(): lax.ppermute(value, axis, [(i, (i + steps) % count) for i in range(count)])  11.8 us
    ppermute x2, waiting for transfers between devices, shards(): lax.ppermute(keys_values, 'section', pairs)  9.6 us
    ppermute x2, starting transfers between devices, shards(): lax.ppermute(keys_values, 'section', pairs)  6.26 us
    pallas_call x1, Pallas kernels, hold(): pl.pallas_call(hold_kernel, out_shape=jax.ShapeDtypeStruct(array.shape, a...  4.14 us
    pallas_call x5, Pallas kernels, project(): pl.pallas_call(functools.partial(project_kernel, parts, rows, first, len(...  3.64 us
    pallas_call x4, Pallas kernels, attend(): pl.pallas_call(kernel, out_shape=out_shape, in_specs=[VMEM_SPEC] * len(op...  3.3 us
    dynamic_slice x1, local copies, waits for them, and re-layouts, shards(): pair_window[jnp.clip(section_id - 1, 0, final_pair)]  1.35 us
  transfers between devices with their start and end apart: 12, of which 9 were waited for; matrix products, arithmetic and copies ran while one was open for 6% of the time, Pallas kernels for 15%

profile of v9, /device:TPU:0, one launch (start us, length us, event | category | flops | bytes accessed | tf_op | source)
XLA Modules:
  0.0 60.7 jit_solution(12050368305829825365)
XLA Ops:
  0.5 0.7 %collective-permute-start.1 = (bf16[2,1,256,1024]{3,2,1,0:T(8,128)(2,1)}, bf16[2,1,256,1024]{3,2,1,0:T(8,128)(2,1)S(1)}, u32[]{:S(2)}, u32[]{:S(2)}) collective-permute-start(bf16[2,1,256,1024]{3,2,1,0:T(8,128)(2,1)} %own_ref.1), channel_id=1, source_target_pairs={{4,8},{8,4},{5,9},{9,5},{6,10},{10,6},{7,11},{11,7},{20,24},{24,20... | collective-permute-start | bytes 3145736 | tf_op jit(solution)/shard_map/ppermute | solution.py:202
  1.2 5.5 %collective-permute-start.2 = (bf16[2,1,256,1024]{3,2,1,0:T(8,128)(2,1)}, bf16[2,1,256,1024]{3,2,1,0:T(8,128)(2,1)S(1)}, u32[]{:S(2)}, u32[]{:S(2)}) collective-permute-start(bf16[2,1,256,1024]{3,2,1,0:T(8,128)(2,1)} %own_ref.1), channel_id=1, source_target_pairs={{0,4},{4,0},{8,12},{12,8},{1,5},{5,1},{9,13},{13,9},{2,6},{6,2},{1... | collective-permute-start | bytes 3145736 | tf_op jit(solution)/shard_map/ppermute | solution.py:202
  7.4 1.3 %fusion.5 = (s32[1]{0:T(128)}, s32[1]{0:T(128)}) fusion(s32[3]{0:T(128)} %param.13, s32[]{:T(128)S(6)} %min.7, s32[]{:T(128)S(6)} %min.8), kind=kLoop, calls=%fused_computation.15 | loop fusion | bytes 24 | tf_op jit(solution)/shard_map/dynamic_slice | solution.py:194
  9.9 1.1 %dynamic-slice_bitcast_fusion.3 = (bf16[64,1024]{1,0:T(8,128)(2,1)S(1)}, bf16[64,1024]{1,0:T(8,128)(2,1)S(1)}, bf16[64,1024]{1,0:T(8,128)(2,1)S(1)}, bf16[64,1024]{1,0:T(8,128)(2,1)S(1)}) fusion(bf16[4,64,1024]{2,1,0:T(8,128)(2,1)} %bitcast.26, s32[]{:T(128)S(6)} %select_n.93, s32[]{:T(128)S(6)} %select_n.98, s32[]{:T(128)S(6)} %select_n.97, s32[]{:T(128)S(6)} %select_n.95), kind=kLoop, calls=%fused_computation.11 | loop fusion | bytes 1048592 | tf_op jit(solution)/shard_map/jit(dynamic_index_in_dim)/squeeze | solution.py:213
  11.1 0.9 %attend_own.1 = (f32[256,1024]{1,0:T(8,128)S(1)}, f32[256,1024]{1,0:T(8,128)S(1)}, f32[256,1024]{1,0:T(8,128)S(1)}) custom-call(bf16[256,1024]{1,0:T(8,128)(2,1)S(1)} %pad_maximum_fusion.q_ref, bf16[2,1,256,1024]{3,2,1,0:T(8,128)(2,1)S(1)} %copy-done.2), custom_call_target="tpu_custom_call" | custom-call | flops 268435456 | bytes 1572864 | tf_op jit(solution)/shard_map/attend_own/pallas_call | solution.py:81
  12.1 4.5 %collective-permute-done.src_ref = bf16[1024,5120]{1,0:T(8,128)(2,1)} collective-permute-done((bf16[1024,5120]{1,0:T(8,128)(2,1)}, bf16[1024,5120]{1,0:T(8,128)(2,1)}, u32[]{:S(2)}, u32[]{:S(2)}) %collective-permute-start) | collective-permute-done | bytes 10485792 | tf_op jit(solution)/shard_map/ppermute | solution.py:186
  16.6 4.1 %hold.1.refs_1_.refs_3_ = bf16[1024,5120]{1,0:T(8,128)(2,1)S(1)} custom-call(bf16[1024,5120]{1,0:T(8,128)(2,1)} %collective-permute-done.src_ref), custom_call_target="tpu_custom_call" | custom-call | bytes 1024 | tf_op jit(solution)/shard_map/hold/pallas_call | solution.py:103
  20.7 9.6 %collective-permute-done.2.halo_ref = bf16[2,1,256,1024]{3,2,1,0:T(8,128)(2,1)S(1)} collective-permute-done((bf16[2,1,256,1024]{3,2,1,0:T(8,128)(2,1)}, bf16[2,1,256,1024]{3,2,1,0:T(8,128)(2,1)S(1)}, u32[]{:S(2)}, u32[]{:S(2)}) %collective-permute-start.2) | collective-permute-done | bytes 1048608 | tf_op jit(solution)/shard_map/ppermute | solution.py:202
  30.3 1.1 %attend_first.1 = (f32[256,1024]{1,0:T(8,128)S(1)}, f32[256,1024]{1,0:T(8,128)S(1)}, f32[256,1024]{1,0:T(8,128)S(1)}) custom-call(bf16[256,1024]{1,0:T(8,128)(2,1)S(1)} %pad_maximum_fusion.q_ref, bf16[2,1,256,1024]{3,2,1,0:T(8,128)(2,1)S(1)} %collective-permute-done.2.halo_ref, f32[1,256]{1,0:T(1,128)S(1)} %select_select_fusion.mask_ref, ...), custom_call_target="tpu_custom_call" | custom-call | flops 268435456 | bytes 4719616 | tf_op jit(solution)/shard_map/attend_first/pallas_call | solution.py:81
  31.5 0.7 %attend_second.3 = bf16[128,1024]{1,0:T(8,128)(2,1)S(1)} custom-call(bf16[256,1024]{1,0:T(8,128)(2,1)S(1)} %pad_maximum_fusion.q_ref, bf16[2,1,256,1024]{3,2,1,0:T(8,128)(2,1)S(1)} %collective-permute-done.1.halo_ref, f32[1,256]{1,0:T(1,128)S(1)} %select_select_fusion.1.mask_ref, f32[256,1024]{1,0:T(8,128)S(1)} %get-tuple-element.38.acc_ref, ...), custom_call_target="tpu_custom_call" | custom-call | flops 134217728 | bytes 4719616 | tf_op jit(solution)/shard_map/attend_second/pallas_call | solution.py:81
  32.2 0.6 %attend_second.2.refs_0_ = bf16[128,1024]{1,0:T(8,128)(2,1)S(1)} custom-call(bf16[256,1024]{1,0:T(8,128)(2,1)S(1)} %pad_maximum_fusion.q_ref, bf16[2,1,256,1024]{3,2,1,0:T(8,128)(2,1)S(1)} %collective-permute-done.1.halo_ref, f32[1,256]{1,0:T(1,128)S(1)} %select_select_fusion.1.mask_ref, f32[256,1024]{1,0:T(8,128)S(1)} %get-tuple-element.38.acc_ref, ...), custom_call_target="tpu_custom_call" | custom-call | flops 134217728 | bytes 4719616 | tf_op jit(solution)/shard_map/attend_second/pallas_call | solution.py:81
  32.9 0.5 project.5.refs_2_
  33.8 0.5 project.6
  34.3 0.9 %project.8 = (bf16[64,1280]{1,0:T(8,128)(2,1)S(1)}, f32[64,1280]{1,0:T(8,128)S(1)}) custom-call(bf16[128,1024]{1,0:T(8,128)(2,1)S(1)} %attend_second.2.refs_0_, bf16[128,1024]{1,0:T(8,128)(2,1)S(1)} %collective-permute-done.3.refs_0_.refs_1_, bf16[1024,5120]{1,0:T(8,128)(2,1)S(1)} %bitcast.20, bf16[1024,5120]{1,0:T(8,128)(2,1)S(1)} %hold.1.refs_1_.refs_3_), custom_call_target="tpu_custom_call" | custom-call | flops 671088640 | bytes 5242880 | tf_op jit(solution)/shard_map/project/pallas_call | solution.py:143
  35.2 1.5 %collective-permute-start.8 = (bf16[64,1280]{1,0:T(8,128)(2,1)S(1)}, bf16[64,1280]{1,0:T(8,128)(2,1)S(1)}, u32[]{:S(2)}, u32[]{:S(2)}) collective-permute-start(bf16[64,1280]{1,0:T(8,128)(2,1)S(1)} %get-tuple-element.52), channel_id=1, source_target_pairs={{0,2},{2,0},{1,3},{3,1},{4,6},{6,4},{5,7},{7,5},{8,10},{10,8},{9,1... | collective-permute-start | bytes 491528 | tf_op jit(solution)/shard_map/ppermute | solution.py:186
  36.7 0.9 %project.7 = (bf16[64,1280]{1,0:T(8,128)(2,1)S(1)}, f32[64,1280]{1,0:T(8,128)S(1)}) custom-call(bf16[128,1024]{1,0:T(8,128)(2,1)S(1)} %attend_second.2.refs_0_, bf16[128,1024]{1,0:T(8,128)(2,1)S(1)} %collective-permute-done.3.refs_0_.refs_1_, bf16[1024,5120]{1,0:T(8,128)(2,1)S(1)} %bitcast.20, bf16[1024,5120]{1,0:T(8,128)(2,1)S(1)} %hold.1.refs_1_.refs_3_), custom_call_target="tpu_custom_call" | custom-call | flops 671088640 | bytes 5242880 | tf_op jit(solution)/shard_map/project/pallas_call | solution.py:143
  37.6 0.6 %collective-permute-start.6 = (bf16[64,1280]{1,0:T(8,128)(2,1)S(1)}, bf16[64,1280]{1,0:T(8,128)(2,1)S(1)}, u32[]{:S(2)}, u32[]{:S(2)}) collective-permute-start(bf16[64,1280]{1,0:T(8,128)(2,1)S(1)} %get-tuple-element.50), channel_id=1, source_target_pairs={{0,2},{2,0},{1,3},{3,1},{4,6},{6,4},{5,7},{7,5},{8,10},{10,8},{9,1... | collective-permute-start | bytes 491528 | tf_op jit(solution)/shard_map/ppermute | solution.py:186
  38.2 1.5 %collective-permute-start.4 = (bf16[64,1280]{1,0:T(8,128)(2,1)S(1)}, bf16[64,1280]{1,0:T(8,128)(2,1)S(1)}, u32[]{:S(2)}, u32[]{:S(2)}) collective-permute-start(bf16[64,1280]{1,0:T(8,128)(2,1)S(1)} %get-tuple-element.44), channel_id=1, source_target_pairs={{0,2},{2,0},{1,3},{3,1},{4,6},{6,4},{5,7},{7,5},{8,10},{10,8},{9,1... | collective-permute-start | bytes 491528 | tf_op jit(solution)/shard_map/ppermute | solution.py:186
  39.7 0.9 %project.9 = (bf16[64,1280]{1,0:T(8,128)(2,1)S(1)}, f32[64,1280]{1,0:T(8,128)S(1)}) custom-call(bf16[128,1024]{1,0:T(8,128)(2,1)S(1)} %attend_second.2.refs_0_, bf16[128,1024]{1,0:T(8,128)(2,1)S(1)} %collective-permute-done.3.refs_0_.refs_1_, bf16[1024,5120]{1,0:T(8,128)(2,1)S(1)} %bitcast.20, bf16[1024,5120]{1,0:T(8,128)(2,1)S(1)} %hold.1.refs_1_.refs_3_), custom_call_target="tpu_custom_call" | custom-call | flops 671088640 | bytes 5242880 | tf_op jit(solution)/shard_map/project/pallas_call | solution.py:143
  40.5 0.6 %collective-permute-start.10 = (bf16[64,1280]{1,0:T(8,128)(2,1)S(1)}, bf16[64,1280]{1,0:T(8,128)(2,1)S(1)}, u32[]{:S(2)}, u32[]{:S(2)}) collective-permute-start(bf16[64,1280]{1,0:T(8,128)(2,1)S(1)} %get-tuple-element.54), channel_id=1, source_target_pairs={{0,2},{2,0},{1,3},{3,1},{4,6},{6,4},{5,7},{7,5},{8,10},{10,8},{9,1... | collective-permute-start | bytes 491528 | tf_op jit(solution)/shard_map/ppermute | solution.py:186
  41.1 1.1 %collective-permute-done.8.refs_0_ = bf16[64,1280]{1,0:T(8,128)(2,1)S(1)} collective-permute-done((bf16[64,1280]{1,0:T(8,128)(2,1)S(1)}, bf16[64,1280]{1,0:T(8,128)(2,1)S(1)}, u32[]{:S(2)}, u32[]{:S(2)}) %collective-permute-start.8) | collective-permute-done | bytes 163872 | tf_op jit(solution)/shard_map/ppermute | solution.py:186
  42.3 1.8 %collective-permute-start.9 = (bf16[64,1280]{1,0:T(8,128)(2,1)S(1)}, bf16[64,1280]{1,0:T(8,128)(2,1)S(1)}, u32[]{:S(2)}, u32[]{:S(2)}) collective-permute-start(bf16[64,1280]{1,0:T(8,128)(2,1)S(1)} %combine.6), channel_id=1, source_target_pairs={{0,4},{4,8},{8,12},{12,0},{1,5},{5,9},{9,13},{13,1},{2,6},{6,10},{... | collective-permute-start | bytes 491528 | tf_op jit(solution)/shard_map/ppermute | solution.py:186
  44.1 1.7 %collective-permute-done.6.refs_0_ = bf16[64,1280]{1,0:T(8,128)(2,1)S(1)} collective-permute-done((bf16[64,1280]{1,0:T(8,128)(2,1)S(1)}, bf16[64,1280]{1,0:T(8,128)(2,1)S(1)}, u32[]{:S(2)}, u32[]{:S(2)}) %collective-permute-start.6) | collective-permute-done | bytes 163872 | tf_op jit(solution)/shard_map/ppermute | solution.py:186
  45.8 1.8 %collective-permute-start.7 = (bf16[64,1280]{1,0:T(8,128)(2,1)S(1)}, bf16[64,1280]{1,0:T(8,128)(2,1)S(1)}, u32[]{:S(2)}, u32[]{:S(2)}) collective-permute-start(bf16[64,1280]{1,0:T(8,128)(2,1)S(1)} %combine.5), channel_id=1, source_target_pairs={{0,4},{4,8},{8,12},{12,0},{1,5},{5,9},{9,13},{13,1},{2,6},{6,10},{... | collective-permute-start | bytes 491528 | tf_op jit(solution)/shard_map/ppermute | solution.py:186
  47.6 1.7 %collective-permute-done.4.refs_0_ = bf16[64,1280]{1,0:T(8,128)(2,1)S(1)} collective-permute-done((bf16[64,1280]{1,0:T(8,128)(2,1)S(1)}, bf16[64,1280]{1,0:T(8,128)(2,1)S(1)}, u32[]{:S(2)}, u32[]{:S(2)}) %collective-permute-start.4) | collective-permute-done | bytes 163872 | tf_op jit(solution)/shard_map/ppermute | solution.py:186
  49.4 1.8 %collective-permute-start.5 = (bf16[64,1280]{1,0:T(8,128)(2,1)S(1)}, bf16[64,1280]{1,0:T(8,128)(2,1)S(1)}, u32[]{:S(2)}, u32[]{:S(2)}) collective-permute-start(bf16[64,1280]{1,0:T(8,128)(2,1)S(1)} %combine.4), channel_id=1, source_target_pairs={{0,4},{4,8},{8,12},{12,0},{1,5},{5,9},{9,13},{13,1},{2,6},{6,10},{... | collective-permute-start | bytes 491528 | tf_op jit(solution)/shard_map/ppermute | solution.py:186
  51.1 0.9 %collective-permute-done.10.refs_0_ = bf16[64,1280]{1,0:T(8,128)(2,1)S(1)} collective-permute-done((bf16[64,1280]{1,0:T(8,128)(2,1)S(1)}, bf16[64,1280]{1,0:T(8,128)(2,1)S(1)}, u32[]{:S(2)}, u32[]{:S(2)}) %collective-permute-start.10) | collective-permute-done | bytes 163872 | tf_op jit(solution)/shard_map/ppermute | solution.py:186
  52.1 1.8 %collective-permute-start.11 = (bf16[64,1280]{1,0:T(8,128)(2,1)S(1)}, bf16[64,1280]{1,0:T(8,128)(2,1)S(1)}, u32[]{:S(2)}, u32[]{:S(2)}) collective-permute-start(bf16[64,1280]{1,0:T(8,128)(2,1)S(1)} %combine.7), channel_id=1, source_target_pairs={{0,4},{4,8},{8,12},{12,0},{1,5},{5,9},{9,13},{13,1},{2,6},{6,10},{... | collective-permute-start | bytes 491528 | tf_op jit(solution)/shard_map/ppermute | solution.py:186
  53.9 3.2 %collective-permute-done.5 = bf16[64,1280]{1,0:T(8,128)(2,1)S(1)} collective-permute-done((bf16[64,1280]{1,0:T(8,128)(2,1)S(1)}, bf16[64,1280]{1,0:T(8,128)(2,1)S(1)}, u32[]{:S(2)}, u32[]{:S(2)}) %collective-permute-start.5) | collective-permute-done | bytes 163872 | tf_op jit(solution)/shard_map/ppermute | solution.py:186
  57.1 0.9 %fusion.4 = bf16[64,5120]{1,0:T(8,128)(2,1)} fusion(bf16[64,1280]{1,0:T(8,128)(2,1)S(1)} %collective-permute-done.9, bf16[64,1280]{1,0:T(8,128)(2,1)S(1)} %collective-permute-done.7, bf16[64,1280]{1,0:T(8,128)(2,1)S(1)} %collective-permute-done.5), kind=kLoop, calls=%fused_computation.5 | loop fusion | flops 3276800 | bytes 1146880 | tf_op jit(solution)/shard_map/concatenate | solution.py:260
  58.0 2.1 %collective-permute-done.11 = bf16[64,1280]{1,0:T(8,128)(2,1)S(1)} collective-permute-done((bf16[64,1280]{1,0:T(8,128)(2,1)S(1)}, bf16[64,1280]{1,0:T(8,128)(2,1)S(1)}, u32[]{:S(2)}, u32[]{:S(2)}) %collective-permute-start.11) | collective-permute-done | bytes 163872 | tf_op jit(solution)/shard_map/ppermute | solution.py:186
  60.0 0.7 %bitcast_dynamic-update-slice_fusion = bf16[1,64,5120]{2,1,0:T(8,128)(2,1)} fusion(bf16[1,64,5120]{2,1,0:T(8,128)(2,1)} %bitcast.25, bf16[64,1280]{1,0:T(8,128)(2,1)S(1)} %collective-permute-done.11), kind=kLoop, calls=%fused_computation.7 | loop fusion | bytes 327680 | tf_op jit(solution)/shard_map/dynamic_update_slice | solution.py:262
  (27 shorter events, 1.2 us)
Async XLA Ops:
  0.0 12.1 %copy-start = (f32[8,5120]{1,0:T(8,128)S(1)}, f32[8,5120]{1,0:T(8,128)}, u32[]{:S(2)}) copy-start(f32[8,5120]{1,0:T(8,128)} %param.11) | copy-start | bytes 491524
  0.0 11.1 %copy-start.2 = (bf16[2,1,256,1024]{3,2,1,0:T(8,128)(2,1)S(1)}, bf16[2,1,256,1024]{3,2,1,0:T(8,128)(2,1)}, u32[]{:S(2)}) copy-start(bf16[2,1,256,1024]{3,2,1,0:T(8,128)(2,1)} %own_ref.1) | copy-start | bytes 3145732
  0.0 16.6 %collective-permute-start = (bf16[1024,5120]{1,0:T(8,128)(2,1)}, bf16[1024,5120]{1,0:T(8,128)(2,1)}, u32[]{:S(2)}, u32[]{:S(2)}) collective-permute-start(bf16[1024,5120]{1,0:T(8,128)(2,1)} %refs_2_.5), channel_id=1, source_target_pairs={{0,1},{1,0},{2,3},{3,2},{4,5},{5,4},{6,7},{7,6},{8,9},{9,8},{10,11... | collective-permute-start | bytes 31457288 | tf_op jit(solution)/shard_map/ppermute | solution.py:186
  0.5 31.0 %collective-permute-start.1 = (bf16[2,1,256,1024]{3,2,1,0:T(8,128)(2,1)}, bf16[2,1,256,1024]{3,2,1,0:T(8,128)(2,1)S(1)}, u32[]{:S(2)}, u32[]{:S(2)}) collective-permute-start(bf16[2,1,256,1024]{3,2,1,0:T(8,128)(2,1)} %own_ref.1), channel_id=1, source_target_pairs={{4,8},{8,4},{5,9},{9,5},{6,10},{10,6},{7,11},{11,7},{20,24},{24,20... | collective-permute-start | bytes 3145736 | tf_op jit(solution)/shard_map/ppermute | solution.py:202
  1.2 29.2 %collective-permute-start.2 = (bf16[2,1,256,1024]{3,2,1,0:T(8,128)(2,1)}, bf16[2,1,256,1024]{3,2,1,0:T(8,128)(2,1)S(1)}, u32[]{:S(2)}, u32[]{:S(2)}) collective-permute-start(bf16[2,1,256,1024]{3,2,1,0:T(8,128)(2,1)} %own_ref.1), channel_id=1, source_target_pairs={{0,4},{4,0},{8,12},{12,8},{1,5},{5,1},{9,13},{13,9},{2,6},{6,2},{1... | collective-permute-start | bytes 3145736 | tf_op jit(solution)/shard_map/ppermute | solution.py:202
  16.6 16.3 %slice-start = ((s8[10485760]{0:T(1024)(128)(4,1)}), s8[4194304]{0:T(1024)(128)(4,1)S(1)}, s32[]{:S(2)}) async-start(s8[10485760]{0:T(1024)(128)(4,1)} %bitcast.19), calls=%async_computation | async-start | bytes 8388608
  16.6 16.3 %slice-start.1 = ((s8[10485760]{0:T(1024)(128)(4,1)}), s8[4194304]{0:T(1024)(128)(4,1)S(1)}, s32[]{:S(2)}) async-start(s8[10485760]{0:T(1024)(128)(4,1)} %bitcast.19), calls=%async_computation.1 | async-start | bytes 8388608
  20.7 12.1 %slice-start.2 = ((s8[10485760]{0:T(1024)(128)(4,1)}), s8[2097152]{0:T(1024)(128)(4,1)S(1)}, s32[]{:S(2)}) async-start(s8[10485760]{0:T(1024)(128)(4,1)} %bitcast.19), calls=%async_computation.2 | async-start | bytes 4194304
  32.1 1.6 %collective-permute-start.3 = (bf16[128,1024]{1,0:T(8,128)(2,1)S(1)}, bf16[128,1024]{1,0:T(8,128)(2,1)S(1)}, u32[]{:S(2)}, u32[]{:S(2)}) collective-permute-start(bf16[128,1024]{1,0:T(8,128)(2,1)S(1)} %attend_second.3), channel_id=1, source_target_pairs={{0,1},{1,0},{2,3},{3,2},{4,5},{5,4},{6,7},{7,6},{8,9},{9,8},{10,11... | collective-permute-start | bytes 786440 | tf_op jit(solution)/shard_map/ppermute | solution.py:186
  35.2 7.1 %collective-permute-start.8 = (bf16[64,1280]{1,0:T(8,128)(2,1)S(1)}, bf16[64,1280]{1,0:T(8,128)(2,1)S(1)}, u32[]{:S(2)}, u32[]{:S(2)}) collective-permute-start(bf16[64,1280]{1,0:T(8,128)(2,1)S(1)} %get-tuple-element.52), channel_id=1, source_target_pairs={{0,2},{2,0},{1,3},{3,1},{4,6},{6,4},{5,7},{7,5},{8,10},{10,8},{9,1... | collective-permute-start | bytes 491528 | tf_op jit(solution)/shard_map/ppermute | solution.py:186
  37.6 8.2 %collective-permute-start.6 = (bf16[64,1280]{1,0:T(8,128)(2,1)S(1)}, bf16[64,1280]{1,0:T(8,128)(2,1)S(1)}, u32[]{:S(2)}, u32[]{:S(2)}) collective-permute-start(bf16[64,1280]{1,0:T(8,128)(2,1)S(1)} %get-tuple-element.50), channel_id=1, source_target_pairs={{0,2},{2,0},{1,3},{3,1},{4,6},{6,4},{5,7},{7,5},{8,10},{10,8},{9,1... | collective-permute-start | bytes 491528 | tf_op jit(solution)/shard_map/ppermute | solution.py:186
  38.2 4.1 %copy-start.1 = (bf16[1,64,5120]{2,1,0:T(8,128)(2,1)S(1)}, bf16[1,64,5120]{2,1,0:T(8,128)(2,1)}, u32[]{:S(2)}) copy-start(bf16[1,64,5120]{2,1,0:T(8,128)(2,1)} %param.9) | copy-start | bytes 1966084
  38.2 11.1 %collective-permute-start.4 = (bf16[64,1280]{1,0:T(8,128)(2,1)S(1)}, bf16[64,1280]{1,0:T(8,128)(2,1)S(1)}, u32[]{:S(2)}, u32[]{:S(2)}) collective-permute-start(bf16[64,1280]{1,0:T(8,128)(2,1)S(1)} %get-tuple-element.44), channel_id=1, source_target_pairs={{0,2},{2,0},{1,3},{3,1},{4,6},{6,4},{5,7},{7,5},{8,10},{10,8},{9,1... | collective-permute-start | bytes 491528 | tf_op jit(solution)/shard_map/ppermute | solution.py:186
  40.5 11.5 %collective-permute-start.10 = (bf16[64,1280]{1,0:T(8,128)(2,1)S(1)}, bf16[64,1280]{1,0:T(8,128)(2,1)S(1)}, u32[]{:S(2)}, u32[]{:S(2)}) collective-permute-start(bf16[64,1280]{1,0:T(8,128)(2,1)S(1)} %get-tuple-element.54), channel_id=1, source_target_pairs={{0,2},{2,0},{1,3},{3,1},{4,6},{6,4},{5,7},{7,5},{8,10},{10,8},{9,1... | collective-permute-start | bytes 491528 | tf_op jit(solution)/shard_map/ppermute | solution.py:186
  42.3 11.6 %collective-permute-start.9 = (bf16[64,1280]{1,0:T(8,128)(2,1)S(1)}, bf16[64,1280]{1,0:T(8,128)(2,1)S(1)}, u32[]{:S(2)}, u32[]{:S(2)}) collective-permute-start(bf16[64,1280]{1,0:T(8,128)(2,1)S(1)} %combine.6), channel_id=1, source_target_pairs={{0,4},{4,8},{8,12},{12,0},{1,5},{5,9},{9,13},{13,1},{2,6},{6,10},{... | collective-permute-start | bytes 491528 | tf_op jit(solution)/shard_map/ppermute | solution.py:186
  45.8 8.1 %collective-permute-start.7 = (bf16[64,1280]{1,0:T(8,128)(2,1)S(1)}, bf16[64,1280]{1,0:T(8,128)(2,1)S(1)}, u32[]{:S(2)}, u32[]{:S(2)}) collective-permute-start(bf16[64,1280]{1,0:T(8,128)(2,1)S(1)} %combine.5), channel_id=1, source_target_pairs={{0,4},{4,8},{8,12},{12,0},{1,5},{5,9},{9,13},{13,1},{2,6},{6,10},{... | collective-permute-start | bytes 491528 | tf_op jit(solution)/shard_map/ppermute | solution.py:186
  49.4 7.7 %collective-permute-start.5 = (bf16[64,1280]{1,0:T(8,128)(2,1)S(1)}, bf16[64,1280]{1,0:T(8,128)(2,1)S(1)}, u32[]{:S(2)}, u32[]{:S(2)}) collective-permute-start(bf16[64,1280]{1,0:T(8,128)(2,1)S(1)} %combine.4), channel_id=1, source_target_pairs={{0,4},{4,8},{8,12},{12,0},{1,5},{5,9},{9,13},{13,1},{2,6},{6,10},{... | collective-permute-start | bytes 491528 | tf_op jit(solution)/shard_map/ppermute | solution.py:186
  52.1 7.9 %collective-permute-start.11 = (bf16[64,1280]{1,0:T(8,128)(2,1)S(1)}, bf16[64,1280]{1,0:T(8,128)(2,1)S(1)}, u32[]{:S(2)}, u32[]{:S(2)}) collective-permute-start(bf16[64,1280]{1,0:T(8,128)(2,1)S(1)} %combine.7), channel_id=1, source_target_pairs={{0,4},{4,8},{8,12},{12,0},{1,5},{5,9},{9,13},{13,1},{2,6},{6,10},{... | collective-permute-start | bytes 491528 | tf_op jit(solution)/shard_map/ppermute | solution.py:186
